TPU v7x, 128 devices: a whole 4x4x4 slice. The times are simulated.
128 devices in a mesh: dp: 16 (over y, z_lo, core), tensor: 8 (over z_hi, x).
Axes of the slice: x: 4, y: 4, z: 4 (z_hi: 2, z_lo: 2; z = z_hi * 2 + z_lo), core: 2. Of those that a mesh axis runs over, the one named last changes fastest.
Arguments:
- tokens: bfloat16 [16384, 2048], P(('dp', 'tensor')), may hold values from -6 to 6
- seq_length: int32 [64], replicated, may hold values from 0 to 1024, as said below
- seq_owner: int32 [64], replicated, may hold values from 0 to 15, as said below
- ln1_gain: float32 [2048], replicated, may hold values from 0.5 to 1.5
- ln1_bias: float32 [2048], replicated, may hold values from -3 to 3
- qkv_weight: bfloat16 [3, 2048, 2048], P(None, None, 'tensor'), may hold values from -0.1875 to 0.1875
- qkv_bias: float32 [3, 2048], P(None, 'tensor'), may hold values from -3 to 3
- out_weight: bfloat16 [2048, 2048], P('tensor'), may hold values from -0.75 to 0.75
- ln2_gain: float32 [2048], replicated, may hold values from 0.5 to 1.5
- ln2_bias: float32 [2048], replicated, may hold values from -3 to 3
- gate_up_weight: bfloat16 [2, 2048, 5632], P(None, None, 'tensor'), may hold values from -0.125 to 0.125
- down_weight: bfloat16 [5632, 2048], P('tensor'), may hold values from -0.15625 to 0.15625
- out_grad: bfloat16 [16384, 2048], P(('dp', 'tensor')), may hold values from -6 to 6
Outputs:
- mixed: bfloat16 [16384, 2048], P(('dp', 'tensor'))
- input_grad: float32 [16384, 2048], P(('dp', 'tensor'))
- ln1_gain_grad: float32 [2048], replicated
- ln1_bias_grad: float32 [2048], replicated
- qkv_weight_grad: float32 [3, 2048, 2048], P(None, None, 'tensor')
- qkv_bias_grad: float32 [3, 2048], P(None, 'tensor')
- out_weight_grad: float32 [2048, 2048], P('tensor')
- ln2_gain_grad: float32 [2048], replicated
- ln2_bias_grad: float32 [2048], replicated
- gate_up_grad: float32 [2, 2048, 5632], P(None, None, 'tensor')
- down_grad: float32 [5632, 2048], P('tensor')
Inputs may be any that keep to these rules, and one draw needn't show every extreme that they name: `seq_length`: 0 marks an unused entry; the entries that one dp index owns sum to at most 1024; one entry has length exactly 1024. `seq_owner`: every dp index owns exactly 4 entries.
All inputs are finite; a program needn't handle non-finite values.
Results may differ from a plain program's by a relative error of at most 0.02.
The roundings to bfloat16 on the way count: a program that leaves them out, or rounds other values in their place, can miss the bound.
Values may be sent and summed in bfloat16 or wider, within the bound.
A program may use at most 192 MiB of HBM per device.

v0:
```python
import jax
import jax.numpy as jnp
from jax import lax
from jax.sharding import PartitionSpec as P

HEAD_DIM = 64
ROT = 16


def member_layout(seq_length, seq_owner, member, row_total):
    entry_total = seq_length.shape[0]
    row_ids = jnp.arange(row_total, dtype=jnp.int32)
    entry_ids = jnp.arange(entry_total, dtype=jnp.int32)
    earlier = (entry_ids[:, None] < entry_ids[None, :]).astype(jnp.int32)
    sharing = (seq_owner[:, None] == seq_owner[None, :]).astype(jnp.int32)
    starts = jnp.sum(seq_length[:, None] * sharing * earlier, axis=0)
    owned_now = (seq_owner == member).astype(jnp.int32)
    inside = (
        owned_now[None, :]
        * (row_ids[:, None] >= starts[None, :]).astype(jnp.int32)
        * (row_ids[:, None] < (starts + seq_length)[None, :]).astype(jnp.int32)
    )
    live_rows = jnp.sum(inside, axis=1)
    segment = jnp.sum(inside * entry_ids[None, :], axis=1) + (1 - live_rows) * (
        entry_total + row_ids
    )
    position = jnp.sum(inside * (row_ids[:, None] - starts[None, :]), axis=1)
    return (segment, position, live_rows)


def rotary_tables(position):
    half_rot = ROT // 2
    frequency = jnp.power(
        jnp.float32(10000.0), -2.0 * jnp.arange(half_rot, dtype=jnp.float32) / ROT
    )
    angles = position.astype(jnp.float32)[:, None] * frequency[None, :]
    return (jnp.cos(angles)[:, None, :], jnp.sin(angles)[:, None, :])


def rotate(values, cosine, sine_table):
    half_rot = ROT // 2
    first_half = values[..., :half_rot]
    second_half = values[..., half_rot:ROT]
    return jnp.concatenate(
        [
            first_half * cosine - second_half * sine_table,
            second_half * cosine + first_half * sine_table,
            values[..., ROT:],
        ],
        axis=-1,
    )


def layer_norm(values, gain_vec, shift_vec):
    centre = values - jnp.mean(values, axis=-1, keepdims=True)
    scale_inv = lax.rsqrt(jnp.mean(centre * centre, axis=-1, keepdims=True) + 1e-05)
    return centre * scale_inv * gain_vec + shift_vec


def norm_backward(values, gain_vec, grad_out):
    centre = values - jnp.mean(values, axis=-1, keepdims=True)
    scale_inv = lax.rsqrt(jnp.mean(centre * centre, axis=-1, keepdims=True) + 1e-05)
    unit_rows = centre * scale_inv
    scaled = grad_out * gain_vec
    grad_in = scale_inv * (
        scaled
        - jnp.mean(scaled, axis=-1, keepdims=True)
        - unit_rows * jnp.mean(scaled * unit_rows, axis=-1, keepdims=True)
    )
    return (grad_in, jnp.sum(grad_out * unit_rows, axis=0), jnp.sum(grad_out, axis=0))


def contract_rows(left_rows, right_rows):
    return lax.dot_general(
        left_rows, right_rows, (((0,), (0,)), ((), ())), preferred_element_type=jnp.float32
    )


def times_transposed(left_rows, right_rows):
    return lax.dot_general(
        left_rows, right_rows, (((1,), (1,)), ((), ())), preferred_element_type=jnp.float32
    )


def block_mask(segment, row_ids, begin_row, end_row):
    return (segment[begin_row:end_row, None] == segment[None, :end_row]) & (
        row_ids[None, :end_row] <= row_ids[begin_row:end_row, None]
    )


def body(
    tokens,
    seq_length,
    seq_owner,
    ln1_gain,
    ln1_bias,
    qkv_weight,
    qkv_bias,
    out_weight,
    ln2_gain,
    ln2_bias,
    gate_up_weight,
    down_weight,
    out_grad,
):
    groups = lax.axis_size("tensor")
    local_rows = tokens.shape[0]
    row_total = local_rows * groups
    local_heads = qkv_weight.shape[2] // HEAD_DIM
    member = lax.axis_index("dp")
    tensor_rank = lax.axis_index("tensor")
    score_scale = HEAD_DIM ** (-0.5)
    segment, position, live_rows = member_layout(seq_length, seq_owner, member, row_total)
    cosine, sine_table = rotary_tables(position)
    row_ids = jnp.arange(row_total, dtype=jnp.int32)
    live_local = lax.dynamic_slice_in_dim(live_rows, tensor_rank * local_rows, local_rows, 0)
    stream_in = tokens.astype(jnp.float32)
    normed1_local = layer_norm(stream_in, ln1_gain, ln1_bias).astype(jnp.bfloat16)
    normed1 = lax.all_gather(normed1_local, "tensor", axis=0, tiled=True)
    projected = [
        jnp.dot(normed1, qkv_weight[channel], preferred_element_type=jnp.float32)
        + qkv_bias[channel]
        for channel in range(3)
    ]
    queries = rotate(
        projected[0].reshape(row_total, local_heads, HEAD_DIM), cosine, sine_table
    ).astype(jnp.bfloat16)
    keys_low = rotate(
        projected[1].reshape(row_total, local_heads, HEAD_DIM), cosine, sine_table
    ).astype(jnp.bfloat16)
    values_low = projected[2].reshape(row_total, local_heads, HEAD_DIM).astype(jnp.bfloat16)
    block_size = min(512, row_total)
    block_count = row_total // block_size
    out_blocks = []
    log_norms = []
    for block_index in range(block_count):
        begin_row = block_index * block_size
        end_row = begin_row + block_size
        allowed = block_mask(segment, row_ids, begin_row, end_row)
        scores = (
            jnp.einsum(
                "qhd,khd->hqk",
                queries[begin_row:end_row],
                keys_low[:end_row],
                preferred_element_type=jnp.float32,
            )
            * score_scale
        )
        scores = jnp.where(allowed[None], scores, -1e30)
        row_max = jnp.max(scores, axis=-1, keepdims=True)
        exp_scores = jnp.exp(scores - row_max)
        exp_sum = jnp.sum(exp_scores, axis=-1, keepdims=True)
        attn_prob = (exp_scores / exp_sum).astype(jnp.bfloat16)
        out_blocks.append(
            jnp.einsum(
                "hqk,khd->qhd", attn_prob, values_low[:end_row], preferred_element_type=jnp.float32
            ).astype(jnp.bfloat16)
        )
        log_norms.append(row_max + jnp.log(exp_sum))
    attended = jnp.concatenate(out_blocks, axis=0).reshape(row_total, local_heads * HEAD_DIM)
    attn_out = lax.psum_scatter(
        jnp.dot(attended, out_weight, preferred_element_type=jnp.float32),
        "tensor",
        scatter_dimension=0,
        tiled=True,
    )
    mid_stream = stream_in + attn_out
    normed2_local = layer_norm(mid_stream, ln2_gain, ln2_bias).astype(jnp.bfloat16)
    normed2 = lax.all_gather(normed2_local, "tensor", axis=0, tiled=True)
    gate_act = jnp.dot(normed2, gate_up_weight[0], preferred_element_type=jnp.float32)
    up_act = jnp.dot(normed2, gate_up_weight[1], preferred_element_type=jnp.float32)
    hidden = (jax.nn.silu(gate_act) * up_act).astype(jnp.bfloat16)
    ffn_out = lax.psum_scatter(
        jnp.dot(hidden, down_weight, preferred_element_type=jnp.float32).astype(jnp.bfloat16),
        "tensor",
        scatter_dimension=0,
        tiled=True,
    ).astype(jnp.float32)
    mixed = (mid_stream + ffn_out).astype(jnp.bfloat16)
    cotangent = out_grad.astype(jnp.float32) * live_local[:, None].astype(jnp.float32)
    cot_rows = lax.all_gather(cotangent.astype(jnp.bfloat16), "tensor", axis=0, tiled=True)
    down_grad = contract_rows(hidden, cot_rows)
    d_hidden = times_transposed(cot_rows, down_weight)
    sigmoid_g = jax.nn.sigmoid(gate_act)
    d_gate = (d_hidden * up_act * sigmoid_g * (1.0 + gate_act * (1.0 - sigmoid_g))).astype(
        jnp.bfloat16
    )
    d_up = (d_hidden * jax.nn.silu(gate_act)).astype(jnp.bfloat16)
    gate_up_grad = jnp.stack([contract_rows(normed2, d_gate), contract_rows(normed2, d_up)])
    d_normed2 = lax.psum_scatter(
        times_transposed(d_gate, gate_up_weight[0]) + times_transposed(d_up, gate_up_weight[1]),
        "tensor",
        scatter_dimension=0,
        tiled=True,
    )
    d_mid_norm, ln2_gain_part, ln2_bias_part = norm_backward(mid_stream, ln2_gain, d_normed2)
    d_mid = cotangent + d_mid_norm
    d_attn_rows = lax.all_gather(d_mid.astype(jnp.bfloat16), "tensor", axis=0, tiled=True)
    out_weight_grad = contract_rows(attended, d_attn_rows)
    d_attended = (
        times_transposed(d_attn_rows, out_weight)
        .astype(jnp.bfloat16)
        .reshape(row_total, local_heads, HEAD_DIM)
    )
    query_grads = []
    d_key = jnp.zeros((row_total, local_heads, HEAD_DIM), jnp.float32)
    d_value = jnp.zeros((row_total, local_heads, HEAD_DIM), jnp.float32)
    for block_index in range(block_count):
        begin_row = block_index * block_size
        end_row = begin_row + block_size
        allowed = block_mask(segment, row_ids, begin_row, end_row)
        query_block = queries[begin_row:end_row]
        key_block = keys_low[:end_row]
        grad_block = d_attended[begin_row:end_row]
        scores = (
            jnp.einsum("qhd,khd->hqk", query_block, key_block, preferred_element_type=jnp.float32)
            * score_scale
        )
        scores = jnp.where(allowed[None], scores, -1e30)
        attn_full = jnp.exp(scores - log_norms[block_index])
        attn_prob = attn_full.astype(jnp.bfloat16)
        d_prob = jnp.einsum(
            "qhd,khd->hqk", grad_block, values_low[:end_row], preferred_element_type=jnp.float32
        )
        row_dots = jnp.sum(attn_full * d_prob, axis=-1, keepdims=True)
        d_score = (attn_full * (d_prob - row_dots)).astype(jnp.bfloat16)
        query_grads.append(
            jnp.einsum("hqk,khd->qhd", d_score, key_block, preferred_element_type=jnp.float32)
            * score_scale
        )
        d_key = d_key.at[:end_row].add(
            jnp.einsum("hqk,qhd->khd", d_score, query_block, preferred_element_type=jnp.float32)
            * score_scale
        )
        d_value = d_value.at[:end_row].add(
            jnp.einsum("hqk,qhd->khd", attn_prob, grad_block, preferred_element_type=jnp.float32)
        )
    d_query = jnp.concatenate(query_grads, axis=0)
    d_proj = [
        rotate(d_query, cosine, -sine_table).reshape(row_total, -1).astype(jnp.bfloat16),
        rotate(d_key, cosine, -sine_table).reshape(row_total, -1).astype(jnp.bfloat16),
        d_value.reshape(row_total, -1).astype(jnp.bfloat16),
    ]
    qkv_weight_grad = jnp.stack([contract_rows(normed1, d_proj[channel]) for channel in range(3)])
    qkv_bias_grad = jnp.stack(
        [jnp.sum(d_proj[channel].astype(jnp.float32), axis=0) for channel in range(3)]
    )
    summed = times_transposed(d_proj[0], qkv_weight[0])
    summed = summed + times_transposed(d_proj[1], qkv_weight[1])
    d_normed1 = lax.psum_scatter(
        (summed + times_transposed(d_proj[2], qkv_weight[2])).astype(jnp.bfloat16),
        "tensor",
        scatter_dimension=0,
        tiled=True,
    ).astype(jnp.float32)
    d_in_norm, ln1_gain_part, ln1_bias_part = norm_backward(stream_in, ln1_gain, d_normed1)
    input_grad = d_mid + d_in_norm
    ln1_gain_grad, ln1_bias_grad, ln2_gain_grad, ln2_bias_grad = lax.psum(
        (ln1_gain_part, ln1_bias_part, ln2_gain_part, ln2_bias_part), ("dp", "tensor")
    )
    qkv_weight_grad, qkv_bias_grad, out_weight_grad, gate_up_grad, down_grad = (
        lax.psum(qkv_weight_grad.astype(jnp.bfloat16), "dp").astype(jnp.float32),
        lax.psum(qkv_bias_grad.astype(jnp.bfloat16), "dp").astype(jnp.float32),
        lax.psum(out_weight_grad.astype(jnp.bfloat16), "dp").astype(jnp.float32),
        lax.psum(gate_up_grad.astype(jnp.bfloat16), "dp").astype(jnp.float32),
        lax.psum(down_grad.astype(jnp.bfloat16), "dp").astype(jnp.float32),
    )
    return (
        mixed,
        input_grad,
        ln1_gain_grad,
        ln1_bias_grad,
        qkv_weight_grad,
        qkv_bias_grad,
        out_weight_grad,
        ln2_gain_grad,
        ln2_bias_grad,
        gate_up_grad,
        down_grad,
    )


def solution(mesh):
    placed = (
        P(("dp", "tensor"), None),
        P(),
        P(),
        P(),
        P(),
        P(None, None, "tensor"),
        P(None, "tensor"),
        P("tensor", None),
        P(),
        P(),
        P(None, None, "tensor"),
        P("tensor", None),
        P(("dp", "tensor"), None),
    )
    return jax.shard_map(
        body,
        mesh=mesh,
        in_specs=placed,
        out_specs=(
            P(("dp", "tensor"), None),
            P(("dp", "tensor"), None),
            P(),
            P(),
            P(None, None, "tensor"),
            P(None, "tensor"),
            P("tensor", None),
            P(),
            P(),
            P(None, None, "tensor"),
            P("tensor", None),
        ),
        check_vma=False,
    )
```

profile of v0, /device:TPU:1, one launch (start us, length us, event | category | flops | bytes accessed | tf_op | source)
XLA Modules:
  0.0 1085.3 jit_solution(5334107917747817480)
XLA Ops:
  7.2 1.3 convert_reduce_fusion.1
  8.6 1.3 fusion.64
  9.9 2.3 fusion.60
  16.3 1.0 compare_and_fusion
  17.3 1.4 fusion.28
  18.7 68.1 %all-gather.5.cloned.1.call-done = bf16[1024,2048]{1,0:T(8,128)(2,1)} async-done(((bf16[128,2048]{1,0:T(8,128)(2,1)}), bf16[1024,2048]{1,0:T(8,128)(2,1)}) %all-gather.5.cloned.1.call-update) | async-done | bytes 4194320 | tf_op jit(solution)/shard_map/all_gather | solution.py:119
  86.8 3.9 fusion.41
  91.5 1.3 convolution_add_fusion.1
  92.9 1.3 convolution_add_fusion.2
  94.4 0.9 fusion.101
  95.3 1.8 fusion.100
  98.9 2.4 fusion
  101.3 2.1 fusion.57
  103.6 4.7 fusion.103
  108.4 112.7 %reduce-scatter.5.cloned.1.call-done = f32[128,2048]{1,0:T(8,128)} async-done(((f32[1024,2048]{1,0:T(8,128)}), f32[128,2048]{1,0:T(8,128)}) %reduce-scatter.5.cloned.1.call-update) | async-done | bytes 1048592 | tf_op jit(solution)/shard_map/reduce_scatter | solution.py:161
  221.0 1.4 fusion.96
  223.9 1.7 add_convert_fusion.2
  227.0 2.0 fusion.77
  229.1 66.2 %all-gather.7.cloned.1.call-done = bf16[1024,2048]{1,0:T(8,128)(2,1)} async-done(((bf16[128,2048]{1,0:T(8,128)(2,1)}), bf16[1024,2048]{1,0:T(8,128)(2,1)}) %all-gather.7.cloned.1.call-update) | async-done | bytes 4194320 | tf_op jit(solution)/shard_map/all_gather | solution.py:169
  295.2 8.0 fusion.11
  303.2 6.6 fusion.15
  309.8 57.6 %all-gather.9.cloned.1.call-done = bf16[1024,2048]{1,0:T(8,128)(2,1)} async-done(((bf16[128,2048]{1,0:T(8,128)(2,1)}), bf16[1024,2048]{1,0:T(8,128)(2,1)}) %all-gather.9.cloned.1.call-update) | async-done | bytes 4194320 | tf_op jit(solution)/shard_map/all_gather | solution.py:181
  367.3 8.5 multiply_convert_fusion.2
  375.8 6.4 fusion.13
  382.2 7.7 convolution_add_fusion
  390.0 6.4 convolution_convert_fusion
  396.6 106.0 %reduce-scatter.9.cloned.1.call-done = f32[128,2048]{1,0:T(8,128)} async-done(((f32[1024,2048]{1,0:T(8,128)}), f32[128,2048]{1,0:T(8,128)}) %reduce-scatter.9.cloned.1.call-update) | async-done | bytes 1048592 | tf_op jit(solution)/shard_map/reduce_scatter | solution.py:190
  502.5 2.3 multiply_reduce_fusion.2
  504.8 84.1 %reduce-scatter.7.cloned.1.call-done = bf16[128,2048]{1,0:T(8,128)(2,1)} async-done(((bf16[1024,2048]{1,0:T(8,128)(2,1)}), bf16[128,2048]{1,0:T(8,128)(2,1)}) %reduce-scatter.7.cloned.1.call-update) | async-done | bytes 524304 | tf_op jit(solution)/shard_map/reduce_scatter | solution.py:173
  588.8 3.3 fusion.95
  592.3 71.0 %all-gather.11.cloned.1.call-done = bf16[1024,2048]{1,0:T(8,128)(2,1)} async-done(((bf16[128,2048]{1,0:T(8,128)(2,1)}), bf16[1024,2048]{1,0:T(8,128)(2,1)}) %all-gather.11.cloned.1.call-update) | async-done | bytes 4194320 | tf_op jit(solution)/shard_map/all_gather | solution.py:198
  663.3 3.6 convolution_convert_fusion.8
  667.8 0.9 multiply_reduce_fusion.1
  668.8 1.2 multiply_convert_fusion.1
  671.3 1.2 slice-done.1
  672.8 2.8 multiply_reduce_fusion
  675.5 1.9 fusion.102
  677.5 1.8 multiply_convert_fusion
  679.2 1.4 fusion.52
  680.7 0.9 fusion.37
  681.9 1.7 copy-done.12
  683.6 1.3 fusion.72
  685.1 1.3 fusion.69
  686.4 3.4 add_convert_fusion
  689.9 5.9 fusion.9
  695.9 3.8 fusion.8
  699.7 3.4 pad_maximum_fusion
  704.4 4.5 convolution_convert_fusion.3
  708.9 1.3 fusion.24
  710.3 1.3 fusion.23
  711.6 1.3 fusion.22
  713.0 2.0 pad_maximum_fusion.1
  715.0 1.7 copy-done.63
  716.6 2.2 convolution_convert_fusion.4
  719.2 28.1 %psum.66 = bf16[3,256]{1,0:T(4,128)(2,1)S(1)} all-reduce(bf16[3,256]{1,0:T(4,128)(2,1)S(1)} %pad_maximum_fusion.10), channel_id=1, replica_groups=mesh['dp'=16,'tensor'=8] {'dp'}, use_global_device_ids=true, to_apply=%region_30.31 | all-reduce | flops 768 | bytes 3072 | tf_op jit(solution)/shard_map/psum | solution.py:263
  747.9 24.2 %reduce-scatter.11.cloned.1.call-done = bf16[128,2048]{1,0:T(8,128)(2,1)} async-done(((bf16[1024,2048]{1,0:T(8,128)(2,1)}), bf16[128,2048]{1,0:T(8,128)(2,1)}) %reduce-scatter.11.cloned.1.call-update) | async-done | bytes 524304 | tf_op jit(solution)/shard_map/reduce_scatter | solution.py:250
  772.1 1.5 fusion.66
  773.6 79.3 %all-reduce.2 = (f32[2048]{0:T(1024)}, f32[2048]{0:T(1024)}, f32[2048]{0:T(1024)}, f32[2048]{0:T(1024)}) all-reduce(f32[2048]{0:T(1024)S(1)} %get-tuple-element.78, f32[2048]{0:T(1024)S(1)} %get-tuple-element.82, f32[2048]{0:T(1024)S(1)} %copy-done.41, f32[2048]{0:T(1024)S(1)} %copy-done.42), channel_id=1, replica_groups=mesh['dp'=16,'tensor'=8] {'dp','tensor'}, use_global_device_ids=true, to_apply=%region_23.24 | all-reduce | flops 8192 | bytes 65536 | tf_op jit(solution)/shard_map/psum | solution.py:258
  852.9 2.5 fusion.63
  855.4 207.2 %all-reduce.6.cloned.1.call-done = (bf16[3,2048,256]{2,1,0:T(8,128)(2,1)}, bf16[256,2048]{1,0:T(8,128)(2,1)}, bf16[2,2048,704]{1,2,0:T(8,128)(2,1)}, bf16[704,2048]{1,0:T(8,128)(2,1)}) async-done(((bf16[3,2048,256]{2,1,0:T(8,128)(2,1)}, bf16[256,2048]{1,0:T(8,128)(2,1)}, bf16[2,2048,704]{1,2,0:T(8,128)(2,1)}, bf16[704,2048]{1,0:T(8,128)(2,1)}), (bf16[3,2048,256]{2,1,0:T(8,128)(2,1)}, ...) | async-done | bytes 12845072 | tf_op jit(solution)/shard_map/psum | solution.py:262
  1062.6 2.9 convert_element_type.215
  1065.5 3.7 convert_element_type.209
  1069.3 3.3 convert_element_type.218
  1072.6 6.0 convert_element_type.216
  (208 shorter events, 15.3 us)
Async XLA Ops:
  7.2 360.1 %copy-start = (bf16[704,2048]{1,0:T(8,128)(2,1)S(1)}, bf16[704,2048]{1,0:T(8,128)(2,1)}, u32[]{:S(2)}) copy-start(bf16[704,2048]{1,0:T(8,128)(2,1)} %param.36) | copy-start | bytes 8650756
  7.2 79.6 %all-gather.5.cloned.1.call-start = ((), (), s32[]{:S(2)}) async-start(), calls=%async_computation.4 | async-start | bytes 4718592 | tf_op jit(solution)/shard_map/all_gather | solution.py:119
  8.6 4.5 copy-start.50
  9.9 80.8 %copy-start.54 = (f32[128]{0:T(128)}, f32[128]{0:T(128)S(1)}, u32[]{:S(2)}) copy-start(f32[128]{0:T(128)S(1)} %add_rsqrt_fusion.1) | copy-start | bytes 1540
  12.2 208.8 %reduce-scatter.5.cloned.1.call-start = ((), (), s32[]{:S(2)}) async-start(), calls=%async_computation.5 | async-start | bytes 9437184 | tf_op jit(solution)/shard_map/reduce_scatter | solution.py:161
  16.3 77.9 %copy-start.33 = (f32[1024,8]{0,1:T(8,128)}, f32[1024,8]{0,1:T(8,128)S(1)}, u32[]{:S(2)}) copy-start(f32[1024,8]{0,1:T(8,128)S(1)} %get-tuple-element.122) | copy-start | bytes 98308
  86.8 4.0 copy-start.11
  86.8 4.7 copy-start.58
  90.7 10.6 copy-start.26
  90.7 7.0 copy-start.30
  92.8 2.5 copy-start.9
  94.4 2.8 copy-start.19
  95.3 2.5 copy-start.3
  97.1 4.2 copy-start.2
  97.1 4.2 copy-start.43
  101.3 2.2 copy-start.45
  101.3 2.2 copy-start.28
  103.5 4.7 copy-start.23
  108.3 112.7 %copy-start.7 = (bf16[128,2048]{1,0:T(8,128)(2,1)S(1)}, bf16[128,2048]{1,0:T(8,128)(2,1)}, u32[]{:S(2)}) copy-start(bf16[128,2048]{1,0:T(8,128)(2,1)} %param.25) | copy-start | bytes 1572868
  108.3 115.6 %copy-start.37 = (f32[2048]{0:T(1024)S(1)}, f32[2048]{0:T(1024)}, u32[]{:S(2)}) copy-start(f32[2048]{0:T(1024)} %param.33) | copy-start | bytes 24580
  108.3 186.9 %all-gather.7.cloned.1.call-start = ((), (), s32[]{:S(2)}) async-start(), calls=%async_computation.6 | async-start | bytes 4718592 | tf_op jit(solution)/shard_map/all_gather | solution.py:169
  225.7 141.6 %all-gather.9.cloned.1.call-start = ((), (), s32[]{:S(2)}) async-start(), calls=%async_computation.8 | async-start | bytes 4718592 | tf_op jit(solution)/shard_map/all_gather | solution.py:181
  229.0 273.5 %reduce-scatter.9.cloned.1.call-start = ((), (), s32[]{:S(2)}) async-start(), calls=%async_computation.9 | async-start | bytes 9437184 | tf_op jit(solution)/shard_map/reduce_scatter | solution.py:190
  295.2 8.0 copy-start.60
  375.8 6.4 copy-start.65
  375.8 6.4 copy-start.64
  390.0 198.9 %reduce-scatter.7.cloned.1.call-start = ((), (), s32[]{:S(2)}) async-start(), calls=%async_computation.7 | async-start | bytes 4718592 | tf_op jit(solution)/shard_map/reduce_scatter | solution.py:173
  396.4 106.1 %copy-start.6 = (f32[128,2048]{1,0:T(8,128)S(1)}, f32[128,2048]{1,0:T(8,128)}, u32[]{:S(2)}) copy-start(f32[128,2048]{1,0:T(8,128)} %copy-done.5) | copy-start | bytes 3145732
  396.4 106.1 %copy-start.49 = (f32[128]{0:T(128)S(1)}, f32[128]{0:T(128)}, u32[]{:S(2)}) copy-start(f32[128]{0:T(128)} %copy-done.48) | copy-start | bytes 1540
  396.4 106.1 %copy-start.53 = (f32[128]{0:T(128)S(1)}, f32[128]{0:T(128)}, u32[]{:S(2)}) copy-start(f32[128]{0:T(128)} %copy-done.52) | copy-start | bytes 1540
  396.4 192.4 %copy-start.25 = (bf16[128,2048]{1,0:T(8,128)(2,1)S(1)}, bf16[128,2048]{1,0:T(8,128)(2,1)}, u32[]{:S(2)}) copy-start(bf16[128,2048]{1,0:T(8,128)(2,1)} %param.37) | copy-start | bytes 1572868
  396.4 192.4 %copy-start.57 = (f32[128]{0:T(128)S(1)}, f32[128]{0:T(128)}, u32[]{:S(2)}) copy-start(f32[128]{0:T(128)} %copy-done.56) | copy-start | bytes 1540
  396.5 195.7 %copy-start.40 = (f32[4,512]{1,0:T(4,128)S(1)}, f32[4,512]{1,0:T(4,128)}, u32[]{:S(2)}) copy-start(f32[4,512]{1,0:T(4,128)} %copy-done.39) | copy-start | bytes 24580
  396.5 195.7 %copy-start.44 = (f32[4,512]{1,0:T(4,128)S(1)}, f32[4,512]{1,0:T(4,128)}, u32[]{:S(2)}) copy-start(f32[4,512]{1,0:T(4,128)} %copy-done.43) | copy-start | bytes 24580
  396.5 195.7 %copy-start.46 = (f32[4,512]{1,0:T(4,128)S(1)}, f32[4,512]{1,0:T(4,128)}, u32[]{:S(2)}) copy-start(f32[4,512]{1,0:T(4,128)} %copy-done.45) | copy-start | bytes 24580
  396.5 266.8 %copy-start.29 = (bf16[256,2048]{1,0:T(8,128)(2,1)S(1)}, bf16[256,2048]{1,0:T(8,128)(2,1)}, u32[]{:S(2)}) copy-start(bf16[256,2048]{1,0:T(8,128)(2,1)} %param.32) | copy-start | bytes 3145732
  396.5 266.7 %all-gather.11.cloned.1.call-start = ((), (), s32[]{:S(2)}) async-start(), calls=%async_computation.10 | async-start | bytes 4718592 | tf_op jit(solution)/shard_map/all_gather | solution.py:198
  592.1 179.9 %reduce-scatter.11.cloned.1.call-start = ((), (), s32[]{:S(2)}) async-start(), calls=%async_computation.11 | async-start | bytes 4718592 | tf_op jit(solution)/shard_map/reduce_scatter | solution.py:250
  663.3 3.7 copy-start.4
  668.8 2.5 slice-start
  668.8 3.7 slice-start.1
  670.1 2.7 copy-start.27
  677.5 9.0 copy-start.21
  681.5 2.1 copy-start.12
  681.9 3.1 copy-start.15
  689.9 372.7 %all-reduce.6.cloned.1.call-start = ((), (), s32[]{:S(2)}) async-start(), calls=%async_computation.12 | async-start | bytes 25690112 | tf_op jit(solution)/shard_map/psum | solution.py:262
  689.9 5.9 copy-start.61
  689.9 5.9 copy-start.66
  699.7 4.0 copy-start.62
  699.7 4.7 copy-start.67
  704.4 4.5 copy-start.22
  704.4 4.5 copy-start.59
  713.0 3.7 copy-start.63
  718.9 53.2 %copy-start.38 = (f32[2048]{0:T(1024)S(1)}, f32[2048]{0:T(1024)}, u32[]{:S(2)}) copy-start(f32[2048]{0:T(1024)} %param.28) | copy-start | bytes 24580
  718.9 53.2 %copy-start.51 = (f32[128]{0:T(128)S(1)}, f32[128]{0:T(128)}, u32[]{:S(2)}) copy-start(f32[128]{0:T(128)} %copy-done.50) | copy-start | bytes 1540
  718.9 53.2 %copy-start.55 = (f32[128]{0:T(128)S(1)}, f32[128]{0:T(128)}, u32[]{:S(2)}) copy-start(f32[128]{0:T(128)} %copy-done.54) | copy-start | bytes 1540
  718.9 54.8 %copy-start.41 = (f32[2048]{0:T(1024)S(1)}, f32[2048]{0:T(1024)}, u32[]{:S(2)}) copy-start(f32[2048]{0:T(1024)} %get-tuple-element.75) | copy-start | bytes 24580
  718.9 54.8 %copy-start.42 = (f32[2048]{0:T(1024)S(1)}, f32[2048]{0:T(1024)}, u32[]{:S(2)}) copy-start(f32[2048]{0:T(1024)} %get-tuple-element.80) | copy-start | bytes 24580
  718.9 134.0 %copy-start.8 = (f32[128,2048]{1,0:T(8,128)S(1)}, f32[128,2048]{1,0:T(8,128)}, u32[]{:S(2)}) copy-start(f32[128,2048]{1,0:T(8,128)} %get-tuple-element.102) | copy-start | bytes 3145732
  1062.6 2.9 copy-start.13
  1062.6 10.0 slice-start.2
  1065.5 3.7 copy-start.14
  1065.5 7.1 slice-start.3
  1072.6 6.0 copy-start.1
  (17 other events, 19.6 us)
Sparse Core Ops, SparseCore 0:
  12.3 74.3 all-gather.4
  108.4 112.5 reduce-scatter.4
  225.8 69.3 all-gather.6
  298.0 69.2 all-gather.8
  390.1 112.3 reduce-scatter.8
  506.8 81.9 reduce-scatter.6
  592.3 70.9 all-gather.10
  690.0 82.0 reduce-scatter.10
  776.0 286.5 all-reduce.5
where the time goes:
time: 1090 us
  waiting for transfers between devices  797 us (73%)
  blocking collectives  107 us (10%)
  matrix products  100 us (9%)
  other arithmetic  54.7 us (5%)
  between operations  15 us (1%)
    psum x1, waiting for transfers between devices, body(): lax.psum(qkv_weight_grad.astype(jnp.bfloat16), 'dp').astype(jnp.float32)  207 us
    reduce_scatter x1, waiting for transfers between devices, body(): lax.psum_scatter(jnp.dot(attended, out_weight, preferred_element_type=jnp...  113 us
    reduce_scatter x1, waiting for transfers between devices, body(): lax.psum_scatter(times_transposed(d_gate, gate_up_weight[0]) + times_tran...  106 us
    reduce_scatter x1, waiting for transfers between devices, body(): lax.psum_scatter(jnp.dot(hidden, down_weight, preferred_element_type=jnp....  84.1 us
    psum x1, blocking collectives, body(): lax.psum((ln1_gain_part, ln1_bias_part, ln2_gain_part, ln2_bias_part), ('...  79.3 us
    all_gather x1, waiting for transfers between devices, body(): lax.all_gather(d_mid.astype(jnp.bfloat16), 'tensor', axis=0, tiled=True)  71 us
    all_gather x1, waiting for transfers between devices, body(): normed1 = lax.all_gather(normed1_local, 'tensor', axis=0, tiled=True)  68.1 us
    all_gather x1, waiting for transfers between devices, body(): normed2 = lax.all_gather(normed2_local, 'tensor', axis=0, tiled=True)  66.2 us
  transfers between devices with their start and end apart: 9, of which 9 were waited for; matrix products, arithmetic and copies ran while one was open for 6% of the time, Pallas kernels for 0%

commit v1 on v0

v1 whole, which is shorter than its diff:
```python
import functools

import jax
import jax.numpy as jnp
from jax import lax
from jax.experimental import pallas as pl
from jax.experimental.pallas import tpu as pltpu
from jax.sharding import PartitionSpec as P

HEAD_DIM = 64
ROT = 16
SIDE = 4
BLOCK = 128
AXES = ("dp", "tensor")
MESH = pl.DeviceIdType.MESH
VMEM_LIMIT = 56 * 2**20


def here():
    dp, tensor = lax.axis_index("dp"), lax.axis_index("tensor")
    x, z_hi = lax.rem(tensor, SIDE), lax.div(tensor, SIDE)
    y, z_lo, core = lax.div(dp, SIDE), lax.rem(lax.div(dp, 2), 2), lax.rem(dp, 2)
    return x, y, z_hi, z_lo, core


def device(x, y, z_hi, z_lo, core):
    return ((y * 2 + z_lo) * 2 + core, z_hi * SIDE + x)


def turned(value, by):
    return lax.rem(value + by, SIDE)


def pairs(move):
    found = []
    for dp in range(16):
        for tensor in range(8):
            goal = move(tensor % 4, dp // 4, tensor // 4, (dp // 2) % 2, dp % 2)
            if goal is not None:
                to_dp, to_tensor = device(*goal)
                found.append((dp * 8 + tensor, to_dp * 8 + to_tensor))
    return found


def permute(array, move):
    return lax.ppermute(array, AXES, pairs(move))


def swap_rows(x, y, z_hi, z_lo, core):
    return (x, y, core, z_lo, z_hi)


def remote(source, target, sends, arrives, index, device_id):
    return pltpu.make_async_remote_copy(
        src_ref=source,
        dst_ref=target,
        send_sem=sends.at[index],
        recv_sem=arrives.at[index],
        device_id=device_id,
        device_id_type=MESH,
    )


def greet(peers):
    barrier = pltpu.get_barrier_semaphore()
    for peer in peers:
        pl.semaphore_signal(barrier, inc=1, device_id=peer, device_id_type=MESH)
    pl.semaphore_wait(barrier, len(peers))


def line_peers(place):
    x, y, z_hi, z_lo, core = place
    found = [device(turned(x, k), y, z_hi, z_lo, core) for k in (1, 2, 3)]
    return found + [device(x, y, z_hi, z_lo, 1 - core)]


def row_block(full, core, x):
    return full.at[pl.ds(pl.multiple_of((core * SIDE + x) * BLOCK, BLOCK), BLOCK)]


class Gather:
    scratch = (
        pltpu.SemaphoreType.DMA((3,)),
        pltpu.SemaphoreType.DMA((3,)),
        pltpu.SemaphoreType.DMA((4,)),
        pltpu.SemaphoreType.DMA((4,)),
        pltpu.SemaphoreType.DMA,
    )

    def __init__(self, block, full, place, sems):
        x, y, z_hi, z_lo, core = place
        x_send, x_arrive, core_send, core_arrive, own_sem = sems
        self.own = pltpu.make_async_copy(block, row_block(full, core, x), own_sem)
        self.along = [
            remote(
                block,
                row_block(full, core, x),
                x_send,
                x_arrive,
                step - 1,
                device(turned(x, step), y, z_hi, z_lo, core),
            )
            for step in (1, 2, 3)
        ]
        partner = device(x, y, z_hi, z_lo, 1 - core)
        self.across = [remote(block, row_block(full, core, x), core_send, core_arrive, 0, partner)]
        for step in (1, 2, 3):
            arrived = row_block(full, core, turned(x, SIDE - step))
            self.across.append(remote(arrived, arrived, core_send, core_arrive, step, partner))

    def start(self):
        for step in (2, 1, 3):
            self.along[step - 1].start()
        self.across[0].start()
        self.own.start()

    def finish(self):
        for step in (1, 3, 2):
            self.along[step - 1].wait_recv()
            self.across[step].start()
        for copy in self.along:
            copy.wait_send()
        for copy in self.across:
            copy.wait()
        self.own.wait()


class Scatter:
    scratch = (
        pltpu.VMEM((SIDE, BLOCK, 2048), jnp.bfloat16),
        pltpu.VMEM((SIDE, BLOCK, 2048), jnp.bfloat16),
        pltpu.VMEM((3, BLOCK, 2048), jnp.bfloat16),
        pltpu.VMEM((3, BLOCK, 2048), jnp.bfloat16),
        pltpu.SemaphoreType.DMA((4,)),
        pltpu.SemaphoreType.DMA((4,)),
        pltpu.SemaphoreType.DMA((4,)),
        pltpu.SemaphoreType.DMA((3,)),
        pltpu.SemaphoreType.DMA((3,)),
    )

    def __init__(self, part, place, scratch):
        x, y, z_hi, z_lo, core = place
        self.own, self.other, self.leaving, self.arrived = scratch[:4]
        own_sem, core_send, core_arrive, x_send, x_arrive = scratch[4:]
        partner = device(x, y, z_hi, z_lo, 1 - core)
        self.across, self.load, self.along = [], [], []
        for step in range(SIDE):
            there = turned(x, step)
            self.across.append(
                remote(row_block(part, 1 - core, there), self.other.at[step], core_send, core_arrive, step, partner)
            )
            self.load.append(
                pltpu.make_async_copy(row_block(part, core, there), self.own.at[step], own_sem.at[step])
            )
        for step in (1, 2, 3):
            self.along.append(
                remote(
                    self.leaving.at[step - 1],
                    self.arrived.at[step - 1],
                    x_send,
                    x_arrive,
                    step - 1,
                    device(turned(x, step), y, z_hi, z_lo, core),
                )
            )

    def start(self):
        for step in (2, 1, 3, 0):
            self.across[step].start()
            self.load[step].start()
        for step in (2, 1, 3):
            self.across[step].wait_recv()
            self.load[step].wait()

            @pl.loop(0, BLOCK, step=16)
            def _(row):
                rows = pl.ds(pl.multiple_of(row, 16), 16)
                both = self.own[step, rows, :].astype(jnp.float32) + self.other[step, rows, :].astype(jnp.float32)
                self.leaving[step - 1, rows, :] = both.astype(jnp.bfloat16)

            self.along[step - 1].start()
        self.across[0].wait_recv()
        self.load[0].wait()

    def finish(self):
        for copy in self.along:
            copy.wait()
        for copy in self.across:
            copy.wait_send()

    def rows(self, rows):
        total = self.own[0, rows, :].astype(jnp.float32) + self.other[0, rows, :].astype(jnp.float32)
        for step in range(3):
            total = total + self.arrived[step, rows, :].astype(jnp.float32)
        return total


class Fetch:
    def __init__(self, weight, filled, quarter, place, sems, index):
        x, y, z_hi, z_lo, core = place
        send, arrive, own_sem = sems
        self.own = pltpu.make_async_copy(weight, filled, own_sem.at[index])
        mine = quarter(filled, y)
        across = device(x, y, 1 - z_hi, 1 - z_lo, z_hi)
        self.across = remote(quarter(weight, y), mine, send, arrive, index * 4, across)
        self.along = [
            remote(mine, mine, send, arrive, index * 4 + k, device(x, turned(y, k), z_hi, z_lo, core))
            for k in (1, 2, 3)
        ]

    def spread(self):
        self.across.wait_recv()
        for copy in self.along:
            copy.start()

    def finish(self):
        self.across.wait_send()
        for copy in self.along:
            copy.wait()


def fetch_scratch(count):
    return (
        pltpu.SemaphoreType.DMA((4 * count,)),
        pltpu.SemaphoreType.DMA((4 * count,)),
        pltpu.SemaphoreType.DMA((count,)),
    )


def fetch_peers(place):
    x, y, z_hi, z_lo, core = place
    return [device(x, y, 1 - z_hi, 1 - z_lo, z_hi)] + [
        device(x, turned(y, k), z_hi, z_lo, core) for k in (1, 2, 3)
    ]


def quarter_qkv(weight, y):
    return weight.at[:, pl.ds(pl.multiple_of(y * 512, 512), 512), :]


def quarter_out(weight, y):
    return weight.at[pl.ds(pl.multiple_of(y * 64, 64), 64), :]


def quarter_down(weight, y):
    return weight.at[pl.ds(pl.multiple_of(y * 176, 16), 176), :]


def quarter_gate_up(weight, y):
    return weight.at[:, pl.ds(pl.multiple_of(y * 176, 16), 176), :]


def moments(values):
    centre = values - jnp.mean(values, axis=-1, keepdims=True)
    return centre, lax.rsqrt(jnp.mean(centre * centre, axis=-1, keepdims=True) + 1e-05)


def tile_rows(body):
    @pl.loop(0, BLOCK, step=16)
    def _(row):
        body(pl.ds(pl.multiple_of(row, 16), 16))


def first_kernel(
    tokens,
    out_grad,
    live,
    gain,
    shift,
    qkv,
    out,
    down,
    tokens_here,
    cot_here,
    normed_full,
    cot_full,
    qkv_here,
    out_here,
    down_here,
    tok_buf,
    grad_buf,
    norm_buf,
    cot_buf,
    swap_send,
    swap_arrive,
    own_sems,
    *sems,
):
    place = here()
    x, y, z_hi, z_lo, core = place
    lacking = core != z_hi
    swap_with = device(x, y, core, z_lo, z_hi)
    fetch_sems = sems[10:]
    fetches = [
        Fetch(weight, filled, cut, place, fetch_sems, index)
        for index, (weight, filled, cut) in enumerate(
            [(qkv, qkv_here, quarter_qkv), (out, out_here, quarter_out), (down, down_here, quarter_down)]
        )
    ]
    swaps = [
        remote(source, target, swap_send, swap_arrive, index, swap_with)
        for index, (source, target) in enumerate([(tokens, tok_buf), (out_grad, grad_buf)])
    ]
    stays = [
        pltpu.make_async_copy(source, target, own_sems.at[index])
        for index, (source, target) in enumerate([(tokens, tok_buf), (out_grad, grad_buf)])
    ]

    @pl.when(lacking)
    def _():
        greet(line_peers(place) + [swap_with] + fetch_peers(place))
        swaps[0].start()
        for fetch in fetches:
            fetch.across.start()
        swaps[1].start()
        swaps[0].wait()

    @pl.when(jnp.logical_not(lacking))
    def _():
        greet(line_peers(place))
        for copy in stays:
            copy.start()
        for fetch in fetches:
            fetch.own.start()
        stays[0].wait()

    def norm(rows):
        centre, scale = moments(tok_buf[rows, :].astype(jnp.float32))
        norm_buf[rows, :] = (centre * scale * gain[...] + shift[...]).astype(jnp.bfloat16)

    tile_rows(norm)
    gather = Gather(norm_buf, normed_full, place, sems[:5])
    gather.start()
    tokens_out = pltpu.make_async_copy(tok_buf, tokens_here, own_sems.at[2])
    tokens_out.start()

    @pl.when(lacking)
    def _():
        fetches[0].spread()
        swaps[1].wait()

    @pl.when(jnp.logical_not(lacking))
    def _():
        stays[1].wait()

    def mask(rows):
        cot_buf[rows, :] = (grad_buf[rows, :].astype(jnp.float32) * live[rows, :]).astype(jnp.bfloat16)

    tile_rows(mask)
    gather_cot = Gather(cot_buf, cot_full, place, sems[5:10])
    gather_cot.start()
    cot_out = pltpu.make_async_copy(cot_buf, cot_here, own_sems.at[3])
    cot_out.start()

    @pl.when(lacking)
    def _():
        fetches[1].spread()
        fetches[2].spread()

    gather.finish()
    gather_cot.finish()
    tokens_out.wait()
    cot_out.wait()

    @pl.when(lacking)
    def _():
        for fetch in fetches:
            fetch.finish()

    @pl.when(jnp.logical_not(lacking))
    def _():
        for fetch in fetches:
            fetch.own.wait()


def middle_kernel(
    part, tokens, gain, shift, gate_up, mid, normed_full, gate_up_here, norm_buf, *scratch
):
    place = here()
    lacking = place[4] != place[2]
    scatter = Scatter(part, place, scratch[:9])
    gather = Gather(norm_buf, normed_full, place, scratch[9:14])
    fetch = Fetch(gate_up, gate_up_here, quarter_gate_up, place, scratch[14:], 0)

    @pl.when(lacking)
    def _():
        greet(line_peers(place) + fetch_peers(place))
        fetch.across.start()

    @pl.when(jnp.logical_not(lacking))
    def _():
        greet(line_peers(place))
        fetch.own.start()

    scatter.start()
    scatter.finish()

    def norm(rows):
        stream = tokens[rows, :].astype(jnp.float32) + scatter.rows(rows)
        mid[rows, :] = stream
        centre, scale = moments(stream)
        norm_buf[rows, :] = (centre * scale * gain[...] + shift[...]).astype(jnp.bfloat16)

    tile_rows(norm)
    gather.start()

    @pl.when(lacking)
    def _():
        fetch.spread()

    gather.finish()

    @pl.when(lacking)
    def _():
        fetch.finish()

    @pl.when(jnp.logical_not(lacking))
    def _():
        fetch.own.wait()


def back_kernel(part, mid, cot, gain, d_mid, d_full, gain_part, shift_part, low_buf, *scratch):
    place = here()
    scatter = Scatter(part, place, scratch[:9])
    gather = Gather(low_buf, d_full, place, scratch[9:])
    greet(line_peers(place))
    scatter.start()
    gain_part[...] = jnp.zeros_like(gain_part)
    shift_part[...] = jnp.zeros_like(shift_part)
    scatter.finish()

    def back(rows):
        grad = scatter.rows(rows)
        centre, scale = moments(mid[rows, :])
        unit = centre * scale
        gain_part[...] += jnp.sum(grad * unit, axis=0, keepdims=True)
        shift_part[...] += jnp.sum(grad, axis=0, keepdims=True)
        scaled = grad * gain[...]
        total = cot[rows, :].astype(jnp.float32) + scale * (
            scaled
            - jnp.mean(scaled, axis=-1, keepdims=True)
            - unit * jnp.mean(scaled * unit, axis=-1, keepdims=True)
        )
        d_mid[rows, :] = total
        low_buf[rows, :] = total.astype(jnp.bfloat16)

    tile_rows(back)
    gather.start()
    gather.finish()


def last_kernel(part, tokens, d_mid, gain, d_in, gain_part, shift_part, *scratch):
    place = here()
    scatter = Scatter(part, place, scratch)
    greet(line_peers(place))
    scatter.start()
    gain_part[...] = jnp.zeros_like(gain_part)
    shift_part[...] = jnp.zeros_like(shift_part)
    scatter.finish()

    def back(rows):
        grad = scatter.rows(rows)
        centre, scale = moments(tokens[rows, :].astype(jnp.float32))
        unit = centre * scale
        gain_part[...] += jnp.sum(grad * unit, axis=0, keepdims=True)
        shift_part[...] += jnp.sum(grad, axis=0, keepdims=True)
        scaled = grad * gain[...]
        d_in[rows, :] = d_mid[rows, :] + scale * (
            scaled
            - jnp.mean(scaled, axis=-1, keepdims=True)
            - unit * jnp.mean(scaled * unit, axis=-1, keepdims=True)
        )

    tile_rows(back)


ANY = pl.BlockSpec(memory_space=pl.ANY)
HELD = pl.BlockSpec(memory_space=pltpu.VMEM)


def call(kernel, collective_id, args, in_specs, outs, out_specs, scratch):
    return pl.pallas_call(
        kernel,
        out_shape=[jax.ShapeDtypeStruct(shape, kind) for shape, kind in outs],
        in_specs=in_specs,
        out_specs=out_specs,
        scratch_shapes=list(scratch),
        compiler_params=pltpu.CompilerParams(
            collective_id=collective_id, has_side_effects=True, vmem_limit_bytes=VMEM_LIMIT
        ),
    )(*args)


def member_layout(seq_length, seq_owner, member, row_total):
    entry_total = seq_length.shape[0]
    row_ids = jnp.arange(row_total, dtype=jnp.int32)
    entry_ids = jnp.arange(entry_total, dtype=jnp.int32)
    earlier = (entry_ids[:, None] < entry_ids[None, :]).astype(jnp.int32)
    sharing = (seq_owner[:, None] == seq_owner[None, :]).astype(jnp.int32)
    starts = jnp.sum(seq_length[:, None] * sharing * earlier, axis=0)
    owned_now = (seq_owner == member).astype(jnp.int32)
    inside = (
        owned_now[None, :]
        * (row_ids[:, None] >= starts[None, :]).astype(jnp.int32)
        * (row_ids[:, None] < (starts + seq_length)[None, :]).astype(jnp.int32)
    )
    live_rows = jnp.sum(inside, axis=1)
    segment = jnp.sum(inside * entry_ids[None, :], axis=1) + (1 - live_rows) * (
        entry_total + row_ids
    )
    position = jnp.sum(inside * (row_ids[:, None] - starts[None, :]), axis=1)
    return (segment, position, live_rows)


def rotary_tables(position):
    half_rot = ROT // 2
    frequency = jnp.power(
        jnp.float32(10000.0), -2.0 * jnp.arange(half_rot, dtype=jnp.float32) / ROT
    )
    angles = position.astype(jnp.float32)[:, None] * frequency[None, :]
    return (jnp.cos(angles)[:, None, :], jnp.sin(angles)[:, None, :])


def rotate(values, cosine, sine_table):
    half_rot = ROT // 2
    first_half = values[..., :half_rot]
    second_half = values[..., half_rot:ROT]
    return jnp.concatenate(
        [
            first_half * cosine - second_half * sine_table,
            second_half * cosine + first_half * sine_table,
            values[..., ROT:],
        ],
        axis=-1,
    )


def contract_rows(left_rows, right_rows):
    return lax.dot_general(
        left_rows, right_rows, (((0,), (0,)), ((), ())), preferred_element_type=jnp.float32
    )


def times_transposed(left_rows, right_rows):
    return lax.dot_general(
        left_rows, right_rows, (((1,), (1,)), ((), ())), preferred_element_type=jnp.float32
    )


def block_mask(segment, row_ids, begin_row, end_row):
    return (segment[begin_row:end_row, None] == segment[None, :end_row]) & (
        row_ids[None, :end_row] <= row_ids[begin_row:end_row, None]
    )


def owns(x, y, z_hi, z_lo, core):
    return core == z_hi


def sum_over_lines(parts):
    x, y, z_hi, z_lo, core = here()
    quarter = parts.shape[1] // SIDE

    def cut(k):
        return lax.dynamic_slice_in_dim(parts, turned(y, k) * quarter, quarter, 1)

    def along(k, held, only=lambda *place: True):
        return permute(
            held,
            lambda x, y, z_hi, z_lo, core: (x, (y + k) % 4, z_hi, z_lo, core)
            if only(x, y, z_hi, z_lo, core)
            else None,
        )

    arrived = [along(k, cut(k)) for k in (1, 2, 3)]
    total = cut(0).astype(jnp.float32)
    for piece in arrived:
        total = total + piece.astype(jnp.float32)
    total = total.astype(jnp.bfloat16)
    arrived = permute(
        total,
        lambda x, y, z_hi, z_lo, core: None
        if core == z_hi
        else (x, y, 1 - z_hi, 1 - z_lo, core),
    )
    total = (total.astype(jnp.float32) + arrived.astype(jnp.float32)).astype(jnp.bfloat16)
    arrived = permute(
        total,
        lambda x, y, z_hi, z_lo, core: (x, y, z_hi, 1 - z_lo, core) if core == z_hi else None,
    )
    total = (total.astype(jnp.float32) + arrived.astype(jnp.float32)).astype(jnp.bfloat16)
    pieces = [total] + [along(k, total, owns) for k in (1, 2, 3)]
    full = jnp.zeros_like(parts)
    for k, piece in enumerate(pieces):
        full = lax.dynamic_update_slice_in_dim(full, piece, turned(y, SIDE - k) * quarter, 1)
    arrived = permute(
        full,
        lambda x, y, z_hi, z_lo, core: (x, y, z_hi, z_lo, 1 - core) if core == z_hi else None,
    )
    return jnp.where(core == z_hi, full, arrived).astype(jnp.float32)


def body(
    tokens,
    seq_length,
    seq_owner,
    ln1_gain,
    ln1_bias,
    qkv_weight,
    qkv_bias,
    out_weight,
    ln2_gain,
    ln2_bias,
    gate_up_weight,
    down_weight,
    out_grad,
):
    bf16, f32 = jnp.bfloat16, jnp.float32
    x, y, z_hi, z_lo, core = here()
    row_total = BLOCK * 8
    rows_here, rows_all = (BLOCK, 2048), (row_total, 2048)
    local_heads = qkv_weight.shape[2] // HEAD_DIM
    member = (y * 2 + z_lo) * 2 + z_hi
    shard = core * SIDE + x
    score_scale = HEAD_DIM ** (-0.5)
    segment, position, live_rows = member_layout(seq_length, seq_owner, member, row_total)
    row_ids = jnp.arange(row_total, dtype=jnp.int32)
    live = lax.dynamic_slice_in_dim(live_rows, shard * BLOCK, BLOCK, 0)[:, None].astype(f32)
    bias = permute(qkv_bias, swap_rows)

    dma = pltpu.SemaphoreType.DMA
    tokens_here, cot, normed1, cot_rows, qkv, out, down = call(
        first_kernel,
        1,
        (tokens, out_grad, live, ln1_gain[None], ln1_bias[None], qkv_weight, out_weight, down_weight),
        [ANY, ANY, HELD, HELD, HELD, ANY, ANY, ANY],
        [
            (rows_here, bf16),
            (rows_here, bf16),
            (rows_all, bf16),
            (rows_all, bf16),
            (qkv_weight.shape, bf16),
            (out_weight.shape, bf16),
            (down_weight.shape, bf16),
        ],
        [ANY] * 4 + [HELD] * 3,
        (pltpu.VMEM(rows_here, bf16),) * 4
        + (dma((2,)), dma((2,)), dma((4,)))
        + Gather.scratch * 2
        + fetch_scratch(3),
    )

    cosine, sine_table = rotary_tables(position)
    projected = [
        jnp.dot(normed1, qkv[channel], preferred_element_type=jnp.float32) + bias[channel]
        for channel in range(3)
    ]
    queries = rotate(
        projected[0].reshape(row_total, local_heads, HEAD_DIM), cosine, sine_table
    ).astype(bf16)
    keys_low = rotate(
        projected[1].reshape(row_total, local_heads, HEAD_DIM), cosine, sine_table
    ).astype(bf16)
    values_low = projected[2].reshape(row_total, local_heads, HEAD_DIM).astype(bf16)
    block_size = min(512, row_total)
    block_count = row_total // block_size
    out_blocks = []
    log_norms = []
    for block_index in range(block_count):
        begin_row = block_index * block_size
        end_row = begin_row + block_size
        allowed = block_mask(segment, row_ids, begin_row, end_row)
        scores = (
            jnp.einsum(
                "qhd,khd->hqk",
                queries[begin_row:end_row],
                keys_low[:end_row],
                preferred_element_type=jnp.float32,
            )
            * score_scale
        )
        scores = jnp.where(allowed[None], scores, -1e30)
        row_max = jnp.max(scores, axis=-1, keepdims=True)
        exp_scores = jnp.exp(scores - row_max)
        exp_sum = jnp.sum(exp_scores, axis=-1, keepdims=True)
        attn_prob = (exp_scores / exp_sum).astype(bf16)
        out_blocks.append(
            jnp.einsum(
                "hqk,khd->qhd", attn_prob, values_low[:end_row], preferred_element_type=jnp.float32
            ).astype(bf16)
        )
        log_norms.append(row_max + jnp.log(exp_sum))
    attended = jnp.concatenate(out_blocks, axis=0).reshape(row_total, local_heads * HEAD_DIM)
    attn_part = jnp.dot(attended, out, preferred_element_type=jnp.float32).astype(bf16)

    gate_up_t = jnp.swapaxes(gate_up_weight, 1, 2)
    mid_stream, normed2, gate_up = call(
        middle_kernel,
        2,
        (attn_part, tokens_here, ln2_gain[None], ln2_bias[None], gate_up_t),
        [ANY, HELD, HELD, HELD, ANY],
        [(rows_here, f32), (rows_all, bf16), (gate_up_t.shape, bf16)],
        [HELD, ANY, HELD],
        (pltpu.VMEM(rows_here, bf16),) + Scatter.scratch + Gather.scratch + fetch_scratch(1),
    )

    gate_act = times_transposed(normed2, gate_up[0])
    up_act = times_transposed(normed2, gate_up[1])
    hidden = (jax.nn.silu(gate_act) * up_act).astype(bf16)
    d_hidden = times_transposed(cot_rows, down)
    sigmoid_g = jax.nn.sigmoid(gate_act)
    d_gate = (d_hidden * up_act * sigmoid_g * (1.0 + gate_act * (1.0 - sigmoid_g))).astype(bf16)
    d_up = (d_hidden * jax.nn.silu(gate_act)).astype(bf16)
    d_norm_part = (
        jnp.dot(d_gate, gate_up[0], preferred_element_type=f32)
        + jnp.dot(d_up, gate_up[1], preferred_element_type=f32)
    ).astype(bf16)

    d_mid, d_rows, gain2_part, shift2_part = call(
        back_kernel,
        3,
        (d_norm_part, mid_stream, cot, ln2_gain[None]),
        [ANY, HELD, HELD, HELD],
        [(rows_here, f32), (rows_all, bf16), ((1, 2048), f32), ((1, 2048), f32)],
        [HELD, ANY, HELD, HELD],
        (pltpu.VMEM(rows_here, bf16),) + Scatter.scratch + Gather.scratch,
    )

    ffn_part = jnp.dot(hidden, down, preferred_element_type=jnp.float32).astype(bf16)
    ffn_part = ffn_part.reshape(2, SIDE, BLOCK, 2048)
    kept = lax.dynamic_index_in_dim(ffn_part, core, 0, False)
    given = lax.dynamic_index_in_dim(ffn_part, 1 - core, 0, False)
    arrived = permute(given, lambda x, y, z_hi, z_lo, core: (x, y, z_hi, z_lo, 1 - core))
    both = (kept.astype(f32) + arrived.astype(f32)).astype(bf16)
    mixed = mid_stream + lax.dynamic_index_in_dim(both, x, 0, False).astype(f32)
    for k in (1, 2, 3):
        arrived = permute(
            lax.dynamic_index_in_dim(both, turned(x, k), 0, False),
            lambda x, y, z_hi, z_lo, core, k=k: ((x + k) % 4, y, z_hi, z_lo, core),
        )
        mixed = mixed + arrived.astype(f32)
    mixed = permute(mixed.astype(bf16), swap_rows)

    ffn_grad = jnp.stack(
        [contract_rows(d_gate, normed2), contract_rows(d_up, normed2), contract_rows(hidden, cot_rows)]
    ).astype(bf16)
    ffn_grad = sum_over_lines(ffn_grad)
    gate_up_grad, down_grad = jnp.swapaxes(ffn_grad[:2], 1, 2), ffn_grad[2]

    out_grad_t = contract_rows(d_rows, attended)
    d_attended = (
        times_transposed(d_rows, out).astype(bf16).reshape(row_total, local_heads, HEAD_DIM)
    )
    query_grads = []
    d_key = jnp.zeros((row_total, local_heads, HEAD_DIM), f32)
    d_value = jnp.zeros((row_total, local_heads, HEAD_DIM), f32)
    for block_index in range(block_count):
        begin_row = block_index * block_size
        end_row = begin_row + block_size
        allowed = block_mask(segment, row_ids, begin_row, end_row)
        query_block = queries[begin_row:end_row]
        key_block = keys_low[:end_row]
        grad_block = d_attended[begin_row:end_row]
        scores = (
            jnp.einsum("qhd,khd->hqk", query_block, key_block, preferred_element_type=jnp.float32)
            * score_scale
        )
        scores = jnp.where(allowed[None], scores, -1e30)
        attn_full = jnp.exp(scores - log_norms[block_index])
        attn_prob = attn_full.astype(bf16)
        d_prob = jnp.einsum(
            "qhd,khd->hqk", grad_block, values_low[:end_row], preferred_element_type=jnp.float32
        )
        row_dots = jnp.sum(attn_full * d_prob, axis=-1, keepdims=True)
        d_score = (attn_full * (d_prob - row_dots)).astype(bf16)
        query_grads.append(
            jnp.einsum("hqk,khd->qhd", d_score, key_block, preferred_element_type=jnp.float32)
            * score_scale
        )
        d_key = d_key.at[:end_row].add(
            jnp.einsum("hqk,qhd->khd", d_score, query_block, preferred_element_type=jnp.float32)
            * score_scale
        )
        d_value = d_value.at[:end_row].add(
            jnp.einsum("hqk,qhd->khd", attn_prob, grad_block, preferred_element_type=jnp.float32)
        )
    d_query = jnp.concatenate(query_grads, axis=0)
    d_proj = [
        rotate(d_query, cosine, -sine_table).reshape(row_total, -1).astype(bf16),
        rotate(d_key, cosine, -sine_table).reshape(row_total, -1).astype(bf16),
        d_value.reshape(row_total, -1).astype(bf16),
    ]
    summed = times_transposed(d_proj[0], qkv[0])
    summed = summed + times_transposed(d_proj[1], qkv[1])
    d_norm_part = (summed + times_transposed(d_proj[2], qkv[2])).astype(bf16)

    d_in, gain1_part, shift1_part = call(
        last_kernel,
        4,
        (d_norm_part, tokens_here, d_mid, ln1_gain[None]),
        [ANY, HELD, HELD, HELD],
        [(rows_here, f32), ((1, 2048), f32), ((1, 2048), f32)],
        [HELD, HELD, HELD],
        Scatter.scratch,
    )
    input_grad = permute(d_in, swap_rows)

    attn_grad = jnp.stack(
        [contract_rows(normed1, d_proj[channel]) for channel in range(3)] + [out_grad_t]
    ).astype(bf16)
    attn_grad = sum_over_lines(attn_grad)
    qkv_weight_grad, out_weight_grad = attn_grad[:3], attn_grad[3].T

    bias_part = jnp.stack([jnp.sum(d.astype(f32), axis=0) for d in d_proj])
    spread = jnp.zeros((8, 3, bias_part.shape[1]), f32)
    spread = lax.dynamic_update_slice_in_dim(spread, bias_part[None], shard, 0)
    norm_grads, bias_all = lax.psum(
        (jnp.concatenate([gain1_part, shift1_part, gain2_part, shift2_part]), spread), AXES
    )
    qkv_bias_grad = lax.dynamic_index_in_dim(bias_all, z_hi * SIDE + x, 0, False)
    return (
        mixed,
        input_grad,
        norm_grads[0],
        norm_grads[1],
        qkv_weight_grad,
        qkv_bias_grad,
        out_weight_grad,
        norm_grads[2],
        norm_grads[3],
        gate_up_grad,
        down_grad,
    )


def solution(mesh):
    placed = (
        P(("dp", "tensor"), None),
        P(),
        P(),
        P(),
        P(),
        P(None, None, "tensor"),
        P(None, "tensor"),
        P("tensor", None),
        P(),
        P(),
        P(None, None, "tensor"),
        P("tensor", None),
        P(("dp", "tensor"), None),
    )
    return jax.shard_map(
        body,
        mesh=mesh,
        in_specs=placed,
        out_specs=(
            P(("dp", "tensor"), None),
            P(("dp", "tensor"), None),
            P(),
            P(),
            P(None, None, "tensor"),
            P(None, "tensor"),
            P("tensor", None),
            P(),
            P(),
            P(None, None, "tensor"),
            P("tensor", None),
        ),
        check_vma=False,
    )
```

time: 1090 us -> 770 us (0.71)
  waiting for transfers between devices: 797 us -> 163 us
  Pallas kernels: 0 us -> 245 us
  starting transfers between devices: 0.37 us -> 76.1 us
  local copies, waits for them, and re-layouts: 10.5 us -> 73.5 us
  blocking collectives: 107 us -> 65.8 us
  between operations: 15 us -> 2.29 us
  matrix products: 100 us -> 88.8 us
    reduce_scatter x4 -> x0, waiting for transfers between devices: 327 us -> none  [the longest x1 113 us: body(): lax.psum_scatter(jnp.dot(attended, out_weight, preferred_element_type=jnp...]
    all_gather x4 -> x0, waiting for transfers between devices: 263 us -> none  [the longest x1 71 us: body(): lax.all_gather(d_mid.astype(jnp.bfloat16), 'tensor', axis=0, tiled=True)]
    pallas_call x0 -> x4, Pallas kernels: none -> 245 us  [call(): pl.pallas_call(kernel, out_shape=[jax.ShapeDtypeStruct(shape, kind) for s...]
    psum x1 -> x0, waiting for transfers between devices: 207 us -> none  [body(): lax.psum(qkv_weight_grad.astype(jnp.bfloat16), 'dp').astype(jnp.float32)]
    ppermute x0 -> x25, waiting for transfers between devices: none -> 163 us  [permute(): return lax.ppermute(array, AXES, pairs(move))]
    ppermute x0 -> x25, starting transfers between devices: none -> 76.1 us  [permute(): return lax.ppermute(array, AXES, pairs(move))]
    psum x2 -> x1, blocking collectives: 107 us -> 65.8 us  [body(): lax.psum((jnp.concatenate([gain1_part, shift1_part, gain2_part, shift2_pa...]
    transpose x0 -> x2, local copies, waits for them, and re-layouts: none -> 13.8 us  [the longest x1 10.6 us: body(): gate_up_grad, down_grad = (jnp.swapaxes(ffn_grad[:2], 1, 2), ffn_grad[2])]
  transfers between devices with their start and end apart: 9 -> 25, of which waited for: 9 -> 10; matrix products, arithmetic and copies ran while one was open for 6% -> 13% of each run, Pallas kernels for 0% -> 15%
where the time goes in v1:
time: 770 us; the launch traced here: 759 us
  Pallas kernels  245 us (32%)
  waiting for transfers between devices  163 us (21%)
  matrix products  88.8 us (12%)
  starting transfers between devices  76.1 us (10%)
  local copies, waits for them, and re-layouts  73.5 us (10%)
  blocking collectives  65.8 us (9%)
  other arithmetic  45.1 us (6%)
    pallas_call x4, Pallas kernels, call(): pl.pallas_call(kernel, out_shape=[jax.ShapeDtypeStruct(shape, kind) for s...  245 us
    ppermute x25, waiting for transfers between devices, permute(): return lax.ppermute(array, AXES, pairs(move))  163 us
    ppermute x25, starting transfers between devices, permute(): return lax.ppermute(array, AXES, pairs(move))  76.1 us
    psum x1, blocking collectives, body(): lax.psum((jnp.concatenate([gain1_part, shift1_part, gain2_part, shift2_pa...  65.8 us
    dot_general x7, matrix products, times_transposed(): lax.dot_general(left_rows, right_rows, (((1,), (1,)), ((), ())), preferre...  28.7 us
    unnamed x77, local copies, waits for them, and re-layouts  19.2 us
    dot_general x7, matrix products, contract_rows(): lax.dot_general(left_rows, right_rows, (((0,), (0,)), ((), ())), preferre...  18.1 us
  transfers between devices with their start and end apart: 25, of which 10 were waited for; matrix products, arithmetic and copies ran while one was open for 13% of the time, Pallas kernels for 15%

profile of v1, /device:TPU:1, one launch (start us, length us, event | category | flops | bytes accessed | tf_op | source)
XLA Modules:
  0.0 759.5 jit_solution(15032857598673248603)
XLA Ops:
  0.6 6.9 collective-permute-start
  12.0 71.0 %shard_map.222 = (bf16[128,2048]{1,0:T(8,128)(2,1)}, bf16[128,2048]{1,0:T(8,128)(2,1)}, bf16[1024,2048]{1,0:T(8,128)(2,1)}, bf16[1024,2048]{1,0:T(8,128)(2,1)}, ...) custom-call(bf16[128,2048]{1,0:T(8,128)(2,1)} %tokens.1, ...), custom_call_target="tpu_custom_call" | custom-call | tf_op jit(solution)/shard_map/pallas_call | solution.py:482
  83.0 3.9 add_convert_fusion.8
  90.6 1.8 fusion.91
  93.3 1.9 fusion
  95.8 2.1 fusion.52
  99.7 3.3 convolution_convert_fusion.1.part
  103.0 68.8 %shard_map.223 = (f32[128,2048]{1,0:T(8,128)}, bf16[1024,2048]{1,0:T(8,128)(2,1)}, bf16[2,704,2048]{2,1,0:T(8,128)(2,1)}) custom-call(bf16[1024,2048]{1,0:T(8,128)(2,1)} %convolution_convert_fusion.1.part, bf16[128,2048]{1,0:T(8,128)(2,1)} %get-tuple-element.95.tokens, f32[1,2048]{1,0:T(1,128)} %bitcast.189, f32[1,2048]{1,0:T(1,128)} %bitcast.193, ...), custom_call_target="tpu_custom_call" | custom-call | tf_op jit(solution)/shard_map/pallas_call | solution.py:482
  171.9 6.0 fusion.17
  177.9 4.8 fusion.13
  182.7 7.0 multiply_convert_fusion.2
  189.7 3.5 fusion.15
  193.2 4.5 fusion.9
  197.7 4.7 fusion.10
  202.4 5.3 add_convert_fusion.1.part
  207.7 60.5 %shard_map.224 = (f32[128,2048]{1,0:T(8,128)}, bf16[1024,2048]{1,0:T(8,128)(2,1)}, f32[1,2048]{1,0:T(1,128)}, f32[1,2048]{1,0:T(1,128)}) custom-call(bf16[1024,2048]{1,0:T(8,128)(2,1)} %add_convert_fusion.1.part, f32[128,2048]{1,0:T(8,128)} %get-tuple-element.96.mid, bf16[128,2048]{1,0:T(8,128)(2,1)} %get-tuple-element.101.cot, f32[1,2048]{1,0:T(1,128)} %bitcast.190), custom_call_target="tpu_custom_call" | custom-call | tf_op jit(solution)/shard_map/pallas_call | solution.py:482
  268.3 3.6 convolution_convert_fusion.9
  272.1 3.4 fusion.11
  276.6 3.0 constant_dynamic-slice_fusion.2
  286.1 4.9 multiply_reduce_fusion
  290.9 4.3 multiply_convert_fusion
  295.3 33.1 %collective-permute-done.18 = bf16[3,176,2048]{2,1,0:T(8,128)(2,1)} collective-permute-done((bf16[3,176,2048]{2,1,0:T(8,128)(2,1)}, bf16[3,176,2048]{2,1,0:T(8,128)(2,1)}, u32[]{:S(2)}, u32[]{:S(2)}) %collective-permute-start.18) | collective-permute-done | bytes 2162720 | tf_op jit(solution)/shard_map/ppermute | solution.py:46
  328.4 2.6 collective-permute-done.17
  331.0 47.1 %collective-permute-done.16 = bf16[3,176,2048]{2,1,0:T(8,128)(2,1)} collective-permute-done((bf16[3,176,2048]{2,1,0:T(8,128)(2,1)}, bf16[3,176,2048]{2,1,0:T(8,128)(2,1)}, u32[]{:S(2)}, u32[]{:S(2)}) %collective-permute-start.16) | collective-permute-done | bytes 2162720 | tf_op jit(solution)/shard_map/ppermute | solution.py:46
  378.1 6.1 add_convert_fusion.4
  384.2 6.2 collective-permute-start.19
  394.3 1.9 convert_reduce_fusion
  396.2 18.0 %collective-permute-done.19 = bf16[3,176,2048]{2,1,0:T(8,128)(2,1)S(1)} collective-permute-done((bf16[3,176,2048]{2,1,0:T(8,128)(2,1)}, bf16[3,176,2048]{2,1,0:T(8,128)(2,1)S(1)}, u32[]{:S(2)}, u32[]{:S(2)}) %collective-permute-start.19) | collective-permute-done | bytes 2162720 | tf_op jit(solution)/shard_map/ppermute | solution.py:46
  422.4 2.0 copy-done.2
  424.4 1.7 constant_dynamic-slice_fusion.6
  427.6 4.6 broadcast_in_dim.59
  432.2 3.1 constant_dynamic-update-slice_fusion.1
  435.3 2.0 collective-permute-start.21
  438.1 10.7 %collective-permute-done.9 = bf16[4,512,256]{2,1,0:T(8,128)(2,1)S(1)} collective-permute-done((bf16[4,512,256]{2,1,0:T(8,128)(2,1)}, bf16[4,512,256]{2,1,0:T(8,128)(2,1)S(1)}, u32[]{:S(2)}, u32[]{:S(2)}) %collective-permute-start.9) | collective-permute-done | bytes 1048608 | tf_op jit(solution)/shard_map/ppermute | solution.py:46
  449.7 25.8 %collective-permute-done.7 = bf16[4,512,256]{2,1,0:T(8,128)(2,1)} collective-permute-done((bf16[4,512,256]{2,1,0:T(8,128)(2,1)}, bf16[4,512,256]{2,1,0:T(8,128)(2,1)}, u32[]{:S(2)}, u32[]{:S(2)}) %collective-permute-start.7) | collective-permute-done | bytes 1048608 | tf_op jit(solution)/shard_map/ppermute | solution.py:46
  475.5 2.4 add_convert_fusion.7
  477.9 3.5 collective-permute-start.10
  481.4 11.7 %collective-permute-done.10 = bf16[4,512,256]{2,1,0:T(8,128)(2,1)S(1)} collective-permute-done((bf16[4,512,256]{2,1,0:T(8,128)(2,1)S(1)}, bf16[4,512,256]{2,1,0:T(8,128)(2,1)S(1)}, u32[]{:S(2)}, u32[]{:S(2)}) %collective-permute-start.10) | collective-permute-done | bytes 1048608 | tf_op jit(solution)/shard_map/ppermute | solution.py:46
  495.0 3.2 constant_dynamic-update-slice_fusion
  504.7 1.7 collective-permute-start.13
  506.3 1.8 collective-permute-start.14
  508.2 5.7 convolution_convert_fusion
  513.9 2.0 copy-done.4
  517.5 32.6 %collective-permute-start.1 = (bf16[4,128,2048]{2,1,0:T(8,128)(2,1)}, bf16[4,128,2048]{2,1,0:T(8,128)(2,1)}, u32[]{:S(2)}, u32[]{:S(2)}) collective-permute-start(bf16[4,128,2048]{2,1,0:T(8,128)(2,1)} %dynamic-slice_bitcast_fusion), channel_id=1, source_target_pairs={{0,8},{1,9},{2,10},{3,11},{4,12},{5,13},{6,14},{7,15},{8,0},{9,1},... | collective-permute-start | bytes 6291464 | tf_op jit(solution)/shard_map/ppermute | solution.py:46
  550.6 2.5 broadcast_in_dim.56
  562.3 2.7 fusion.64
  567.2 2.4 fusion.4
  571.4 1.6 collective-permute-start.3
  573.3 3.4 add_convert_fusion.part
  577.0 44.9 %shard_map.225 = (f32[128,2048]{1,0:T(8,128)}, f32[1,2048]{1,0:T(1,128)}, f32[1,2048]{1,0:T(1,128)}) custom-call(bf16[1024,2048]{1,0:T(8,128)(2,1)} %add_convert_fusion.part, bf16[128,2048]{1,0:T(8,128)(2,1)} %get-tuple-element.95.tokens, f32[128,2048]{1,0:T(8,128)} %get-tuple-element.103.d_mid, f32[1,2048]{1,0:T(1,128)} %bitcast.192), custom_call_target="tpu_custom_call" | custom-call | tf_op jit(solution)/shard_map/pallas_call | solution.py:482
  622.7 65.8 %all-reduce.2 = (f32[4,2048]{1,0:T(4,128)S(1)}, f32[8,3,256]{2,1,0:T(4,128)S(1)}) all-reduce(f32[4,2048]{1,0:T(4,128)S(1)} %pad_maximum_fusion.10, f32[8,3,256]{2,1,0:T(4,128)S(1)} %constant_dynamic-update-slice_fusion.2), channel_id=1, replica_groups=mesh['dp'=16,'tensor'=8] {'dp','tensor'}, use_global_device_ids=true, to_apply=%region_10.11 | all-reduce | flops 14336 | bytes 114688 | tf_op jit(solution)/shard_map/psum | solution.py:817
  688.5 4.0 collective-permute-start.6
  692.5 1.7 fusion.59
  694.3 3.1 collective-permute-start.5
  698.6 7.7 %collective-permute-done.6 = f32[128,2048]{1,0:T(8,128)S(1)} collective-permute-done((f32[128,2048]{1,0:T(8,128)}, f32[128,2048]{1,0:T(8,128)S(1)}, u32[]{:S(2)}, u32[]{:S(2)}) %collective-permute-start.6) | collective-permute-done | bytes 1048608 | tf_op jit(solution)/shard_map/ppermute | solution.py:46
  706.3 5.6 collective-permute-done.5
  712.0 2.7 select_convert_fusion.1
  714.7 3.3 copy-done.1
  718.0 3.1 slice.282
  721.1 6.6 copy.43
  727.7 3.1 slice_bitcast_fusion.2
  730.8 9.8 %select_convert_fusion = f32[3,704,2048]{2,1,0:T(8,128)} fusion(bf16[3,704,2048]{2,1,0:T(8,128)(2,1)} %constant_dynamic-update-slice_fusion.7, bf16[3,704,2048]{2,1,0:T(8,128)(2,1)} %collective-permute-done.24, pred[]{:T(512)S(6)} %eq.82), kind=kLoop, calls=%fused_computation.2 | loop fusion | flops 8650752 | bytes 34603008 | tf_op jit(solution)/shard_map/convert_element_type | solution.py:600
  740.7 10.6 %slice_bitcast_fusion = f32[2,2048,704]{1,2,0:T(8,128)} fusion(f32[3,704,2048]{2,1,0:T(8,128)} %select_convert_fusion), kind=kLoop, calls=%fused_computation | loop fusion | bytes 23068672 | tf_op jit(solution)/shard_map/transpose | solution.py:748
  751.3 6.0 slice_bitcast_fusion.1
  (178 shorter events, 61.8 us)
Async XLA Ops:
  0.6 82.4 %collective-permute-start = (f32[3,256]{1,0:T(4,128)}, f32[3,256]{1,0:T(4,128)S(1)}, u32[]{:S(2)}, u32[]{:S(2)}) collective-permute-start(f32[3,256]{1,0:T(4,128)} %param.31), channel_id=1, source_target_pairs={{0,0},{1,1},{2,2},{3,3},{4,8},{5,9},{6,10},{7,11},{8,4},{9,5},{10,... | collective-permute-start | bytes 9224 | tf_op jit(solution)/shard_map/ppermute | solution.py:46
  83.0 4.0 copy-start.7
  83.0 4.7 copy-start.25
  87.0 8.2 %copy-start.17 = (bf16[1024,256]{0,1:T(8,128)(2,1)}, bf16[1024,256]{0,1:T(8,128)(2,1)S(1)}, u32[]{:S(2)}) copy-start(bf16[1024,256]{0,1:T(8,128)(2,1)S(1)} %add_convert_fusion.8) | copy-start | bytes 1572868
  92.4 3.4 copy-start
  98.5 1.2 copy-start.21
  171.9 6.0 copy-start.24
  171.9 6.0 copy-start.30
  177.9 4.8 copy-start.28
  177.9 4.8 copy-start.31
  193.2 4.5 copy-start.32
  197.7 4.7 copy-start.33
  268.2 3.7 copy-start.29
  268.3 3.9 copy-start.34
  272.1 3.4 copy-start.9
  272.1 3.4 copy-start.10
  279.6 48.8 %collective-permute-start.18 = (bf16[3,176,2048]{2,1,0:T(8,128)(2,1)}, bf16[3,176,2048]{2,1,0:T(8,128)(2,1)}, u32[]{:S(2)}, u32[]{:S(2)}) collective-permute-start(bf16[3,176,2048]{2,1,0:T(8,128)(2,1)} %get-tuple-element.146), channel_id=1, source_target_pairs={{0,96},{1,97},{2,98},{3,99},{4,100},{5,101},{6,102},{7,103},{8,104... | collective-permute-start | bytes 6488072 | tf_op jit(solution)/shard_map/ppermute | solution.py:46
  281.0 50.0 %collective-permute-start.17 = (bf16[3,176,2048]{2,1,0:T(8,128)(2,1)}, bf16[3,176,2048]{2,1,0:T(8,128)(2,1)}, u32[]{:S(2)}, u32[]{:S(2)}) collective-permute-start(bf16[3,176,2048]{2,1,0:T(8,128)(2,1)} %get-tuple-element.147), channel_id=1, source_target_pairs={{0,64},{1,65},{2,66},{3,67},{4,68},{5,69},{6,70},{7,71},{8,72},{9,... | collective-permute-start | bytes 6488072 | tf_op jit(solution)/shard_map/ppermute | solution.py:46
  281.5 96.7 %collective-permute-start.16 = (bf16[3,176,2048]{2,1,0:T(8,128)(2,1)}, bf16[3,176,2048]{2,1,0:T(8,128)(2,1)}, u32[]{:S(2)}, u32[]{:S(2)}) collective-permute-start(bf16[3,176,2048]{2,1,0:T(8,128)(2,1)} %get-tuple-element.145), channel_id=1, source_target_pairs={{0,32},{1,33},{2,34},{3,35},{4,36},{5,37},{6,38},{7,39},{8,40},{9,... | collective-permute-start | bytes 6488072 | tf_op jit(solution)/shard_map/ppermute | solution.py:46
  282.3 2.9 slice-start
  283.3 2.7 slice-start.1
  283.3 2.7 copy-start.18
  384.2 30.0 %collective-permute-start.19 = (bf16[3,176,2048]{2,1,0:T(8,128)(2,1)}, bf16[3,176,2048]{2,1,0:T(8,128)(2,1)S(1)}, u32[]{:S(2)}, u32[]{:S(2)}) collective-permute-start(bf16[3,176,2048]{2,1,0:T(8,128)(2,1)} %add_convert_fusion.4), channel_id=1, source_target_pairs={{4,16},{5,17},{6,18},{7,19},{8,28},{9,29},{10,30},{11,31},{20,0},{... | collective-permute-start | bytes 6488072 | tf_op jit(solution)/shard_map/ppermute | solution.py:46
  393.5 25.5 %copy-start.11 = (bf16[1024,4,64]{0,2,1:T(8,128)(2,1)}, bf16[1024,4,64]{0,2,1:T(8,128)(2,1)S(1)}, u32[]{:S(2)}) copy-start(bf16[1024,4,64]{0,2,1:T(8,128)(2,1)S(1)} %get-tuple-element.141) | copy-start | bytes 1572868
  393.5 26.9 %copy-start.13 = (bf16[1024,4,64]{0,2,1:T(8,128)(2,1)}, bf16[1024,4,64]{0,2,1:T(8,128)(2,1)S(1)}, u32[]{:S(2)}) copy-start(bf16[1024,4,64]{0,2,1:T(8,128)(2,1)S(1)} %get-tuple-element.191) | copy-start | bytes 1572868
  394.3 19.9 %copy-start.3 = (bf16[3,176,2048]{2,1,0:T(8,128)(2,1)S(1)}, bf16[3,176,2048]{2,1,0:T(8,128)(2,1)}, u32[]{:S(2)}) copy-start(bf16[3,176,2048]{2,1,0:T(8,128)(2,1)} %add_convert_fusion.4) | copy-start | bytes 6488068
  396.2 21.4 %copy-start.15 = (bf16[1024,4,64]{0,2,1:T(8,128)(2,1)}, bf16[1024,4,64]{0,2,1:T(8,128)(2,1)S(1)}, u32[]{:S(2)}) copy-start(bf16[1024,4,64]{0,2,1:T(8,128)(2,1)S(1)} %get-tuple-element.189) | copy-start | bytes 1572868
  396.2 20.0 %copy-start.27 = (bf16[1024,2048]{1,0:T(8,128)(2,1)S(1)}, bf16[1024,2048]{1,0:T(8,128)(2,1)}, u32[]{:S(2)}) copy-start(bf16[1024,2048]{1,0:T(8,128)(2,1)} %get-tuple-element.102) | copy-start | bytes 12582916
  415.1 2.5 copy-start.26
  415.1 12.5 %collective-permute-start.20 = (bf16[3,176,2048]{2,1,0:T(8,128)(2,1)S(1)}, bf16[3,176,2048]{2,1,0:T(8,128)(2,1)S(1)}, u32[]{:S(2)}, u32[]{:S(2)}) collective-permute-start(bf16[3,176,2048]{2,1,0:T(8,128)(2,1)S(1)} %add_convert_fusion.3), channel_id=1, source_target_pairs={{0,16},{1,17},{2,18},{3,19},{12,28},{13,29},{14,30},{15,31},{16,0}... | collective-permute-start | bytes 6488072 | tf_op jit(solution)/shard_map/ppermute | solution.py:46
  422.4 2.0 copy-start.2
  426.1 22.6 %collective-permute-start.9 = (bf16[4,512,256]{2,1,0:T(8,128)(2,1)}, bf16[4,512,256]{2,1,0:T(8,128)(2,1)S(1)}, u32[]{:S(2)}, u32[]{:S(2)}) collective-permute-start(bf16[4,512,256]{2,1,0:T(8,128)(2,1)} %get-tuple-element.152), channel_id=1, source_target_pairs={{0,96},{1,97},{2,98},{3,99},{4,100},{5,101},{6,102},{7,103},{8,104... | collective-permute-start | bytes 3145736 | tf_op jit(solution)/shard_map/ppermute | solution.py:46
  426.1 23.6 %collective-permute-start.8 = (bf16[4,512,256]{2,1,0:T(8,128)(2,1)}, bf16[4,512,256]{2,1,0:T(8,128)(2,1)}, u32[]{:S(2)}, u32[]{:S(2)}) collective-permute-start(bf16[4,512,256]{2,1,0:T(8,128)(2,1)} %get-tuple-element.153), channel_id=1, source_target_pairs={{0,64},{1,65},{2,66},{3,67},{4,68},{5,69},{6,70},{7,71},{8,72},{9,... | collective-permute-start | bytes 3145736 | tf_op jit(solution)/shard_map/ppermute | solution.py:46
  426.6 48.9 %collective-permute-start.7 = (bf16[4,512,256]{2,1,0:T(8,128)(2,1)}, bf16[4,512,256]{2,1,0:T(8,128)(2,1)}, u32[]{:S(2)}, u32[]{:S(2)}) collective-permute-start(bf16[4,512,256]{2,1,0:T(8,128)(2,1)} %get-tuple-element.151), channel_id=1, source_target_pairs={{0,32},{1,33},{2,34},{3,35},{4,36},{5,37},{6,38},{7,39},{8,40},{9,... | collective-permute-start | bytes 3145736 | tf_op jit(solution)/shard_map/ppermute | solution.py:46
  435.3 59.7 %collective-permute-start.21 = (bf16[3,176,2048]{2,1,0:T(8,128)(2,1)}, bf16[3,176,2048]{2,1,0:T(8,128)(2,1)}, u32[]{:S(2)}, u32[]{:S(2)}) collective-permute-start(bf16[3,176,2048]{2,1,0:T(8,128)(2,1)} %get-tuple-element.137), channel_id=1, source_target_pairs={{0,32},{1,33},{2,34},{3,35},{12,44},{13,45},{14,46},{15,47},{16,48... | collective-permute-start | bytes 6488072 | tf_op jit(solution)/shard_map/ppermute | solution.py:46
  437.3 60.9 %collective-permute-start.22 = (bf16[3,176,2048]{2,1,0:T(8,128)(2,1)}, bf16[3,176,2048]{2,1,0:T(8,128)(2,1)S(1)}, u32[]{:S(2)}, u32[]{:S(2)}) collective-permute-start(bf16[3,176,2048]{2,1,0:T(8,128)(2,1)} %get-tuple-element.137), channel_id=1, source_target_pairs={{0,64},{1,65},{2,66},{3,67},{12,76},{13,77},{14,78},{15,79},{16,80... | collective-permute-start | bytes 6488072 | tf_op jit(solution)/shard_map/ppermute | solution.py:46
  448.8 50.9 %collective-permute-start.23 = (bf16[3,176,2048]{2,1,0:T(8,128)(2,1)}, bf16[3,176,2048]{2,1,0:T(8,128)(2,1)S(1)}, u32[]{:S(2)}, u32[]{:S(2)}) collective-permute-start(bf16[3,176,2048]{2,1,0:T(8,128)(2,1)} %get-tuple-element.137), channel_id=1, source_target_pairs={{0,96},{1,97},{2,98},{3,99},{12,108},{13,109},{14,110},{15,111},{1... | collective-permute-start | bytes 6488072 | tf_op jit(solution)/shard_map/ppermute | solution.py:46
  477.9 15.1 %collective-permute-start.10 = (bf16[4,512,256]{2,1,0:T(8,128)(2,1)S(1)}, bf16[4,512,256]{2,1,0:T(8,128)(2,1)S(1)}, u32[]{:S(2)}, u32[]{:S(2)}) collective-permute-start(bf16[4,512,256]{2,1,0:T(8,128)(2,1)S(1)} %add_convert_fusion.7), channel_id=1, source_target_pairs={{4,16},{5,17},{6,18},{7,19},{8,28},{9,29},{10,30},{11,31},{20,0},{... | collective-permute-start | bytes 3145736 | tf_op jit(solution)/shard_map/ppermute | solution.py:46
  493.3 9.1 %collective-permute-start.11 = (bf16[4,512,256]{2,1,0:T(8,128)(2,1)S(1)}, bf16[4,512,256]{2,1,0:T(8,128)(2,1)}, u32[]{:S(2)}, u32[]{:S(2)}) collective-permute-start(bf16[4,512,256]{2,1,0:T(8,128)(2,1)S(1)} %add_convert_fusion.6), channel_id=1, source_target_pairs={{0,16},{1,17},{2,18},{3,19},{12,28},{13,29},{14,30},{15,31},{16,0}... | collective-permute-start | bytes 3145736 | tf_op jit(solution)/shard_map/ppermute | solution.py:46
  501.2 229.7 %collective-permute-start.24 = (bf16[3,704,2048]{2,1,0:T(8,128)(2,1)}, bf16[3,704,2048]{2,1,0:T(8,128)(2,1)}, u32[]{:S(2)}, u32[]{:S(2)}) collective-permute-start(bf16[3,704,2048]{2,1,0:T(8,128)(2,1)} %constant_dynamic-update-slice_fusion.7), channel_id=1, source_target_pairs={{0,8},{1,9},{2,10},{3,11},{12,4},{13,5},{14,6},{15,7},{16,24},{17,... | collective-permute-start | bytes 25952264 | tf_op jit(solution)/shard_map/ppermute | solution.py:46
  503.9 50.3 %collective-permute-start.12 = (bf16[4,512,256]{2,1,0:T(8,128)(2,1)S(1)}, bf16[4,512,256]{2,1,0:T(8,128)(2,1)S(1)}, u32[]{:S(2)}, u32[]{:S(2)}) collective-permute-start(bf16[4,512,256]{2,1,0:T(8,128)(2,1)S(1)} %add_convert_fusion.5), channel_id=1, source_target_pairs={{0,32},{1,33},{2,34},{3,35},{12,44},{13,45},{14,46},{15,47},{16,48... | collective-permute-start | bytes 3145736 | tf_op jit(solution)/shard_map/ppermute | solution.py:46
  504.7 50.1 %collective-permute-start.13 = (bf16[4,512,256]{2,1,0:T(8,128)(2,1)S(1)}, bf16[4,512,256]{2,1,0:T(8,128)(2,1)}, u32[]{:S(2)}, u32[]{:S(2)}) collective-permute-start(bf16[4,512,256]{2,1,0:T(8,128)(2,1)S(1)} %add_convert_fusion.5), channel_id=1, source_target_pairs={{0,64},{1,65},{2,66},{3,67},{12,76},{13,77},{14,78},{15,79},{16,80... | collective-permute-start | bytes 3145736 | tf_op jit(solution)/shard_map/ppermute | solution.py:46
  506.3 49.9 %collective-permute-start.14 = (bf16[4,512,256]{2,1,0:T(8,128)(2,1)S(1)}, bf16[4,512,256]{2,1,0:T(8,128)(2,1)}, u32[]{:S(2)}, u32[]{:S(2)}) collective-permute-start(bf16[4,512,256]{2,1,0:T(8,128)(2,1)S(1)} %add_convert_fusion.5), channel_id=1, source_target_pairs={{0,96},{1,97},{2,98},{3,99},{12,108},{13,109},{14,110},{15,111},{1... | collective-permute-start | bytes 3145736 | tf_op jit(solution)/shard_map/ppermute | solution.py:46
  513.9 2.0 copy-start.4
  517.5 48.8 %collective-permute-start.1 = (bf16[4,128,2048]{2,1,0:T(8,128)(2,1)}, bf16[4,128,2048]{2,1,0:T(8,128)(2,1)}, u32[]{:S(2)}, u32[]{:S(2)}) collective-permute-start(bf16[4,128,2048]{2,1,0:T(8,128)(2,1)} %dynamic-slice_bitcast_fusion), channel_id=1, source_target_pairs={{0,8},{1,9},{2,10},{3,11},{4,12},{5,13},{6,14},{7,15},{8,0},{9,1},... | collective-permute-start | bytes 6291464 | tf_op jit(solution)/shard_map/ppermute | solution.py:46
  558.8 3.4 copy-start.14
  560.9 151.1 %collective-permute-start.15 = (bf16[4,2048,256]{1,2,0:T(8,128)(2,1)}, bf16[4,2048,256]{1,2,0:T(8,128)(2,1)}, u32[]{:S(2)}, u32[]{:S(2)}) collective-permute-start(bf16[4,2048,256]{1,2,0:T(8,128)(2,1)} %constant_dynamic-update-slice_fusion.3), channel_id=1, source_target_pairs={{0,8},{1,9},{2,10},{3,11},{12,4},{13,5},{14,6},{15,7},{16,24},{17,... | collective-permute-start | bytes 12582920 | tf_op jit(solution)/shard_map/ppermute | solution.py:46
  562.2 2.7 copy-start.8
  562.2 2.7 copy-start.12
  565.0 2.2 copy-start.5
  566.3 7.0 copy-start.16
  570.7 117.8 %collective-permute-start.4 = (bf16[128,2048]{1,0:T(8,128)(2,1)}, bf16[128,2048]{1,0:T(8,128)(2,1)}, u32[]{:S(2)}, u32[]{:S(2)}) collective-permute-start(bf16[128,2048]{1,0:T(8,128)(2,1)} %get-tuple-element.155), channel_id=1, source_target_pairs={{0,3},{1,0},{2,1},{3,2},{4,7},{5,4},{6,5},{7,6},{8,11},{9,8},{10,9... | collective-permute-start | bytes 1572872 | tf_op jit(solution)/shard_map/ppermute | solution.py:46
  571.4 121.1 %collective-permute-start.3 = (bf16[128,2048]{1,0:T(8,128)(2,1)}, bf16[128,2048]{1,0:T(8,128)(2,1)}, u32[]{:S(2)}, u32[]{:S(2)}) collective-permute-start(bf16[128,2048]{1,0:T(8,128)(2,1)} %get-tuple-element.156), channel_id=1, source_target_pairs={{0,2},{1,3},{2,0},{3,1},{4,6},{5,7},{6,4},{7,5},{8,10},{9,11},{10,... | collective-permute-start | bytes 1572872 | tf_op jit(solution)/shard_map/ppermute | solution.py:46
  573.1 119.5 %collective-permute-start.2 = (bf16[128,2048]{1,0:T(8,128)(2,1)}, bf16[128,2048]{1,0:T(8,128)(2,1)}, u32[]{:S(2)}, u32[]{:S(2)}) collective-permute-start(bf16[128,2048]{1,0:T(8,128)(2,1)} %get-tuple-element.154), channel_id=1, source_target_pairs={{0,1},{1,2},{2,3},{3,0},{4,5},{5,6},{6,7},{7,4},{8,9},{9,10},{10,1... | collective-permute-start | bytes 1572872 | tf_op jit(solution)/shard_map/ppermute | solution.py:46
  576.7 45.2 %copy-start.22 = (f32[1,2048]{1,0:T(1,128)S(1)}, f32[1,2048]{1,0:T(1,128)}, u32[]{:S(2)}) copy-start(f32[1,2048]{1,0:T(1,128)} %get-tuple-element.107) | copy-start | bytes 24580
  576.7 45.3 %copy-start.23 = (f32[1,2048]{1,0:T(1,128)S(1)}, f32[1,2048]{1,0:T(1,128)}, u32[]{:S(2)}) copy-start(f32[1,2048]{1,0:T(1,128)} %get-tuple-element.108) | copy-start | bytes 24580
  576.7 115.8 %copy-start.6 = (f32[128,2048]{1,0:T(8,128)S(1)}, f32[128,2048]{1,0:T(8,128)}, u32[]{:S(2)}) copy-start(f32[128,2048]{1,0:T(8,128)} %get-tuple-element.96.mid) | copy-start | bytes 3145732
  688.5 17.8 %collective-permute-start.6 = (f32[128,2048]{1,0:T(8,128)}, f32[128,2048]{1,0:T(8,128)S(1)}, u32[]{:S(2)}, u32[]{:S(2)}) collective-permute-start(f32[128,2048]{1,0:T(8,128)} %get-tuple-element.104), channel_id=1, source_target_pairs={{0,0},{1,1},{2,2},{3,3},{4,8},{5,9},{6,10},{7,11},{8,4},{9,5},{10,... | collective-permute-start | bytes 3145736 | tf_op jit(solution)/shard_map/ppermute | solution.py:46
  694.3 17.7 %collective-permute-start.5 = (bf16[128,2048]{1,0:T(8,128)(2,1)S(1)}, bf16[128,2048]{1,0:T(8,128)(2,1)S(1)}, u32[]{:S(2)}, u32[]{:S(2)}) collective-permute-start(bf16[128,2048]{1,0:T(8,128)(2,1)S(1)} %fusion.59), channel_id=1, source_target_pairs={{0,0},{1,1},{2,2},{3,3},{4,8},{5,9},{6,10},{7,11},{8,4},{9,5},{10,... | collective-permute-start | bytes 1572872 | tf_op jit(solution)/shard_map/ppermute | solution.py:46
  706.3 5.6 copy-start.19
  714.7 3.3 copy-start.1
  751.3 6.8 copy-start.20

commit v2 on v1

v2 whole, which is shorter than its diff:
```python
import functools

import jax
import jax.numpy as jnp
from jax import lax
from jax.experimental import pallas as pl
from jax.experimental.pallas import tpu as pltpu
from jax.sharding import PartitionSpec as P

HEAD_DIM = 64
ROT = 16
SIDE = 4
BLOCK = 128
AXES = ("dp", "tensor")
MESH = pl.DeviceIdType.MESH
VMEM_LIMIT = 50 * 2**20


def here():
    dp, tensor = lax.axis_index("dp"), lax.axis_index("tensor")
    x, z_hi = lax.rem(tensor, SIDE), lax.div(tensor, SIDE)
    y, z_lo, core = lax.div(dp, SIDE), lax.rem(lax.div(dp, 2), 2), lax.rem(dp, 2)
    return x, y, z_hi, z_lo, core


def device(x, y, z_hi, z_lo, core):
    return ((y * 2 + z_lo) * 2 + core, z_hi * SIDE + x)


def turned(value, by):
    return lax.rem(value + by, SIDE)


def pairs(move):
    found = []
    for dp in range(16):
        for tensor in range(8):
            goal = move(tensor % 4, dp // 4, tensor // 4, (dp // 2) % 2, dp % 2)
            if goal is not None:
                to_dp, to_tensor = device(*goal)
                found.append((dp * 8 + tensor, to_dp * 8 + to_tensor))
    return found


def permute(array, move):
    return lax.ppermute(array, AXES, pairs(move))


def swap_rows(x, y, z_hi, z_lo, core):
    return (x, y, core, z_lo, z_hi)


def remote(source, target, sends, arrives, index, device_id):
    return pltpu.make_async_remote_copy(
        src_ref=source,
        dst_ref=target,
        send_sem=sends.at[index],
        recv_sem=arrives.at[index],
        device_id=device_id,
        device_id_type=MESH,
    )


def greet(peers):
    barrier = pltpu.get_barrier_semaphore()
    for peer in peers:
        pl.semaphore_signal(barrier, inc=1, device_id=peer, device_id_type=MESH)
    pl.semaphore_wait(barrier, len(peers))


def line_peers(place):
    x, y, z_hi, z_lo, core = place
    found = [device(turned(x, k), y, z_hi, z_lo, core) for k in (1, 2, 3)]
    return found + [device(x, y, z_hi, z_lo, 1 - core)]


def row_block(full, core, x):
    return full.at[pl.ds(pl.multiple_of((core * SIDE + x) * BLOCK, BLOCK), BLOCK)]


class ByRow:
    def __init__(self, full, place):
        self.full, self.x, self.core = full, place[0], place[4]

    def at(self, step, other):
        core = 1 - self.core if other else self.core
        return row_block(self.full, core, turned(self.x, SIDE - step))

    def landing(self, step, other, by, across):
        return self.at(step, other)


class ByStep:
    def __init__(self, full):
        self.full = full

    def at(self, step, other):
        return self.full.at[pl.ds((step * 2 + other) * BLOCK, BLOCK)]

    def landing(self, step, other, by, across):
        return self.at((step + by) % SIDE, 1 - other if across else other)


class Gather:
    scratch = (
        pltpu.SemaphoreType.DMA((4,)),
        pltpu.SemaphoreType.DMA((4,)),
        pltpu.SemaphoreType.DMA((4,)),
        pltpu.SemaphoreType.DMA((4,)),
    )

    def __init__(self, block, layout, place, sems):
        x, y, z_hi, z_lo, core = place
        x_send, x_arrive, core_send, core_arrive = sems
        half = BLOCK // 2
        right = device(turned(x, 1), y, z_hi, z_lo, core)
        left = device(turned(x, 3), y, z_hi, z_lo, core)
        partner = device(x, y, z_hi, z_lo, 1 - core)

        def passed(step, first, by, index, to):
            part = pl.ds(first, half)
            return remote(
                layout.at(step, 0).at[part],
                layout.landing(step, 0, by, False).at[part],
                x_send,
                x_arrive,
                index,
                to,
            )

        self.right = remote(block, layout.landing(0, 0, 1, False), x_send, x_arrive, 0, right)
        self.left = remote(block, layout.landing(0, 0, 3, False), x_send, x_arrive, 1, left)
        self.right_on = passed(1, 0, 1, 2, right)
        self.left_on = passed(3, half, 3, 3, left)
        self.across = [
            remote(
                block if step == 0 else layout.at(step, 0),
                layout.landing(step, 0, 0, True),
                core_send,
                core_arrive,
                step,
                partner,
            )
            for step in range(SIDE)
        ]

    def start(self):
        self.right.start()
        self.left.start()
        self.across[0].start()

    def arrive(self, step):
        if step == 1:
            self.right.wait_recv()
            self.right_on.start()
        elif step == 3:
            self.left.wait_recv()
            self.left_on.start()
        else:
            self.right_on.wait_recv()
            self.left_on.wait_recv()
        self.across[step].start()

    def finish(self):
        for copy in (self.right, self.left, self.right_on, self.left_on, *self.across):
            copy.wait_send()

    def take(self):
        for copy in self.across:
            copy.wait_recv()


class Scatter:
    buffers = (
        pltpu.VMEM((SIDE, BLOCK, 2048), jnp.bfloat16),
        pltpu.VMEM((3, BLOCK, 2048), jnp.bfloat16),
        pltpu.VMEM((3, BLOCK, 2048), jnp.bfloat16),
    )
    sems = (
        pltpu.SemaphoreType.DMA((SIDE,)),
        pltpu.SemaphoreType.DMA((SIDE,)),
        pltpu.SemaphoreType.DMA((3,)),
        pltpu.SemaphoreType.DMA((3,)),
    )
    scratch = buffers + sems

    def __init__(self, own, given, place, scratch):
        x, y, z_hi, z_lo, core = place
        self.own, (self.other, self.leaving, self.arrived) = own, scratch[:3]
        core_send, core_arrive, x_send, x_arrive = scratch[3:]
        partner = device(x, y, z_hi, z_lo, 1 - core)
        self.across = [
            remote(given(step), self.other.at[step], core_send, core_arrive, step, partner)
            for step in range(SIDE)
        ]
        self.along = [
            remote(
                self.leaving.at[step - 1],
                self.arrived.at[step - 1],
                x_send,
                x_arrive,
                step - 1,
                device(turned(x, SIDE - step), y, z_hi, z_lo, core),
            )
            for step in (1, 2, 3)
        ]

    def merge(self, step):
        self.across[step].wait_recv()

        def add(rows):
            both = self.own(step, rows).astype(jnp.float32) + self.other[step, rows, :].astype(jnp.float32)
            self.leaving[step - 1, rows, :] = both.astype(jnp.bfloat16)

        tile_rows(add)
        self.along[step - 1].start()

    def finish(self):
        self.across[0].wait_recv()
        for copy in self.along:
            copy.wait()
        for copy in self.across:
            copy.wait_send()

    def rows(self, rows):
        total = self.own(0, rows).astype(jnp.float32) + self.other[0, rows, :].astype(jnp.float32)
        for step in range(3):
            total = total + self.arrived[step, rows, :].astype(jnp.float32)
        return total


class Loaded:
    def __init__(self, full, held, place, sems):
        there, here_ = ByRow(full, place), ByStep(held)
        self.copies = [
            pltpu.make_async_copy(there.at(step, other), here_.at(step, other), sems.at[step * 2 + other])
            for step in range(SIDE)
            for other in range(2)
        ]

    def start(self):
        for copy in self.copies:
            copy.start()

    def wait(self):
        for copy in self.copies:
            copy.wait()


class Fetch:
    def __init__(self, weight, filled, cut, place, sems, index):
        x, y, z_hi, z_lo, core = place
        send, arrive, own_sem = sems
        self.own = pltpu.make_async_copy(weight, filled, own_sem.at[index])
        across = device(x, y, 1 - z_hi, 1 - z_lo, z_hi)
        up = device(x, turned(y, 1), z_hi, z_lo, core)
        down = device(x, turned(y, 3), z_hi, z_lo, core)
        base = index * 5

        def moved(ref, quarter, half, slot, to):
            source = cut(ref, quarter, half)
            return remote(source, cut(filled, quarter, half), send, arrive, base + slot, to)

        self.across = moved(weight, y, None, 0, across)
        self.up = moved(filled, y, None, 1, up)
        self.down = moved(filled, y, None, 2, down)
        self.up_on = moved(filled, turned(y, 3), 0, 3, up)
        self.down_on = moved(filled, turned(y, 1), 1, 4, down)

    def spread(self):
        self.across.wait_recv()
        self.up.start()
        self.down.start()

    def pass_on(self):
        self.up.wait_recv()
        self.up_on.start()
        self.down.wait_recv()
        self.down_on.start()

    def finish(self):
        self.up_on.wait_recv()
        self.down_on.wait_recv()
        for copy in (self.across, self.up, self.down, self.up_on, self.down_on):
            copy.wait_send()


def fetch_scratch(count):
    return (
        pltpu.SemaphoreType.DMA((5 * count,)),
        pltpu.SemaphoreType.DMA((5 * count,)),
        pltpu.SemaphoreType.DMA((count,)),
    )


def fetch_peers(place):
    x, y, z_hi, z_lo, core = place
    return [device(x, y, 1 - z_hi, 1 - z_lo, z_hi)] + [
        device(x, turned(y, k), z_hi, z_lo, core) for k in (1, 3)
    ]


def quarter_rows(size, *before):
    quarter_size = size // SIDE
    split = -(-quarter_size // 32) * 16

    def cut(weight, quarter, half):
        first = pl.multiple_of(quarter * quarter_size, 16)
        if half is None:
            rows = pl.ds(first, quarter_size)
        elif half == 0:
            rows = pl.ds(first, split)
        else:
            rows = pl.ds(first + split, quarter_size - split)
        return weight.at[(*before, rows)]

    return cut


QKV_CUT = quarter_rows(2048, slice(None))
OUT_CUT = quarter_rows(256)
FF_CUT = quarter_rows(704)


def moments(values):
    centre = values - jnp.mean(values, axis=-1, keepdims=True)
    return centre, lax.rsqrt(jnp.mean(centre * centre, axis=-1, keepdims=True) + 1e-05)


def tile_rows(body):
    @pl.loop(0, BLOCK, step=16)
    def _(row):
        body(pl.ds(pl.multiple_of(row, 16), 16))


def first_kernel(
    tokens,
    out_grad,
    live,
    gain,
    shift,
    qkv,
    out,
    down,
    tokens_here,
    cot_here,
    normed_full,
    cot_full,
    qkv_here,
    out_here,
    down_here,
    tok_buf,
    grad_buf,
    norm_buf,
    cot_buf,
    swap_send,
    swap_arrive,
    own_sems,
    *sems,
):
    place = here()
    x, y, z_hi, z_lo, core = place
    lacking = core != z_hi
    swap_with = device(x, y, core, z_lo, z_hi)
    fetch_sems = sems[8:]
    fetches = [
        Fetch(weight, filled, cut, place, fetch_sems, index)
        for index, (weight, filled, cut) in enumerate(
            [(qkv, qkv_here, QKV_CUT), (out, out_here, OUT_CUT), (down, down_here, FF_CUT)]
        )
    ]
    swaps = [
        remote(source, target, swap_send, swap_arrive, index, swap_with)
        for index, (source, target) in enumerate([(tokens, tok_buf), (out_grad, grad_buf)])
    ]
    stays = [
        pltpu.make_async_copy(source, target, own_sems.at[index])
        for index, (source, target) in enumerate([(tokens, tok_buf), (out_grad, grad_buf)])
    ]

    @pl.when(lacking)
    def _():
        greet(line_peers(place) + [swap_with] + fetch_peers(place))
        swaps[0].start()
        swaps[0].wait_recv()
        fetches[0].across.start()
        swaps[1].start()
        fetches[1].across.start()
        fetches[2].across.start()

    @pl.when(jnp.logical_not(lacking))
    def _():
        greet(line_peers(place))
        for copy in stays:
            copy.start()
        for fetch in fetches:
            fetch.own.start()
        stays[0].wait()

    def norm(rows):
        centre, scale = moments(tok_buf[rows, :].astype(jnp.float32))
        norm_buf[rows, :] = (centre * scale * gain[...] + shift[...]).astype(jnp.bfloat16)

    tile_rows(norm)
    gather = Gather(norm_buf, ByRow(normed_full, place), place, sems[:4])
    gather_cot = Gather(cot_buf, ByRow(cot_full, place), place, sems[4:8])
    stored = [
        pltpu.make_async_copy(source, target, own_sems.at[2 + index])
        for index, (source, target) in enumerate(
            [
                (norm_buf, row_block(normed_full, core, x)),
                (tok_buf, tokens_here),
                (cot_buf, cot_here),
                (cot_buf, row_block(cot_full, core, x)),
            ]
        )
    ]
    gather.start()
    stored[0].start()
    stored[1].start()

    @pl.when(lacking)
    def _():
        fetches[0].spread()
        swaps[0].wait_send()
        swaps[1].wait()

    @pl.when(jnp.logical_not(lacking))
    def _():
        stays[1].wait()

    def mask(rows):
        cot_buf[rows, :] = (grad_buf[rows, :].astype(jnp.float32) * live[rows, :]).astype(jnp.bfloat16)

    tile_rows(mask)
    gather_cot.start()
    stored[2].start()
    stored[3].start()
    gather.arrive(1)
    gather.arrive(3)

    @pl.when(lacking)
    def _():
        fetches[1].spread()
        fetches[2].spread()
        fetches[0].pass_on()

    gather.arrive(2)
    gather_cot.arrive(1)
    gather_cot.arrive(3)

    @pl.when(lacking)
    def _():
        fetches[1].pass_on()
        fetches[2].pass_on()

    gather_cot.arrive(2)
    for each in (gather, gather_cot):
        each.take()
        each.finish()
    for copy in stored:
        copy.wait()

    @pl.when(lacking)
    def _():
        for fetch in fetches:
            fetch.finish()

    @pl.when(jnp.logical_not(lacking))
    def _():
        for fetch in fetches:
            fetch.own.wait()


def matmul(left, right, contract):
    return lax.dot_general(left, right, ((contract, ((), ()))), preferred_element_type=jnp.float32)


NN, NT, TN = ((1,), (0,)), ((1,), (1,)), ((0,), (0,))
PAIR = 2 * BLOCK


def middle_kernel(
    part,
    tokens,
    gain,
    shift,
    gate_up_own,
    down_held,
    cot_full,
    attended_full,
    out_held,
    cot,
    mid,
    d_mid,
    gain_part,
    shift_part,
    grads,
    ffn_part,
    d_attended,
    out_grad,
    gate_up,
    down,
    out,
    normed,
    cot_rows,
    d_rows,
    attended,
    hidden,
    d_gate,
    d_up,
    d_hidden,
    own_rows,
    given_terms,
    ffn_tile,
    grad_tile,
    load_sems,
    att_sems,
    own_sems,
    ffn_sem,
    grad_sems,
    *scratch,
):
    bf16 = jnp.bfloat16
    place = here()
    x, y, z_hi, z_lo, core = place
    lacking = core != z_hi
    attn = ByRow(part, place)
    first = Scatter(
        lambda step, rows: own_rows[step, rows, :], lambda step: attn.at(step, 1), place, scratch[:7]
    )
    second = Scatter(
        lambda step, rows: own_rows[step, rows, :],
        lambda step: given_terms.at[step],
        place,
        scratch[:3] + scratch[7:11],
    )
    gather = Gather(normed.at[pl.ds(0, BLOCK)], ByStep(normed), place, scratch[11:15])
    gather_d = Gather(d_rows.at[pl.ds(0, BLOCK)], ByStep(d_rows), place, scratch[15:19])
    fetches = [
        Fetch(gate_up_own.at[index], gate_up.at[index], FF_CUT, place, scratch[19:], index) for index in range(2)
    ]
    load_cot = Loaded(cot_full, cot_rows, place, load_sems)
    load_att = Loaded(attended_full, attended, place, att_sems)
    load_own = [
        pltpu.make_async_copy(attn.at(step, 0), own_rows.at[step], own_sems.at[step]) for step in range(SIDE)
    ]
    load_down = pltpu.make_async_copy(down_held, down, own_sems.at[4])
    load_out = pltpu.make_async_copy(out_held, out, own_sems.at[5])

    for copy in load_own:
        copy.start()
    load_down.start()
    load_cot.start()
    load_att.start()
    load_out.start()

    @pl.when(lacking)
    def _():
        greet(line_peers(place) + fetch_peers(place))

    @pl.when(jnp.logical_not(lacking))
    def _():
        greet(line_peers(place))

    for step in (2, 1, 3, 0):
        first.across[step].start()

    @pl.when(lacking)
    def _():
        for fetch in fetches:
            fetch.across.start()

    @pl.when(jnp.logical_not(lacking))
    def _():
        for fetch in fetches:
            fetch.own.start()

    for copy in load_own:
        copy.wait()
    for step in (2, 1, 3):
        first.merge(step)
    load_down.wait()
    load_cot.wait()

    @pl.loop(0, 2)
    def _(index):
        rows = pl.ds(pl.multiple_of(index * PAIR, PAIR), PAIR)
        d_hidden[rows, :] = matmul(cot_rows[rows, :], down[...], NT)

    @pl.when(lacking)
    def _():
        for fetch in fetches:
            fetch.spread()

    @pl.loop(2, 4)
    def _(index):
        rows = pl.ds(pl.multiple_of(index * PAIR, PAIR), PAIR)
        d_hidden[rows, :] = matmul(cot_rows[rows, :], down[...], NT)

    first.finish()

    def norm(rows):
        stream = tokens[rows, :].astype(jnp.float32) + first.rows(rows)
        mid[rows, :] = stream
        centre, scale = moments(stream)
        normed[rows, :] = (centre * scale * gain[...] + shift[...]).astype(bf16)

    tile_rows(norm)
    gather.start()

    @pl.when(lacking)
    def _():
        for fetch in fetches:
            fetch.pass_on()
        for fetch in fetches:
            fetch.finish()

    @pl.when(jnp.logical_not(lacking))
    def _():
        for fetch in fetches:
            fetch.own.wait()

    order = (0, 1, 3, 2)

    @pl.loop(0, 4)
    def _(turn):
        step = turn + lax.div(turn, 2) * (5 - 2 * turn)
        for index in range(4):

            @pl.when(turn == index)
            def _(index=index):
                for arrived in ((), (1, 3), (), (2,))[index]:
                    gather.arrive(arrived)
                gather.across[order[index]].wait_recv()

        rows = pl.ds(pl.multiple_of(step * PAIR, PAIR), PAIR)
        gate = matmul(normed[rows, :], gate_up[0], NT)
        up = matmul(normed[rows, :], gate_up[1], NT)
        sigmoid = jax.nn.sigmoid(gate)
        silu = gate * sigmoid
        hidden[rows, :] = (silu * up).astype(bf16)
        d_hid = d_hidden[rows, :]
        d_gate[rows, :] = (d_hid * up * sigmoid * (1.0 + gate * (1.0 - sigmoid))).astype(bf16)
        d_up[rows, :] = (d_hid * silu).astype(bf16)
        for index in (2, 3):

            @pl.when(turn == index)
            def _(index=index):
                second.merge(order[index - 1])

        @pl.loop(0, 2048, step=512)
        def _(column):
            columns = pl.ds(pl.multiple_of(column, 512), 512)
            terms = matmul(d_gate[rows, :], gate_up[0, :, columns], NN) + matmul(
                d_up[rows, :], gate_up[1, :, columns], NN
            )
            terms = terms.astype(bf16)
            own_rows[step, :, columns] = terms[:BLOCK]
            given_terms[step, :, columns] = terms[BLOCK:]

        for index in range(4):

            @pl.when(turn == index)
            def _(index=index):
                second.across[order[index]].start()

    second.merge(2)
    load_att.wait()
    load_out.wait()

    @pl.loop(0, 4)
    def _(index):
        rows = pl.ds(pl.multiple_of(index * PAIR, PAIR), PAIR)

        @pl.when(index > 0)
        def _():
            pltpu.make_async_copy(ffn_tile, ffn_part.at[rows], ffn_sem).wait()

        @pl.loop(0, 2048, step=512)
        def _(column):
            columns = pl.ds(pl.multiple_of(column, 512), 512)
            ffn_tile[:, columns] = matmul(hidden[rows, :], down[:, columns], NN).astype(bf16)

        pltpu.make_async_copy(ffn_tile, ffn_part.at[rows], ffn_sem).start()

    def weight_grad(index, left, right):
        @pl.loop(0, 4)
        def _(tile):
            columns = pl.ds(pl.multiple_of(tile * 512, 512), 512)
            target = grads.at[index, :, columns]
            slot = lax.rem(tile, 2)
            copy = pltpu.make_async_copy(grad_tile.at[slot], target, grad_sems.at[slot])

            @pl.when(jnp.logical_or(index > 0, tile > 1))
            def _():
                copy.wait()

            grad_tile[slot] = matmul(left[...], right[:, columns], TN).astype(bf16)
            copy.start()

    weight_grad(0, d_gate, normed)
    second.finish()
    gain_part[...] = jnp.zeros_like(gain_part)
    shift_part[...] = jnp.zeros_like(shift_part)

    def back(rows):
        grad = second.rows(rows)
        centre, scale = moments(mid[rows, :])
        unit = centre * scale
        gain_part[...] += jnp.sum(grad * unit, axis=0, keepdims=True)
        shift_part[...] += jnp.sum(grad, axis=0, keepdims=True)
        scaled = grad * gain[...]
        total = cot[rows, :].astype(jnp.float32) + scale * (
            scaled
            - jnp.mean(scaled, axis=-1, keepdims=True)
            - unit * jnp.mean(scaled * unit, axis=-1, keepdims=True)
        )
        d_mid[rows, :] = total
        d_rows[rows, :] = total.astype(bf16)

    tile_rows(back)
    gather_d.start()
    weight_grad(1, d_up, normed)
    gather_d.arrive(1)
    gather_d.arrive(3)
    weight_grad(2, hidden, cot_rows)
    gather_d.arrive(2)
    for step in range(SIDE):
        gather_d.across[step].wait_recv()
        terms = matmul(d_rows[pl.ds(step * PAIR, PAIR), :], out[...], NT).astype(bf16)
        behind = turned(x, SIDE - step)
        for other in range(2):
            whose = (1 - core) if other else core
            first_row = pl.multiple_of((whose * SIDE + behind) * BLOCK, BLOCK)
            d_attended[pl.ds(first_row, BLOCK), :] = terms[other * BLOCK : (other + 1) * BLOCK]

    @pl.loop(0, 2048, step=512)
    def _(column):
        columns = pl.ds(pl.multiple_of(column, 512), 512)
        out_grad[:, columns] = matmul(attended[...], d_rows[:, columns], TN).astype(bf16)

    gather.finish()
    gather_d.finish()
    pltpu.make_async_copy(ffn_tile, ffn_part.at[pl.ds(0, PAIR)], ffn_sem).wait()
    for slot in range(2):
        pltpu.make_async_copy(grad_tile.at[slot], grads.at[0, :, pl.ds(0, 512)], grad_sems.at[slot]).wait()


class Links:
    def __init__(self, sends, arrives):
        self.sends, self.arrives, self.used = sends, arrives, 0

    def to(self, source, target, device_id):
        self.used += 1
        return remote(source, target, self.sends, self.arrives, self.used - 1, device_id)


class Locals:
    def __init__(self, sems):
        self.sems, self.used = sems, 0

    def of(self, source, target):
        self.used += 1
        return pltpu.make_async_copy(source, target, self.sems.at[self.used - 1])


def each_rows(count, step, body):
    if count == step:
        body(pl.ds(0, count))
        return

    @pl.loop(0, count, step=step)
    def _(row):
        body(pl.ds(pl.multiple_of(row, 16), step))


def add_into(target, *terms, count, step):
    def body(rows):
        total = terms[0](rows).astype(jnp.float32)
        for term in terms[1:]:
            total = total + term(rows).astype(jnp.float32)
        target[rows, :] = total.astype(jnp.bfloat16)

    each_rows(count, step, body)


def of(ref, first=0):
    return lambda rows: ref[pl.ds(rows.start + first, rows.size), :]


class Around:
    def __init__(self, place):
        x, y, z_hi, z_lo, core = place
        self.y, self.z_lo = y, z_lo
        self.up = device(x, turned(y, 1), z_hi, z_lo, core)
        self.down = device(x, turned(y, 3), z_hi, z_lo, core)
        self.beyond = device(x, y, 1 - z_hi, 1 - z_lo, core)
        self.twin = device(x, y, z_hi, 1 - z_lo, core)
        self.partner = device(x, y, z_hi, z_lo, 1 - core)
        self.keeps = core == z_hi
        self.gives = jnp.logical_not(self.keeps)


class RowRing:
    def __init__(self, size, width, step):
        self.size, self.width, self.step = size, width, step
        self.split = -(-size // 32) * 16

    def scratch(self):
        kind = jnp.bfloat16
        return (
            pltpu.VMEM((self.split, self.width), kind),
            pltpu.VMEM((self.size - self.split, self.width), kind),
            pltpu.VMEM((self.size, self.width), kind),
            pltpu.VMEM((self.size, self.width), kind),
            pltpu.VMEM((self.size, self.width), kind),
        )

    def quarter(self, ref, index, first=0):
        return ref.at[pl.ds(pl.multiple_of(first + index * self.size, 16), self.size)]

    def halves(self, ref):
        return ref.at[pl.ds(0, self.split)], ref.at[pl.ds(self.split, self.size - self.split)]

    def bind(self, links, around, scratch, far, up_terms, down_terms, own_terms):
        self.from_below, self.from_above, self.got_up, self.got_down, self.total = scratch
        self.up_terms, self.down_terms, self.own_terms = up_terms, down_terms, own_terms
        first, second = self.halves(far)
        self.first = (
            links.to(first, self.from_below, around.up),
            links.to(second, self.from_above, around.down),
        )
        self.second = (
            links.to(up_terms, self.got_up, around.up),
            links.to(down_terms, self.got_down, around.down),
        )

    def begin(self):
        for copy in self.first:
            copy.start()

    def merge(self):
        self.first[0].wait_recv()
        low, high = self.split, self.size - self.split
        up_low, _ = self.halves(self.up_terms)
        _, down_high = self.halves(self.down_terms)
        add_into(up_low, of(up_low), of(self.from_below), count=low, step=low)
        self.second[0].start()
        self.first[1].wait_recv()
        add_into(down_high, of(down_high), of(self.from_above), count=high, step=high)
        self.second[1].start()

    def sum(self):
        for copy in self.second:
            copy.wait_recv()
        add_into(
            self.total,
            of(self.own_terms),
            of(self.got_up),
            of(self.got_down),
            count=self.size,
            step=self.step,
        )

    def sent(self):
        for copy in (*self.first, *self.second):
            copy.wait_send()


class RowSpread:
    def __init__(self, ring, links, locals_, around, total, full, first=0):
        y = around.y
        mine = ring.quarter(full, y, first)
        below, above = ring.quarter(full, turned(y, 3), first), ring.quarter(full, turned(y, 1), first)
        self.own = locals_.of(total, mine)
        self.direct = (links.to(total, mine, around.up), links.to(total, mine, around.down))
        low, high = ring.halves(below)[0], ring.halves(above)[1]
        self.passed = (links.to(low, low, around.up), links.to(high, high, around.down))

    def begin(self):
        self.own.start()
        for copy in self.direct:
            copy.start()

    def pass_on(self):
        for copy, onward in zip(self.direct, self.passed):
            copy.wait_recv()
            onward.start()

    def end(self):
        self.own.wait()
        for copy in self.passed:
            copy.wait_recv()

    def sent(self):
        for copy in (*self.direct, *self.passed):
            copy.wait_send()


WIDE = 512
FF_RING = (528, 256, 176)
ATTN_UNITS = (((768, 256, 96), 0), ((768, 256, 96), 3072), ((64, 2048, 16), 0))
FF_STEPS, ATTN_STEPS = 9, 8
FF_LINKS, ATTN_LINKS = 12, 11


def ff_scratch(rows):
    kind = jnp.bfloat16
    return (
        pltpu.VMEM((rows, WIDE), kind),
        pltpu.VMEM((rows, WIDE // 2), kind),
    ) + RowRing(*FF_RING).scratch()


def attn_scratch(unit):
    ring = RowRing(*unit[0])
    held = pltpu.VMEM((ring.size, ring.width), jnp.bfloat16)
    return (held,) * 5 + ring.scratch()


def ff_sum(part, full, column, links, locals_, around, mine, scratch):
    got, half = scratch[:2]
    rows = got.shape[0]
    width = WIDE // 2
    ring = RowRing(*FF_RING)
    stretch = lambda ref: ref.at[:, pl.ds(column, WIDE)]
    side = lambda z_lo: pl.ds(pl.multiple_of(z_lo * width, 128), width)
    placed = lambda z_lo: full.at[:, pl.ds(pl.multiple_of(column + z_lo * width, 128), width)]
    load = locals_.of(stretch(part), mine)
    over = links.to(stretch(part), got, around.beyond)
    kept, sent_on = side(around.z_lo), side(1 - around.z_lo)
    twin = links.to(got.at[:, sent_on], half, around.twin)
    y = around.y
    quarter = lambda k: ring.quarter(half, turned(y, k))
    ring.bind(links, around, scratch[2:], quarter(2), quarter(1), quarter(3), quarter(0))
    own_side = placed(around.z_lo)
    spread = RowSpread(ring, links, locals_, around, ring.total, own_side)
    both = links.to(own_side, own_side, around.twin)
    core = links.to(stretch(full), stretch(full), around.partner)

    @pl.when(around.gives)
    def _():
        over.start()

    @pl.when(around.keeps)
    def _():
        load.start()

    yield

    @pl.when(around.keeps)
    def _():
        load.wait()
        over.wait_recv()
        add_into(got, of(got), of(mine), count=rows, step=96)
        twin.start()

    yield

    @pl.when(around.keeps)
    def _():
        twin.wait_recv()
        add_into(half, of(half), lambda rows: got[rows, kept], count=rows, step=96)
        ring.begin()

    yield

    @pl.when(around.keeps)
    def _():
        ring.merge()

    yield

    @pl.when(around.keeps)
    def _():
        ring.sum()
        spread.begin()

    yield

    @pl.when(around.keeps)
    def _():
        spread.pass_on()

    yield

    @pl.when(around.keeps)
    def _():
        spread.end()
        both.start()

    yield

    @pl.when(around.keeps)
    def _():
        both.wait_recv()
        core.start()

    yield

    @pl.when(around.keeps)
    def _():
        twin.wait_send()
        ring.sent()
        spread.sent()
        both.wait_send()
        core.wait_send()

    @pl.when(around.gives)
    def _():
        over.wait_send()
        core.wait_recv()

    yield


def attn_sum(part, full, unit, links, locals_, around, scratch):
    own_terms, up_terms, down_terms, from_beyond, from_twin = scratch[:5]
    sizes, first = unit
    ring = RowRing(*sizes)
    y = around.y
    quarter = lambda k: ring.quarter(part, turned(y, k), first)
    loads = [
        locals_.of(quarter(k), held) for k, held in ((1, up_terms), (3, down_terms), (0, own_terms))
    ]
    ring.bind(links, around, scratch[5:], quarter(2), up_terms, down_terms, own_terms)
    total = ring.total
    over = links.to(total, from_beyond, around.beyond)
    twin = links.to(total, from_twin, around.twin)
    spread = RowSpread(ring, links, locals_, around, own_terms, full, first)
    span = full.at[pl.ds(first, SIDE * ring.size)]
    core = links.to(span, span, around.partner)

    for copy in loads:
        copy.start()
    ring.begin()
    yield
    for copy in loads:
        copy.wait()
    ring.merge()
    yield
    ring.sum()

    @pl.when(around.gives)
    def _():
        over.start()

    yield

    @pl.when(around.keeps)
    def _():
        over.wait_recv()
        add_into(total, of(total), of(from_beyond), count=ring.size, step=ring.step)
        twin.start()

    yield

    @pl.when(around.keeps)
    def _():
        twin.wait_recv()
        add_into(own_terms, of(total), of(from_twin), count=ring.size, step=ring.step)
        spread.begin()

    yield

    @pl.when(around.keeps)
    def _():
        spread.pass_on()

    yield

    @pl.when(around.keeps)
    def _():
        spread.end()
        core.start()

    yield
    ring.sent()

    @pl.when(around.keeps)
    def _():
        twin.wait_send()
        spread.sent()
        core.wait_send()

    @pl.when(around.gives)
    def _():
        over.wait_send()
        core.wait_recv()

    yield


def sum_everywhere(values, places, links, place):
    x, y, z_hi, z_lo, core = place
    by_x, by_core, by_y, by_z = places
    z = z_hi * 2 + z_lo
    rounds = (
        (by_x, x, [device(turned(x, k), y, z_hi, z_lo, core) for k in (1, 2, 3)]),
        (by_core, core, [device(x, y, z_hi, z_lo, 1 - core)]),
        (by_y, y, [device(x, turned(y, k), z_hi, z_lo, core) for k in (1, 2, 3)]),
        (by_z, z, [z_device(x, y, turned(z, k), core) for k in (1, 2, 3)]),
    )
    for slots, mine, peers in rounds:
        slots[mine] = values[...]
        copies = [links.to(slots.at[mine], slots.at[mine], peer) for peer in peers]
        for copy in copies:
            copy.start()
        for copy in copies:
            copy.wait()
        total = slots[0]
        for slot in range(1, slots.shape[0]):
            total = total + slots[slot]
        values[...] = total


def z_device(x, y, z, core):
    return device(x, y, lax.div(z, 2), lax.rem(z, 2), core)


def last_kernel(
    part,
    tokens,
    d_mid,
    gain,
    ffn_part,
    mid,
    ff_part,
    qkv_part,
    out_part,
    norm_part,
    mixed,
    input_grad,
    ff_full,
    qkv_full,
    out_full,
    sums,
    d_in,
    mixed_rows,
    own_rows,
    ffn_rows,
    own_sems,
    sends,
    arrives,
    local_sems,
    by_x,
    by_core,
    by_y,
    by_z,
    *scratch,
):
    place = here()
    x, y, z_hi, z_lo, core = place
    z = z_hi * 2 + z_lo
    around = Around(place)
    links, locals_ = Links(sends, arrives), Locals(local_sems)
    swap_with = device(x, y, core, z_lo, z_hi)
    terms, ffn_terms = ByRow(part, place), ByStep(ffn_part)
    scatter = Scatter(
        lambda step, rows: own_rows[step, rows, :], lambda step: terms.at(step, 1), place, scratch[:7]
    )
    scatter_ffn = Scatter(
        lambda step, rows: ffn_rows[step, rows, :], lambda step: ffn_terms.at(step, 1), place, scratch[7:14]
    )
    scratch = scratch[14:]
    ff_units, attn_units = [], []
    ff_own, scratch = scratch[:2], scratch[2:]
    for index in range(2048 // WIDE):
        mine = ff_own[index % 2]
        ff_units.append(ff_sum(ff_part, ff_full, index * WIDE, links, locals_, around, mine, scratch[:7]))
        scratch = scratch[7:]
    for index, unit in enumerate(ATTN_UNITS):
        refs = (out_part, out_full) if index == 2 else (qkv_part, qkv_full)
        attn_units.append(attn_sum(*refs, unit, links, locals_, around, scratch[:10]))
        scratch = scratch[10:]
    load_own = [locals_.of(terms.at(step, 0), own_rows.at[step]) for step in range(SIDE)]
    load_ffn = [locals_.of(ffn_terms.at(step, 0), ffn_rows.at[step]) for step in range(SIDE)]
    swaps = [links.to(mixed_rows, mixed, swap_with), links.to(d_in, input_grad, swap_with)]
    stays = [locals_.of(mixed_rows, mixed), locals_.of(d_in, input_grad)]

    def ff(*indices):
        for index in indices:
            next(ff_units[index])

    def attn(*indices):
        for index in indices:
            next(attn_units[index])

    def give(index):
        @pl.when(around.gives)
        def _():
            swaps[index].start()

        @pl.when(around.keeps)
        def _():
            stays[index].start()

    for copy in load_own + load_ffn:
        copy.start()
    peers = line_peers(place) + [device(x, turned(y, k), z_hi, z_lo, core) for k in (1, 2, 3)]
    peers += [z_device(x, y, turned(z, k), core) for k in (1, 2, 3)]

    @pl.when(around.gives)
    def _():
        greet(peers + [swap_with])

    @pl.when(around.keeps)
    def _():
        greet(peers)

    for step in (2, 1, 3, 0):
        scatter.across[step].start()
    ff(0, 1)
    attn(0, 1, 2)
    for copy in load_own + load_ffn:
        copy.wait()
    for step in (2, 1, 3):
        scatter.merge(step)
    for step in (2, 1, 3, 0):
        scatter_ffn.across[step].start()
    attn(0, 1, 2)
    for step in (2, 1, 3):
        scatter_ffn.merge(step)
    ff(0, 2)
    attn(0, 1, 2)
    scatter.finish()
    sums[...] = norm_part[...]

    def back(rows):
        grad = scatter.rows(rows)
        centre, scale = moments(tokens[rows, :].astype(jnp.float32))
        unit = centre * scale
        sums[0:1, :] += jnp.sum(grad * unit, axis=0, keepdims=True)
        sums[1:2, :] += jnp.sum(grad, axis=0, keepdims=True)
        scaled = grad * gain[...]
        d_in[rows, :] = d_mid[rows, :] + scale * (
            scaled
            - jnp.mean(scaled, axis=-1, keepdims=True)
            - unit * jnp.mean(scaled * unit, axis=-1, keepdims=True)
        )

    tile_rows(back)
    give(1)
    ff(0)
    attn(0, 1, 2)
    ff(0, 1, 3)
    attn(0, 1, 2)
    scatter_ffn.finish()

    def mix(rows):
        mixed_rows[rows, :] = (mid[rows, :] + scatter_ffn.rows(rows)).astype(jnp.bfloat16)

    tile_rows(mix)
    give(0)
    ff(0, 1, 0)
    attn(0, 1, 2)
    sum_everywhere(sums, (by_x, by_core, by_y, by_z), links, place)
    ff(1, 2, 0, 1, 2)
    attn(0, 1, 2)
    ff(0, 1, 2, 3, 1, 2, 3, 2, 1, 3, 2, 3, 2, 3, 3, 3)
    attn(0, 1, 2)
    ff(0, 1, 2, 3)

    @pl.when(around.gives)
    def _():
        for copy in swaps:
            copy.wait()

    @pl.when(around.keeps)
    def _():
        for copy in stays:
            copy.wait()


ANY = pl.BlockSpec(memory_space=pl.ANY)
HELD = pl.BlockSpec(memory_space=pltpu.VMEM)


def call(kernel, collective_id, args, in_specs, outs, out_specs, scratch):
    return pl.pallas_call(
        kernel,
        out_shape=[jax.ShapeDtypeStruct(shape, kind) for shape, kind in outs],
        in_specs=in_specs,
        out_specs=out_specs,
        scratch_shapes=list(scratch),
        compiler_params=pltpu.CompilerParams(
            collective_id=collective_id, has_side_effects=True, vmem_limit_bytes=VMEM_LIMIT
        ),
    )(*args)


def member_layout(seq_length, seq_owner, member, row_total):
    entry_total = seq_length.shape[0]
    row_ids = jnp.arange(row_total, dtype=jnp.int32)
    entry_ids = jnp.arange(entry_total, dtype=jnp.int32)
    earlier = (entry_ids[:, None] < entry_ids[None, :]).astype(jnp.int32)
    sharing = (seq_owner[:, None] == seq_owner[None, :]).astype(jnp.int32)
    starts = jnp.sum(seq_length[:, None] * sharing * earlier, axis=0)
    owned_now = (seq_owner == member).astype(jnp.int32)
    inside = (
        owned_now[None, :]
        * (row_ids[:, None] >= starts[None, :]).astype(jnp.int32)
        * (row_ids[:, None] < (starts + seq_length)[None, :]).astype(jnp.int32)
    )
    live_rows = jnp.sum(inside, axis=1)
    segment = jnp.sum(inside * entry_ids[None, :], axis=1) + (1 - live_rows) * (
        entry_total + row_ids
    )
    position = jnp.sum(inside * (row_ids[:, None] - starts[None, :]), axis=1)
    return (segment, position, live_rows)


def rotary_tables(position):
    half_rot = ROT // 2
    frequency = jnp.power(
        jnp.float32(10000.0), -2.0 * jnp.arange(half_rot, dtype=jnp.float32) / ROT
    )
    angles = position.astype(jnp.float32)[:, None] * frequency[None, :]
    return (jnp.cos(angles)[:, None, :], jnp.sin(angles)[:, None, :])


def rotate(values, cosine, sine_table):
    half_rot = ROT // 2
    first_half = values[..., :half_rot]
    second_half = values[..., half_rot:ROT]
    return jnp.concatenate(
        [
            first_half * cosine - second_half * sine_table,
            second_half * cosine + first_half * sine_table,
            values[..., ROT:],
        ],
        axis=-1,
    )


def contract_rows(left_rows, right_rows):
    return lax.dot_general(
        left_rows, right_rows, (((0,), (0,)), ((), ())), preferred_element_type=jnp.float32
    )


def times_transposed(left_rows, right_rows):
    return lax.dot_general(
        left_rows, right_rows, (((1,), (1,)), ((), ())), preferred_element_type=jnp.float32
    )


def block_mask(segment, row_ids, begin_row, end_row):
    return (segment[begin_row:end_row, None] == segment[None, :end_row]) & (
        row_ids[None, :end_row] <= row_ids[begin_row:end_row, None]
    )


def body(
    tokens,
    seq_length,
    seq_owner,
    ln1_gain,
    ln1_bias,
    qkv_weight,
    qkv_bias,
    out_weight,
    ln2_gain,
    ln2_bias,
    gate_up_weight,
    down_weight,
    out_grad,
):
    bf16, f32 = jnp.bfloat16, jnp.float32
    x, y, z_hi, z_lo, core = here()
    row_total = BLOCK * 8
    rows_here, rows_all = (BLOCK, 2048), (row_total, 2048)
    local_heads = qkv_weight.shape[2] // HEAD_DIM
    member = (y * 2 + z_lo) * 2 + z_hi
    shard = core * SIDE + x
    score_scale = HEAD_DIM ** (-0.5)
    segment, position, live_rows = member_layout(seq_length, seq_owner, member, row_total)
    row_ids = jnp.arange(row_total, dtype=jnp.int32)
    live = lax.dynamic_slice_in_dim(live_rows, shard * BLOCK, BLOCK, 0)[:, None].astype(f32)
    bias = permute(qkv_bias, swap_rows)

    dma = pltpu.SemaphoreType.DMA
    tokens_here, cot, normed1, cot_rows, qkv, out, down = call(
        first_kernel,
        1,
        (tokens, out_grad, live, ln1_gain[None], ln1_bias[None], qkv_weight, out_weight, down_weight),
        [ANY, ANY, HELD, HELD, HELD, ANY, ANY, ANY],
        [
            (rows_here, bf16),
            (rows_here, bf16),
            (rows_all, bf16),
            (rows_all, bf16),
            (qkv_weight.shape, bf16),
            (out_weight.shape, bf16),
            (down_weight.shape, bf16),
        ],
        [ANY] * 4 + [HELD] * 3,
        (pltpu.VMEM(rows_here, bf16),) * 4
        + (dma((2,)), dma((2,)), dma((6,)))
        + Gather.scratch * 2
        + fetch_scratch(3),
    )

    cosine, sine_table = rotary_tables(position)
    projected = [
        jnp.dot(normed1, qkv[channel], preferred_element_type=jnp.float32) + bias[channel]
        for channel in range(3)
    ]
    queries = rotate(
        projected[0].reshape(row_total, local_heads, HEAD_DIM), cosine, sine_table
    ).astype(bf16)
    keys_low = rotate(
        projected[1].reshape(row_total, local_heads, HEAD_DIM), cosine, sine_table
    ).astype(bf16)
    values_low = projected[2].reshape(row_total, local_heads, HEAD_DIM).astype(bf16)
    block_size = min(512, row_total)
    block_count = row_total // block_size
    out_blocks = []
    log_norms = []
    for block_index in range(block_count):
        begin_row = block_index * block_size
        end_row = begin_row + block_size
        allowed = block_mask(segment, row_ids, begin_row, end_row)
        scores = (
            jnp.einsum(
                "qhd,khd->hqk",
                queries[begin_row:end_row],
                keys_low[:end_row],
                preferred_element_type=jnp.float32,
            )
            * score_scale
        )
        scores = jnp.where(allowed[None], scores, -1e30)
        row_max = jnp.max(scores, axis=-1, keepdims=True)
        exp_scores = jnp.exp(scores - row_max)
        exp_sum = jnp.sum(exp_scores, axis=-1, keepdims=True)
        attn_prob = (exp_scores / exp_sum).astype(bf16)
        out_blocks.append(
            jnp.einsum(
                "hqk,khd->qhd", attn_prob, values_low[:end_row], preferred_element_type=jnp.float32
            ).astype(bf16)
        )
        log_norms.append(row_max + jnp.log(exp_sum))
    attended = jnp.concatenate(out_blocks, axis=0).reshape(row_total, local_heads * HEAD_DIM)
    attn_part = jnp.dot(attended, out, preferred_element_type=jnp.float32).astype(bf16)

    gate_up_t = jnp.swapaxes(gate_up_weight, 1, 2)
    ff = down_weight.shape[0]
    vmem = pltpu.VMEM
    mid_stream, d_mid, gain2_part, shift2_part, ffn_grad, ffn_part, d_attended, out_grad = call(
        middle_kernel,
        2,
        (
            attn_part,
            tokens_here,
            ln2_gain[None],
            ln2_bias[None],
            gate_up_t,
            down,
            cot_rows,
            attended,
            out,
            cot,
        ),
        [ANY, HELD, HELD, HELD, ANY, ANY, ANY, ANY, ANY, HELD],
        [
            (rows_here, f32),
            (rows_here, f32),
            ((1, 2048), f32),
            ((1, 2048), f32),
            ((3, ff, 2048), bf16),
            (rows_all, bf16),
            (attended.shape, bf16),
            (out.shape, bf16),
        ],
        [HELD, HELD, HELD, HELD, ANY, ANY, HELD, HELD],
        (
            vmem((2, ff, 2048), bf16),
            vmem((ff, 2048), bf16),
            vmem(out.shape, bf16),
            vmem(rows_all, bf16),
            vmem(rows_all, bf16),
            vmem(rows_all, bf16),
            vmem(attended.shape, bf16),
            vmem((row_total, ff), bf16),
            vmem((row_total, ff), bf16),
            vmem((row_total, ff), bf16),
            vmem((row_total, ff), f32),
            vmem((SIDE, BLOCK, 2048), bf16),
            vmem((SIDE, BLOCK, 2048), bf16),
            vmem((PAIR, 2048), bf16),
            vmem((2, ff, 512), bf16),
            dma((8,)),
            dma((8,)),
            dma((6,)),
            dma,
            dma((2,)),
        )
        + Scatter.scratch
        + Scatter.sems
        + Gather.scratch * 2
        + fetch_scratch(2),
    )

    d_attended = d_attended.reshape(row_total, local_heads, HEAD_DIM)
    query_grads = []
    d_key = jnp.zeros((row_total, local_heads, HEAD_DIM), f32)
    d_value = jnp.zeros((row_total, local_heads, HEAD_DIM), f32)
    for block_index in range(block_count):
        begin_row = block_index * block_size
        end_row = begin_row + block_size
        allowed = block_mask(segment, row_ids, begin_row, end_row)
        query_block = queries[begin_row:end_row]
        key_block = keys_low[:end_row]
        grad_block = d_attended[begin_row:end_row]
        scores = (
            jnp.einsum("qhd,khd->hqk", query_block, key_block, preferred_element_type=jnp.float32)
            * score_scale
        )
        scores = jnp.where(allowed[None], scores, -1e30)
        attn_full = jnp.exp(scores - log_norms[block_index])
        attn_prob = attn_full.astype(bf16)
        d_prob = jnp.einsum(
            "qhd,khd->hqk", grad_block, values_low[:end_row], preferred_element_type=jnp.float32
        )
        row_dots = jnp.sum(attn_full * d_prob, axis=-1, keepdims=True)
        d_score = (attn_full * (d_prob - row_dots)).astype(bf16)
        query_grads.append(
            jnp.einsum("hqk,khd->qhd", d_score, key_block, preferred_element_type=jnp.float32)
            * score_scale
        )
        d_key = d_key.at[:end_row].add(
            jnp.einsum("hqk,qhd->khd", d_score, query_block, preferred_element_type=jnp.float32)
            * score_scale
        )
        d_value = d_value.at[:end_row].add(
            jnp.einsum("hqk,qhd->khd", attn_prob, grad_block, preferred_element_type=jnp.float32)
        )
    d_query = jnp.concatenate(query_grads, axis=0)
    d_proj = [
        rotate(d_query, cosine, -sine_table).reshape(row_total, -1).astype(bf16),
        rotate(d_key, cosine, -sine_table).reshape(row_total, -1).astype(bf16),
        d_value.reshape(row_total, -1).astype(bf16),
    ]
    summed = times_transposed(d_proj[0], qkv[0])
    summed = summed + times_transposed(d_proj[1], qkv[1])
    d_norm_part = (summed + times_transposed(d_proj[2], qkv[2])).astype(bf16)

    qkv_part = jnp.concatenate(
        [contract_rows(normed1, d_proj[channel]).astype(bf16) for channel in range(3)]
    )
    bias_part = jnp.stack([jnp.sum(d.astype(f32), axis=0) for d in d_proj])
    bias_part = lax.dynamic_update_slice_in_dim(
        jnp.zeros((3, 2048), f32), bias_part, shard * bias_part.shape[1], 1
    )
    norm_part = jnp.concatenate(
        [jnp.zeros((2, 2048), f32), gain2_part, shift2_part, bias_part, jnp.zeros((1, 2048), f32)]
    )
    ff_part = ffn_grad.reshape(3 * ff, 2048)
    unit_count = 2048 // WIDE
    small = (8, 2048)
    mixed, input_grad, ff_full, qkv_full, out_full, sums = call(
        last_kernel,
        4,
        (
            d_norm_part,
            tokens_here,
            d_mid,
            ln1_gain[None],
            ffn_part,
            mid_stream,
            ff_part,
            qkv_part,
            out_grad,
            norm_part,
        ),
        [ANY, HELD, HELD, HELD, ANY, HELD, ANY, ANY, ANY, HELD],
        [
            (rows_here, bf16),
            (rows_here, f32),
            (ff_part.shape, bf16),
            (qkv_part.shape, bf16),
            (out.shape, bf16),
            (small, f32),
        ],
        [ANY, ANY, ANY, ANY, ANY, HELD],
        (
            vmem(rows_here, f32),
            vmem(rows_here, bf16),
            vmem((SIDE, BLOCK, 2048), bf16),
            vmem((SIDE, BLOCK, 2048), bf16),
            dma((8,)),
            dma((FF_LINKS * unit_count + ATTN_LINKS * 3 + 12,)),
            dma((FF_LINKS * unit_count + ATTN_LINKS * 3 + 12,)),
            dma((2 * unit_count + 4 * 3 + 10,)),
            vmem((SIDE, *small), f32),
            vmem((2, *small), f32),
            vmem((SIDE, *small), f32),
            vmem((SIDE, *small), f32),
        )
        + Scatter.scratch * 2
        + (vmem((3 * ff, WIDE), bf16),) * 2
        + ff_scratch(3 * ff) * unit_count
        + sum((attn_scratch(unit) for unit in ATTN_UNITS), ()),
    )
    ff_grads = ff_full.reshape(3, ff, 2048)
    gate_up_grad = jnp.swapaxes(ff_grads[:2], 1, 2).astype(f32)
    down_grad = ff_grads[2].astype(f32)
    qkv_weight_grad = qkv_full.reshape(3, 2048, -1).astype(f32)
    out_weight_grad = out_full.astype(f32)
    width = qkv_bias.shape[1]
    qkv_bias_grad = lax.dynamic_slice_in_dim(sums[4:7], (z_hi * SIDE + x) * width, width, 1)
    return (
        mixed,
        input_grad,
        sums[0],
        sums[1],
        qkv_weight_grad,
        qkv_bias_grad,
        out_weight_grad,
        sums[2],
        sums[3],
        gate_up_grad,
        down_grad,
    )


def solution(mesh):
    placed = (
        P(("dp", "tensor"), None),
        P(),
        P(),
        P(),
        P(),
        P(None, None, "tensor"),
        P(None, "tensor"),
        P("tensor", None),
        P(),
        P(),
        P(None, None, "tensor"),
        P("tensor", None),
        P(("dp", "tensor"), None),
    )
    return jax.shard_map(
        body,
        mesh=mesh,
        in_specs=placed,
        out_specs=(
            P(("dp", "tensor"), None),
            P(("dp", "tensor"), None),
            P(),
            P(),
            P(None, None, "tensor"),
            P(None, "tensor"),
            P("tensor", None),
            P(),
            P(),
            P(None, None, "tensor"),
            P("tensor", None),
        ),
        check_vma=False,
    )
```

time: 770 us -> 540 us (0.70)
  Pallas kernels: 245 us -> 416 us
  waiting for transfers between devices: 163 us -> 0.01 us
  starting transfers between devices: 76.1 us -> 6.89 us
  blocking collectives: 65.8 us -> 0 us
  local copies, waits for them, and re-layouts: 73.5 us -> 16.8 us
  matrix products: 88.8 us -> 56.8 us
  other arithmetic: 45.1 us -> 31.4 us
    pallas_call x4 -> x3, Pallas kernels: 245 us -> 416 us  [call(): pl.pallas_call(kernel, out_shape=[jax.ShapeDtypeStruct(shape, kind) for s...]
    ppermute x25 -> x1, waiting for transfers between devices: 163 us -> 0.01 us  [permute(): return lax.ppermute(array, AXES, pairs(move))]
    ppermute x25 -> x1, starting transfers between devices: 76.1 us -> 6.89 us  [permute(): return lax.ppermute(array, AXES, pairs(move))]
    psum x1 -> x0, blocking collectives: 65.8 us -> none  [body(): lax.psum((jnp.concatenate([gain1_part, shift1_part, gain2_part, shift2_pa...]
    transpose x2 -> x0, local copies, waits for them, and re-layouts: 13.8 us -> none  [the longest x1 10.6 us: body(): gate_up_grad, down_grad = (jnp.swapaxes(ffn_grad[:2], 1, 2), ffn_grad[2])]
    dot_general x3 -> x1, matrix products: 14.5 us -> 0.92 us  [body(): jnp.einsum('qhd,khd->hqk', query_block, key_block, preferred_element_type...]
    convert_element_type x9 -> x4, other arithmetic: 27.7 us -> 15.9 us  [the longest x1 6 us: body(): gate_up_grad = jnp.swapaxes(ff_grads[:2], 1, 2).astype(f32)]
    dot_general x7 -> x3, matrix products: 18.1 us -> 7.29 us  [contract_rows(): lax.dot_general(left_rows, right_rows, (((0,), (0,)), ((), ())), preferre...]
  transfers between devices with their start and end apart: 25 -> 1, of which waited for: 10 -> 0; matrix products, arithmetic and copies ran while one was open for 13% -> 1% of each run, Pallas kernels for 15% -> 12%
where the time goes in v2:
time: 540 us; the launch traced here: 530 us
  Pallas kernels  416 us (77%)
  matrix products  56.8 us (11%)
  other arithmetic  31.4 us (6%)
  local copies, waits for them, and re-layouts  16.8 us (3%)
  starting transfers between devices  6.89 us (1%)
    pallas_call x3, Pallas kernels, call(): pl.pallas_call(kernel, out_shape=[jax.ShapeDtypeStruct(shape, kind) for s...  416 us
    dot_general x3, matrix products, times_transposed(): lax.dot_general(left_rows, right_rows, (((1,), (1,)), ((), ())), preferre...  18.8 us
    unnamed x78, local copies, waits for them, and re-layouts  11.3 us
  transfers between devices with their start and end apart: 1, of which 0 were waited for; matrix products, arithmetic and copies ran while one was open for 1% of the time, Pallas kernels for 12%

profile of v2, /device:TPU:1, one launch (start us, length us, event | category | flops | bytes accessed | tf_op | source)
XLA Modules:
  0.0 530.2 jit_solution(5503086838043529568)
XLA Ops:
  0.6 6.9 %collective-permute-start = (f32[3,256]{1,0:T(4,128)}, f32[3,256]{1,0:T(4,128)S(1)}, u32[]{:S(2)}, u32[]{:S(2)}) collective-permute-start(f32[3,256]{1,0:T(4,128)} %param.31), channel_id=1, source_target_pairs={{0,0},{1,1},{2,2},{3,3},{4,8},{5,9},{6,10},{7,11},{8,4},{9,5},{10,... | collective-permute-start | bytes 9224 | tf_op jit(solution)/shard_map/ppermute | solution.py:46
  7.6 0.7 compare_convert_fusion
  8.2 0.8 select_reduce_fusion
  9.1 0.7 add.139
  9.7 0.2 multiply_reduce_fusion.3
  10.0 0.8 fusion.58
  10.8 1.0 compare_and_fusion
  11.8 1.4 fusion.11
  13.4 1.0 copy-done.2
  14.4 1.0 copy-done.3
  15.5 0.7 copy-done.4
  16.2 0.7 copy-done.8
  16.9 64.2 %shard_map.222 = (bf16[128,2048]{1,0:T(8,128)(2,1)S(1)}, bf16[128,2048]{1,0:T(8,128)(2,1)S(1)}, bf16[1024,2048]{1,0:T(8,128)(2,1)}, bf16[1024,2048]{1,0:T(8,128)...) custom-call(bf16[128,2048]{1,0:T(8,128)(2,1)S(1)} %copy-done.2, ...), custom_call_target="tpu_custom_call" | custom-call | tf_op jit(solution)/shard_map/pallas_call | solution.py:1281
  81.1 4.2 broadcast_add_fusion
  85.4 0.8 copy-done.34
  86.2 1.3 broadcast_add_fusion.1
  87.7 0.9 fusion.67
  88.7 0.6 fusion.6
  89.3 1.1 log_add_fusion.1
  90.3 1.3 add_convert_fusion.1
  91.7 0.7 copy-done.18
  92.5 0.8 fusion.33
  93.3 0.2 copy-done.27
  93.5 1.8 fusion.66
  95.3 1.9 fusion
  97.2 1.2 log_add_fusion
  98.4 0.3 copy-done.9
  98.7 2.1 fusion.32
  100.9 0.2 copy.44.attended_full
  101.1 3.3 convolution_convert_fusion.part
  104.5 116.4 %shard_map.223 = (f32[128,2048]{1,0:T(8,128)S(1)}, f32[128,2048]{1,0:T(8,128)}, f32[1,2048]{1,0:T(1,128)S(1)}, f32[1,2048]{1,0:T(1,128)S(1)}, bf16[3,704,2048]{2...) custom-call(bf16[1024,2048]{1,0:T(8,128)(2,1)} %convolution_convert_fusion., ...), custom_call_target="tpu_custom_call" | custom-call | tf_op jit(solution)/shard_map/pallas_call | solution.py:1281
  220.9 1.0 copy-done.1
  222.1 3.1 fusion.24
  225.2 0.3 copy-done.11
  225.5 0.9 multiply_reduce_fusion.1
  226.5 1.2 multiply_convert_fusion.1
  227.7 0.5 fusion.29
  228.2 0.8 fusion.28
  228.9 0.1 copy.47
  229.1 5.3 multiply_reduce_fusion
  234.4 0.8 slice-done.1
  235.2 1.7 multiply_convert_fusion
  237.0 1.4 fusion.27
  238.4 0.9 fusion.17
  239.5 0.2 convert_reduce_fusion.1
  239.7 1.8 copy-done.35
  241.5 1.4 convolution_convert_fusion.2
  242.9 4.6 fusion.43
  247.5 2.4 convolution_convert_fusion.3
  249.9 4.7 fusion.39
  254.6 2.1 convert_reduce_fusion
  256.9 3.5 convolution_convert_fusion.1
  260.5 9.5 %add_convert_fusion.part = bf16[1024,2048]{1,0:T(8,128)(2,1)} fusion(f32[1024,2048]{1,0:T(8,128)} %fusion.39, f32[1024,2048]{1,0:T(8,128)} %fusion.43, bf16[1024,256]{0,1:T(8,128)(2,1)S(1)} %bitcast.122, bf16[3,2048,256]{2,1,0:T(8,128)(2,1)} %get-tuple-element.97), kind=kOutput, calls=%fused_computation.1 | convolution fusion | flops 1080033280 | bytes 22544384 | tf_op jit(solution)/shard_map/dot_general | solution.py:1344
  270.0 1.8 pad_maximum_fusion.qkv_part
  271.9 235.8 %shard_map.224 = (bf16[128,2048]{1,0:T(8,128)(2,1)S(1)}, f32[128,2048]{1,0:T(8,128)S(1)}, bf16[2112,2048]{1,0:T(8,128)(2,1)}, bf16[6144,256]{1,0:T(8,128)(2,1)},...) custom-call(bf16[1024,2048]{1,0:T(8,128)(2,1)} %add_convert_fusion.part, ...), custom_call_target="tpu_custom_call" | custom-call | tf_op jit(solution)/shard_map/pallas_call | solution.py:1281
  507.6 3.1 slice.249
  510.8 5.1 slice_convert_fusion
  515.9 0.6 fusion.63
  516.6 6.0 %convert_bitcast_fusion = f32[2,2048,704]{1,2,0:T(8,128)} fusion(bf16[2,704,2048]{2,1,0:T(8,128)(2,1)S(1)} %bitcast.107), kind=kLoop, calls=%fused_computation | loop fusion | flops 2883584 | bytes 17301504 | tf_op jit(solution)/shard_map/convert_element_type | solution.py:1608
  522.6 3.2 convert.29
  525.8 1.6 convert_element_type.173
  527.4 0.6 constant_dynamic-slice_fusion
  528.0 0.8 copy.57
  528.7 1.0 copy.58
  (97 shorter events, 1.3 us)
Async XLA Ops:
  0.6 80.5 %collective-permute-start = (f32[3,256]{1,0:T(4,128)}, f32[3,256]{1,0:T(4,128)S(1)}, u32[]{:S(2)}, u32[]{:S(2)}) collective-permute-start(f32[3,256]{1,0:T(4,128)} %param.31), channel_id=1, source_target_pairs={{0,0},{1,1},{2,2},{3,3},{4,8},{5,9},{6,10},{7,11},{8,4},{9,5},{10,... | collective-permute-start | bytes 9224 | tf_op jit(solution)/shard_map/ppermute | solution.py:46
  10.8 76.7 %copy-start.28 = (f32[1024,8]{0,1:T(8,128)}, f32[1024,8]{0,1:T(8,128)S(1)}, u32[]{:S(2)}) copy-start(f32[1024,8]{0,1:T(8,128)S(1)} %get-tuple-element.144) | copy-start | bytes 98308
  13.4 1.0 copy-start.2
  14.4 1.0 copy-start.3
  15.5 0.7 copy-start.4
  16.2 0.7 copy-start.8
  81.1 20.1 %copy-start = (bf16[256,2048]{1,0:T(8,128)(2,1)}, bf16[256,2048]{1,0:T(8,128)(2,1)S(1)}, u32[]{:S(2)}) copy-start(bf16[256,2048]{1,0:T(8,128)(2,1)S(1)} %get-tuple-element.98.out_held) | copy-start | bytes 3145732
  81.1 4.3 copy-start.12
  81.1 5.1 copy-start.34
  86.2 1.5 copy-start.31
  87.7 5.6 %copy-start.21 = (bf16[1024,4,8]{0,2,1:T(8,128)(2,1)}, bf16[1024,4,8]{0,2,1:T(8,128)(2,1)S(1)}, u32[]{:S(2)}) copy-start(bf16[1024,4,8]{0,2,1:T(8,128)(2,1)S(1)} %get-tuple-element.129) | copy-start | bytes 196612
  87.7 5.6 %copy-start.24 = (bf16[1024,4,8]{0,2,1:T(8,128)(2,1)}, bf16[1024,4,8]{0,2,1:T(8,128)(2,1)S(1)}, u32[]{:S(2)}) copy-start(bf16[1024,4,8]{0,2,1:T(8,128)(2,1)S(1)} %get-tuple-element.130) | copy-start | bytes 196612
  87.7 5.6 %copy-start.15 = (bf16[1024,4,64]{0,2,1:T(8,128)(2,1)}, bf16[1024,4,64]{0,2,1:T(8,128)(2,1)S(1)}, u32[]{:S(2)}) copy-start(bf16[1024,4,64]{0,2,1:T(8,128)(2,1)S(1)} %pad_maximum_fusion.2) | copy-start | bytes 1572868
  88.7 3.0 copy-start.10
  91.7 6.7 %copy-start.17 = (bf16[1024,256]{0,1:T(8,128)(2,1)}, bf16[1024,256]{0,1:T(8,128)(2,1)S(1)}, u32[]{:S(2)}) copy-start(bf16[1024,256]{0,1:T(8,128)(2,1)S(1)} %add_convert_fusion.1) | copy-start | bytes 1572868
  91.7 0.8 copy-start.18
  92.5 1.0 copy-start.27
  95.3 3.4 copy-start.9
  101.1 3.3 copy-start.6
  101.1 3.3 copy-start.7
  104.5 117.6 %copy-start.33 = (f32[4,512]{1,0:T(4,128)S(1)}, f32[4,512]{1,0:T(4,128)}, u32[]{:S(2)}) copy-start(f32[4,512]{1,0:T(4,128)} %log_add_fusion.1) | copy-start | bytes 24580
  220.9 1.0 copy-start.1
  221.8 3.3 copy-start.19
  222.0 3.5 copy-start.11
  226.4 1.2 copy-start.22
  226.5 1.2 copy-start.25
  226.5 1.7 copy-start.16
  229.1 5.3 %slice-start = ((s8[8388608]{0:T(1024)(128)(4,1)}), s8[4194304]{0:T(1024)(128)(4,1)S(1)}, s32[]{:S(2)}) async-start(s8[8388608]{0:T(1024)(128)(4,1)} %bitcast.105), calls=%async_computation | async-start | bytes 8388608
  229.1 6.1 %slice-start.1 = ((s8[8388608]{0:T(1024)(128)(4,1)}), s8[4194304]{0:T(1024)(128)(4,1)S(1)}, s32[]{:S(2)}) async-start(s8[8388608]{0:T(1024)(128)(4,1)} %bitcast.105), calls=%async_computation.1 | async-start | bytes 8388608
  229.1 6.1 %copy-start.32 = (f32[4,512]{1,0:T(4,128)S(1)}, f32[4,512]{1,0:T(4,128)}, u32[]{:S(2)}) copy-start(f32[4,512]{1,0:T(4,128)} %log_add_fusion) | copy-start | bytes 24580
  235.2 1.7 copy-start.23
  235.2 1.8 copy-start.26
  238.4 1.0 copy-start.29
  238.4 1.0 copy-start.30
  239.3 2.2 copy-start.35
  239.7 3.2 copy-start.13
  260.5 9.5 %copy-start.20 = (bf16[2048,256]{1,0:T(8,128)(2,1)S(1)}, bf16[2048,256]{1,0:T(8,128)(2,1)}, u32[]{:S(2)}) copy-start(bf16[2048,256]{1,0:T(8,128)(2,1)} %convolution_convert_fusion.3) | copy-start | bytes 3145732
  270.0 1.9 copy-start.5
  516.5 6.0 %copy-start.14 = (bf16[6144,256]{1,0:T(8,128)(2,1)S(1)}, bf16[6144,256]{1,0:T(8,128)(2,1)}, u32[]{:S(2)}) copy-start(bf16[6144,256]{1,0:T(8,128)(2,1)} %get-tuple-element.114) | copy-start | bytes 9437188

commit v3 on v2

--- a/solution.py
+++ b/solution.py
@@ -13,7 +13,7 @@
 BLOCK = 128
 AXES = ("dp", "tensor")
 MESH = pl.DeviceIdType.MESH
-VMEM_LIMIT = 50 * 2**20
+VMEM_LIMIT = 54 * 2**20
 
 
 def here():
@@ -333,6 +333,58 @@
         body(pl.ds(pl.multiple_of(row, 16), 16))
 
 
+def matmul(left, right, contract):
+    return lax.dot_general(left, right, ((contract, ((), ()))), preferred_element_type=jnp.float32)
+
+
+NN, NT, TN = ((1,), (0,)), ((1,), (1,)), ((0,), (0,))
+PAIR = 2 * BLOCK
+TILE = 256
+
+
+class Locals:
+    def __init__(self, sems):
+        self.sems, self.used = sems, 0
+
+    def of(self, source, target):
+        self.used += 1
+        return pltpu.make_async_copy(source, target, self.sems.at[self.used - 1])
+
+
+def attention(queries, keys, values, row_info, segments, segment_row, attended, score_scale):
+    bf16 = jnp.bfloat16
+    lane = lax.broadcasted_iota(jnp.int32, (1, 128), 1)
+    row_info[...] = jnp.where(lane == 4, segments[...], 0.0)
+    for block in range(4):
+        first, end = block * PAIR, (block + 1) * PAIR
+        rows, before = pl.ds(first, PAIR), pl.ds(0, end)
+        places = first + lax.broadcasted_iota(jnp.int32, (PAIR, end), 0)
+        allowed = (segments[rows, :] == segment_row[:, 0:end]) & (
+            lax.broadcasted_iota(jnp.int32, (PAIR, end), 1) <= places
+        )
+
+        @pl.loop(0, 2)
+        def _(pair):
+            lanes = pl.ds(pl.multiple_of(pair * 128, 128), 128)
+            query, key, value = queries[rows, lanes], keys[before, lanes], values[before, lanes]
+            mixed = jnp.zeros((PAIR, 128), jnp.float32)
+            for head in range(2):
+                inside = (lane >= head * HEAD_DIM) & (lane < (head + 1) * HEAD_DIM)
+                query_h = jnp.where(inside, query, jnp.zeros_like(query))
+                value_h = jnp.where(inside, value, jnp.zeros_like(value))
+                scores = jnp.where(allowed, matmul(query_h, key, NT) * score_scale, -1e30)
+                top = jnp.max(scores, axis=1, keepdims=True)
+                raised = jnp.exp(scores - top)
+                total = jnp.sum(raised, axis=1, keepdims=True)
+                mixed = mixed + matmul((raised / total).astype(bf16), value_h, NN)
+                row_info[rows, :] = jnp.where(
+                    lane == pair * 2 + head, top + jnp.log(total), row_info[rows, :]
+                )
+            attended[rows, lanes] = mixed.astype(bf16)
+
+        yield
+
+
 def first_kernel(
     tokens,
     out_grad,
@@ -342,22 +394,37 @@
     qkv,
     out,
     down,
+    bias,
+    segments,
+    segment_row,
+    keep,
+    from_after,
+    from_before,
     tokens_here,
     cot_here,
     normed_full,
     cot_full,
+    part,
     qkv_here,
     out_here,
     down_here,
+    queries,
+    keys,
+    values,
+    attended,
+    row_info,
     tok_buf,
     grad_buf,
-    norm_buf,
     cot_buf,
+    bias_buf,
+    normed,
+    part_tile,
     swap_send,
     swap_arrive,
     own_sems,
     *sems,
 ):
+    bf16 = jnp.bfloat16
     place = here()
     x, y, z_hi, z_lo, core = place
     lacking = core != z_hi
@@ -369,24 +436,36 @@
             [(qkv, qkv_here, QKV_CUT), (out, out_here, OUT_CUT), (down, down_here, FF_CUT)]
         )
     ]
+    moved = [(tokens, tok_buf), (out_grad, grad_buf), (bias, bias_buf)]
     swaps = [
         remote(source, target, swap_send, swap_arrive, index, swap_with)
-        for index, (source, target) in enumerate([(tokens, tok_buf), (out_grad, grad_buf)])
+        for index, (source, target) in enumerate(moved)
     ]
-    stays = [
-        pltpu.make_async_copy(source, target, own_sems.at[index])
-        for index, (source, target) in enumerate([(tokens, tok_buf), (out_grad, grad_buf)])
+    locals_ = Locals(own_sems)
+    stays = [locals_.of(source, target) for source, target in moved]
+    gather = Gather(normed.at[pl.ds(0, BLOCK)], ByStep(normed), place, sems[:4])
+    gather_cot = Gather(cot_buf, ByRow(cot_full, place), place, sems[4:8])
+    by_step, by_row = ByStep(normed), ByRow(normed_full, place)
+    normed_out = [
+        locals_.of(by_step.at(step, other), by_row.at(step, other)) for step in range(SIDE) for other in range(2)
     ]
+    stored = [
+        locals_.of(tok_buf, tokens_here),
+        locals_.of(cot_buf, cot_here),
+        locals_.of(cot_buf, row_block(cot_full, core, x)),
+    ]
+    part_sem = own_sems.at[locals_.used]
 
     @pl.when(lacking)
     def _():
         greet(line_peers(place) + [swap_with] + fetch_peers(place))
         swaps[0].start()
-        swaps[0].wait_recv()
+        swaps[2].start()
         fetches[0].across.start()
         swaps[1].start()
         fetches[1].across.start()
         fetches[2].across.start()
+        swaps[0].wait_recv()
 
     @pl.when(jnp.logical_not(lacking))
     def _():
@@ -399,85 +478,122 @@
 
     def norm(rows):
         centre, scale = moments(tok_buf[rows, :].astype(jnp.float32))
-        norm_buf[rows, :] = (centre * scale * gain[...] + shift[...]).astype(jnp.bfloat16)
+        normed[rows, :] = (centre * scale * gain[...] + shift[...]).astype(bf16)
 
     tile_rows(norm)
-    gather = Gather(norm_buf, ByRow(normed_full, place), place, sems[:4])
-    gather_cot = Gather(cot_buf, ByRow(cot_full, place), place, sems[4:8])
-    stored = [
-        pltpu.make_async_copy(source, target, own_sems.at[2 + index])
-        for index, (source, target) in enumerate(
-            [
-                (norm_buf, row_block(normed_full, core, x)),
-                (tok_buf, tokens_here),
-                (cot_buf, cot_here),
-                (cot_buf, row_block(cot_full, core, x)),
-            ]
-        )
-    ]
     gather.start()
     stored[0].start()
-    stored[1].start()
 
     @pl.when(lacking)
     def _():
         fetches[0].spread()
-        swaps[0].wait_send()
-        swaps[1].wait()
+        for copy in swaps:
+            copy.wait_send()
+        swaps[1].wait_recv()
+        swaps[2].wait_recv()
 
     @pl.when(jnp.logical_not(lacking))
     def _():
         stays[1].wait()
+        stays[2].wait()
 
     def mask(rows):
-        cot_buf[rows, :] = (grad_buf[rows, :].astype(jnp.float32) * live[rows, :]).astype(jnp.bfloat16)
+        cot_buf[rows, :] = (grad_buf[rows, :].astype(jnp.float32) * live[rows, :]).astype(bf16)
 
     tile_rows(mask)
-    gather_cot.start()
-    stored[2].start()
-    stored[3].start()
     gather.arrive(1)
     gather.arrive(3)
+    gather_cot.start()
+    stored[1].start()
+    stored[2].start()
 
     @pl.when(lacking)
     def _():
+        fetches[0].pass_on()
         fetches[1].spread()
         fetches[2].spread()
-        fetches[0].pass_on()
 
     gather.arrive(2)
+    gather.take()
+    for copy in normed_out:
+        copy.start()
+
+    @pl.when(lacking)
+    def _():
+        fetches[0].finish()
+
+    @pl.when(jnp.logical_not(lacking))
+    def _():
+        fetches[0].own.wait()
+
     gather_cot.arrive(1)
     gather_cot.arrive(3)
 
+    @pl.loop(0, 8)
+    def _(index):
+        step, other = lax.div(index, 2), lax.rem(index, 2)
+        whose = core + other * (1 - 2 * core)
+        first = pl.multiple_of((whose * SIDE + turned(x, SIDE - step)) * BLOCK, BLOCK)
+        rows = pl.ds(first, BLOCK)
+        block = normed[pl.ds(pl.multiple_of(index * BLOCK, BLOCK), BLOCK), :]
+        for channel, target in enumerate((queries, keys, values)):
+            projected = matmul(block, qkv_here[channel], NN) + bias_buf[channel : channel + 1, :]
+            for pair in range(2):
+                lanes = projected[:, pair * 128 : (pair + 1) * 128]
+                if channel < 2:
+                    lanes = (
+                        lanes * keep[rows, :]
+                        - pltpu.roll(lanes, 120, 1) * from_after[rows, :]
+                        - pltpu.roll(lanes, 8, 1) * from_before[rows, :]
+                    )
+                target[rows, pair * 128 : (pair + 1) * 128] = lanes.astype(bf16)
+
     @pl.when(lacking)
     def _():
         fetches[1].pass_on()
         fetches[2].pass_on()
 
     gather_cot.arrive(2)
+    blocks = attention(
+        queries, keys, values, row_info, segments, segment_row, attended, HEAD_DIM ** (-0.5)
+    )
+    for block in range(4):
+        next(blocks)
+        rows = pl.ds(block * PAIR, PAIR)
+        if block == 0:
+
+            @pl.when(lacking)
+            def _():
+                fetches[1].finish()
+
+            @pl.when(jnp.logical_not(lacking))
+            def _():
+                fetches[1].own.wait()
+
+        else:
+            pltpu.make_async_copy(part_tile, part.at[rows], part_sem).wait()
+
+        @pl.loop(0, 2048, step=512)
+        def _(column):
+            columns = pl.ds(pl.multiple_of(column, 512), 512)
+            part_tile[:, columns] = matmul(attended[rows, :], out_here[:, columns], NN).astype(bf16)
+
+        pltpu.make_async_copy(part_tile, part.at[rows], part_sem).start()
+
+    gather_cot.take()
     for each in (gather, gather_cot):
-        each.take()
         each.finish()
-    for copy in stored:
+    for copy in normed_out + stored:
         copy.wait()
+    pltpu.make_async_copy(part_tile, part.at[pl.ds(0, PAIR)], part_sem).wait()
 
     @pl.when(lacking)
     def _():
-        for fetch in fetches:
-            fetch.finish()
+        fetches[2].finish()
 
     @pl.when(jnp.logical_not(lacking))
     def _():
-        for fetch in fetches:
-            fetch.own.wait()
-
-
-def matmul(left, right, contract):
-    return lax.dot_general(left, right, ((contract, ((), ()))), preferred_element_type=jnp.float32)
-
-
-NN, NT, TN = ((1,), (0,)), ((1,), (1,)), ((0,), (0,))
-PAIR = 2 * BLOCK
+        fetches[2].own.wait()
 
 
 def middle_kernel(
@@ -495,7 +611,11 @@
     d_mid,
     gain_part,
     shift_part,
-    grads,
+    gate_grad,
+    up_grad,
+    down_grad,
+    gate_beyond,
+    down_sum,
     ffn_part,
     d_attended,
     out_grad,
@@ -538,8 +658,18 @@
     gather = Gather(normed.at[pl.ds(0, BLOCK)], ByStep(normed), place, scratch[11:15])
     gather_d = Gather(d_rows.at[pl.ds(0, BLOCK)], ByStep(d_rows), place, scratch[15:19])
     fetches = [
-        Fetch(gate_up_own.at[index], gate_up.at[index], FF_CUT, place, scratch[19:], index) for index in range(2)
+        Fetch(gate_up_own.at[index], gate_up.at[index], FF_CUT, place, scratch[19:22], index) for index in range(2)
     ]
+    around = Around(place)
+    links = Links(*scratch[22:24])
+    over = links.to(gate_grad, gate_beyond, around.beyond)
+    ring = RowRing(*DOWN_RING)
+    ring_terms = scratch[24:27]
+    ring_loads = [
+        pltpu.make_async_copy(ring.quarter(down_grad, turned(y, k)), held, load_sems.at[index])
+        for index, (k, held) in enumerate(zip((1, 3, 0), ring_terms))
+    ]
+    ring.bind(links, around, scratch[27:], ring.quarter(down_grad, turned(y, 2)), *ring_terms)
     load_cot = Loaded(cot_full, cot_rows, place, load_sems)
     load_att = Loaded(attended_full, attended, place, att_sems)
     load_own = [
@@ -557,11 +687,11 @@
 
     @pl.when(lacking)
     def _():
-        greet(line_peers(place) + fetch_peers(place))
+        greet(line_peers(place) + fetch_peers(place) + [around.beyond])
 
     @pl.when(jnp.logical_not(lacking))
     def _():
-        greet(line_peers(place))
+        greet(line_peers(place) + [around.up, around.down, around.beyond])
 
     for step in (2, 1, 3, 0):
         first.across[step].start()
@@ -669,37 +799,52 @@
     load_att.wait()
     load_out.wait()
 
-    @pl.loop(0, 4)
-    def _(index):
-        rows = pl.ds(pl.multiple_of(index * PAIR, PAIR), PAIR)
-
-        @pl.when(index > 0)
-        def _():
-            pltpu.make_async_copy(ffn_tile, ffn_part.at[rows], ffn_sem).wait()
-
-        @pl.loop(0, 2048, step=512)
-        def _(column):
-            columns = pl.ds(pl.multiple_of(column, 512), 512)
-            ffn_tile[:, columns] = matmul(hidden[rows, :], down[:, columns], NN).astype(bf16)
-
-        pltpu.make_async_copy(ffn_tile, ffn_part.at[rows], ffn_sem).start()
-
-    def weight_grad(index, left, right):
+    def ffn_terms():
         @pl.loop(0, 4)
+        def _(index):
+            rows = pl.ds(pl.multiple_of(index * PAIR, PAIR), PAIR)
+
+            @pl.when(index > 0)
+            def _():
+                pltpu.make_async_copy(ffn_tile, ffn_part.at[rows], ffn_sem).wait()
+
+            @pl.loop(0, 2048, step=512)
+            def _(column):
+                columns = pl.ds(pl.multiple_of(column, 512), 512)
+                ffn_tile[:, columns] = matmul(hidden[rows, :], down[:, columns], NN).astype(bf16)
+
+            pltpu.make_async_copy(ffn_tile, ffn_part.at[rows], ffn_sem).start()
+
+    def weight_grad(target, left, right):
+        def stored(tile, slot):
+            columns = pl.ds(pl.multiple_of(tile * TILE, TILE), TILE)
+            return pltpu.make_async_copy(grad_tile.at[slot], target.at[:, columns], grad_sems.at[slot])
+
+        @pl.loop(0, 8)
         def _(tile):
-            columns = pl.ds(pl.multiple_of(tile * 512, 512), 512)
-            target = grads.at[index, :, columns]
             slot = lax.rem(tile, 2)
-            copy = pltpu.make_async_copy(grad_tile.at[slot], target, grad_sems.at[slot])
-
-            @pl.when(jnp.logical_or(index > 0, tile > 1))
+
+            @pl.when(tile > 1)
             def _():
-                copy.wait()
-
+                stored(tile, slot).wait()
+
+            columns = pl.ds(pl.multiple_of(tile * TILE, TILE), TILE)
             grad_tile[slot] = matmul(left[...], right[:, columns], TN).astype(bf16)
-            copy.start()
-
-    weight_grad(0, d_gate, normed)
+            stored(tile, slot).start()
+
+        for slot in range(2):
+            stored(slot, slot).wait()
+
+    weight_grad(gate_grad, d_gate, normed)
+
+    @pl.when(lacking)
+    def _():
+        over.start()
+
+    weight_grad(down_grad, hidden, cot_rows)
+    ring.begin()
+    for copy in ring_loads:
+        copy.start()
     second.finish()
     gain_part[...] = jnp.zeros_like(gain_part)
     shift_part[...] = jnp.zeros_like(shift_part)
@@ -721,10 +866,13 @@
 
     tile_rows(back)
     gather_d.start()
-    weight_grad(1, d_up, normed)
+    for copy in ring_loads:
+        copy.wait()
+    ring.merge()
+    ffn_terms()
     gather_d.arrive(1)
     gather_d.arrive(3)
-    weight_grad(2, hidden, cot_rows)
+    weight_grad(up_grad, d_up, normed)
     gather_d.arrive(2)
     for step in range(SIDE):
         gather_d.across[step].wait_recv()
@@ -743,8 +891,19 @@
     gather.finish()
     gather_d.finish()
     pltpu.make_async_copy(ffn_tile, ffn_part.at[pl.ds(0, PAIR)], ffn_sem).wait()
-    for slot in range(2):
-        pltpu.make_async_copy(grad_tile.at[slot], grads.at[0, :, pl.ds(0, 512)], grad_sems.at[slot]).wait()
+    ring.sum()
+    down_stored = pltpu.make_async_copy(ring.total, down_sum, own_sems.at[0])
+    down_stored.start()
+    ring.sent()
+    down_stored.wait()
+
+    @pl.when(lacking)
+    def _():
+        over.wait_send()
+
+    @pl.when(jnp.logical_not(lacking))
+    def _():
+        over.wait_recv()
 
 
 class Links:
@@ -754,15 +913,6 @@
     def to(self, source, target, device_id):
         self.used += 1
         return remote(source, target, self.sends, self.arrives, self.used - 1, device_id)
-
-
-class Locals:
-    def __init__(self, sems):
-        self.sems, self.used = sems, 0
-
-    def of(self, source, target):
-        self.used += 1
-        return pltpu.make_async_copy(source, target, self.sems.at[self.used - 1])
 
 
 def each_rows(count, step, body):
@@ -898,62 +1048,79 @@
             copy.wait_send()
 
 
-WIDE = 512
-FF_RING = (528, 256, 176)
-ATTN_UNITS = (((768, 256, 96), 0), ((768, 256, 96), 3072), ((64, 2048, 16), 0))
-FF_STEPS, ATTN_STEPS = 9, 8
-FF_LINKS, ATTN_LINKS = 12, 11
-
-
-def ff_scratch(rows):
+WIDE = 1024
+DOWN_RING = (176, 2048, 16)
+ATTN_UNITS = ((768, 256, 96, 0), (768, 256, 96, 3072), (64, 2048, 16, 0))
+LINK_COUNT, LOCAL_COUNT = 112, 64
+
+
+def left_ring():
+    return RowRing(176, WIDE // 2, 176)
+
+
+def right_ring():
+    return RowRing(176, WIDE, 16)
+
+
+def left_scratch(rows, count):
     kind = jnp.bfloat16
-    return (
-        pltpu.VMEM((rows, WIDE), kind),
-        pltpu.VMEM((rows, WIDE // 2), kind),
-    ) + RowRing(*FF_RING).scratch()
-
-
-def attn_scratch(unit):
-    ring = RowRing(*unit[0])
-    held = pltpu.VMEM((ring.size, ring.width), jnp.bfloat16)
-    return (held,) * 5 + ring.scratch()
-
-
-def ff_sum(part, full, column, links, locals_, around, mine, scratch):
-    got, half = scratch[:2]
-    rows = got.shape[0]
-    width = WIDE // 2
-    ring = RowRing(*FF_RING)
-    stretch = lambda ref: ref.at[:, pl.ds(column, WIDE)]
+    half = pltpu.VMEM((rows, WIDE // 2), kind)
+    return (pltpu.VMEM((rows, WIDE), kind),) * 3 + ((half,) + left_ring().scratch()) * count
+
+
+def right_scratch(count):
+    return (pltpu.VMEM((176, WIDE), jnp.bfloat16),) * (4 * count)
+
+
+def attn_scratch():
+    found = ()
+    for size, width, step, _ in ATTN_UNITS:
+        ring = RowRing(size, width, step)
+        found += (pltpu.VMEM((size, width), jnp.bfloat16),) * 2 + ring.scratch()
+    return found
+
+
+def left_sum(part, beyond, full, column, fetch, links, locals_, around, mine, got, scratch):
+    half = scratch[0]
+    rows, width = got.shape[0], WIDE // 2
+    ring = left_ring()
     side = lambda z_lo: pl.ds(pl.multiple_of(z_lo * width, 128), width)
-    placed = lambda z_lo: full.at[:, pl.ds(pl.multiple_of(column + z_lo * width, 128), width)]
-    load = locals_.of(stretch(part), mine)
-    over = links.to(stretch(part), got, around.beyond)
+    columns = pl.ds(column, WIDE)
+    stretch = full.at[:, columns]
+    own_side = full.at[:, pl.ds(pl.multiple_of(column + around.z_lo * width, 128), width)]
+    loads = (locals_.of(part.at[:, columns], mine), locals_.of(beyond.at[:, columns], got))
+    if fetch:
+        over = links.to(part.at[:, columns], beyond.at[:, columns], around.beyond)
     kept, sent_on = side(around.z_lo), side(1 - around.z_lo)
     twin = links.to(got.at[:, sent_on], half, around.twin)
-    y = around.y
-    quarter = lambda k: ring.quarter(half, turned(y, k))
-    ring.bind(links, around, scratch[2:], quarter(2), quarter(1), quarter(3), quarter(0))
-    own_side = placed(around.z_lo)
+    quarter = lambda k: ring.quarter(half, turned(around.y, k))
+    ring.bind(links, around, scratch[1:], quarter(2), quarter(1), quarter(3), quarter(0))
     spread = RowSpread(ring, links, locals_, around, ring.total, own_side)
     both = links.to(own_side, own_side, around.twin)
-    core = links.to(stretch(full), stretch(full), around.partner)
-
-    @pl.when(around.gives)
-    def _():
-        over.start()
+    core = links.to(stretch, stretch, around.partner)
+
+    if fetch:
+
+        @pl.when(around.gives)
+        def _():
+            over.start()
+
+        yield
 
     @pl.when(around.keeps)
     def _():
-        load.start()
+        if fetch:
+            over.wait_recv()
+        for copy in loads:
+            copy.start()
 
     yield
 
     @pl.when(around.keeps)
     def _():
-        load.wait()
-        over.wait_recv()
-        add_into(got, of(got), of(mine), count=rows, step=96)
+        for copy in loads:
+            copy.wait()
+        add_into(got, of(got), of(mine), count=rows, step=64)
         twin.start()
 
     yield
@@ -961,8 +1128,9 @@
     @pl.when(around.keeps)
     def _():
         twin.wait_recv()
-        add_into(half, of(half), lambda rows: got[rows, kept], count=rows, step=96)
+        add_into(half, of(half), lambda rows: got[rows, kept], count=rows, step=64)
         ring.begin()
+        twin.wait_send()
 
     yield
 
@@ -1001,7 +1169,6 @@
 
     @pl.when(around.keeps)
     def _():
-        twin.wait_send()
         ring.sent()
         spread.sent()
         both.wait_send()
@@ -1009,86 +1176,105 @@
 
     @pl.when(around.gives)
     def _():
+        if fetch:
+            over.wait_send()
+        core.wait_recv()
+
+    yield
+
+
+def across_and_back(ring, total, spare, from_beyond, from_twin, full, first, links, locals_, around):
+    over = links.to(total, from_beyond, around.beyond)
+    twin = links.to(total, from_twin, around.twin)
+    spread = RowSpread(ring, links, locals_, around, spare, full, first)
+    span = full.at[pl.ds(first, SIDE * ring.size)]
+    core = links.to(span, span, around.partner)
+
+    @pl.when(around.gives)
+    def _():
+        over.start()
+
+    yield
+
+    @pl.when(around.keeps)
+    def _():
+        over.wait_recv()
+        add_into(total, of(total), of(from_beyond), count=ring.size, step=ring.step)
+        twin.start()
+
+    yield
+
+    @pl.when(around.keeps)
+    def _():
+        twin.wait_recv()
+        add_into(spare, of(total), of(from_twin), count=ring.size, step=ring.step)
+        spread.begin()
+
+    yield
+
+    @pl.when(around.keeps)
+    def _():
+        spread.pass_on()
+
+    yield
+
+    @pl.when(around.keeps)
+    def _():
+        spread.end()
+        core.start()
+
+    yield
+
+    @pl.when(around.keeps)
+    def _():
+        twin.wait_send()
+        spread.sent()
+        core.wait_send()
+
+    @pl.when(around.gives)
+    def _():
         over.wait_send()
         core.wait_recv()
 
     yield
 
 
-def attn_sum(part, full, unit, links, locals_, around, scratch):
-    own_terms, up_terms, down_terms, from_beyond, from_twin = scratch[:5]
-    sizes, first = unit
+def right_sum(summed, full, unit, links, locals_, around, scratch):
+    stretch = full.at[:, pl.ds(unit, WIDE)]
+    total, spare, from_beyond, from_twin = scratch
+    ring = right_ring()
+    load = locals_.of(summed.at[:, pl.ds(unit, WIDE)], total)
+    load.start()
+    yield
+    load.wait()
+    yield from across_and_back(
+        ring, total, spare, from_beyond, from_twin, stretch, 0, links, locals_, around
+    )
+
+
+def attn_sum(part, full, unit, links, locals_, around, held_terms, scratch):
+    own_terms, up_terms, down_terms = held_terms
+    from_beyond, from_twin = scratch[:2]
+    *sizes, first = unit
     ring = RowRing(*sizes)
-    y = around.y
-    quarter = lambda k: ring.quarter(part, turned(y, k), first)
+    quarter = lambda k: ring.quarter(part, turned(around.y, k), first)
     loads = [
         locals_.of(quarter(k), held) for k, held in ((1, up_terms), (3, down_terms), (0, own_terms))
     ]
-    ring.bind(links, around, scratch[5:], quarter(2), up_terms, down_terms, own_terms)
-    total = ring.total
-    over = links.to(total, from_beyond, around.beyond)
-    twin = links.to(total, from_twin, around.twin)
-    spread = RowSpread(ring, links, locals_, around, own_terms, full, first)
-    span = full.at[pl.ds(first, SIDE * ring.size)]
-    core = links.to(span, span, around.partner)
-
+    ring.bind(links, around, scratch[2:], quarter(2), up_terms, down_terms, own_terms)
+    ring.begin()
     for copy in loads:
         copy.start()
-    ring.begin()
     yield
     for copy in loads:
         copy.wait()
     ring.merge()
     yield
     ring.sum()
-
-    @pl.when(around.gives)
-    def _():
-        over.start()
-
-    yield
-
-    @pl.when(around.keeps)
-    def _():
-        over.wait_recv()
-        add_into(total, of(total), of(from_beyond), count=ring.size, step=ring.step)
-        twin.start()
-
-    yield
-
-    @pl.when(around.keeps)
-    def _():
-        twin.wait_recv()
-        add_into(own_terms, of(total), of(from_twin), count=ring.size, step=ring.step)
-        spread.begin()
-
-    yield
-
-    @pl.when(around.keeps)
-    def _():
-        spread.pass_on()
-
-    yield
-
-    @pl.when(around.keeps)
-    def _():
-        spread.end()
-        core.start()
-
-    yield
+    yield from across_and_back(
+        ring, ring.total, own_terms, from_beyond, from_twin, full, first, links, locals_, around
+    )
     ring.sent()
-
-    @pl.when(around.keeps)
-    def _():
-        twin.wait_send()
-        spread.sent()
-        core.wait_send()
-
-    @pl.when(around.gives)
-    def _():
-        over.wait_send()
-        core.wait_recv()
-
     yield
 
 
@@ -1107,40 +1293,146 @@
         copies = [links.to(slots.at[mine], slots.at[mine], peer) for peer in peers]
         for copy in copies:
             copy.start()
+        yield
         for copy in copies:
             copy.wait()
         total = slots[0]
         for slot in range(1, slots.shape[0]):
             total = total + slots[slot]
         values[...] = total
+    yield
 
 
 def z_device(x, y, z, core):
     return device(x, y, lax.div(z, 2), lax.rem(z, 2), core)
 
 
+def attention_back(
+    queries, keys, values, d_attended, row_info, segment_row, turns, qkv, d_keys, d_values, d_proj, d_normed, score_scale
+):
+    bf16, f32 = jnp.bfloat16, jnp.float32
+    keep, from_after, from_before = turns
+    lane = lax.broadcasted_iota(jnp.int32, (1, 128), 1)
+    d_keys[...] = jnp.zeros_like(d_keys)
+    d_values[...] = jnp.zeros_like(d_values)
+
+    def turned_back(grads, rows):
+        return (
+            grads * keep[rows, :]
+            + pltpu.roll(grads, 120, 1) * from_after[rows, :]
+            + pltpu.roll(grads, 8, 1) * from_before[rows, :]
+        )
+
+    for block in (3, 2, 1, 0):
+        first, end = block * PAIR, (block + 1) * PAIR
+        rows, before = pl.ds(first, PAIR), pl.ds(0, end)
+        info = row_info[rows, :]
+        places = first + lax.broadcasted_iota(jnp.int32, (PAIR, end), 0)
+        allowed = (info[:, 4:5] == segment_row[:, 0:end]) & (
+            lax.broadcasted_iota(jnp.int32, (PAIR, end), 1) <= places
+        )
+        info_lane = lax.broadcasted_iota(jnp.int32, info.shape, 1)
+
+        @pl.loop(0, 2)
+        def _(pair):
+            lanes = pl.ds(pl.multiple_of(pair * 128, 128), 128)
+            query, grad = queries[rows, lanes], d_attended[rows, lanes]
+            key, value = keys[before, lanes], values[before, lanes]
+            d_query = jnp.zeros((PAIR, 128), f32)
+            for head in range(2):
+                inside = (lane >= head * HEAD_DIM) & (lane < (head + 1) * HEAD_DIM)
+                query_h = jnp.where(inside, query, jnp.zeros_like(query))
+                grad_h = jnp.where(inside, grad, jnp.zeros_like(grad))
+                key_h = jnp.where(inside, key, jnp.zeros_like(key))
+                log_norm = jnp.sum(
+                    jnp.where(info_lane == pair * 2 + head, info, 0.0), axis=1, keepdims=True
+                )
+                scores = jnp.where(allowed, matmul(query_h, key, NT) * score_scale, -1e30)
+                prob = jnp.exp(scores - log_norm)
+                d_prob = matmul(grad_h, value, NT)
+                row_dots = jnp.sum(prob * d_prob, axis=1, keepdims=True)
+                d_score = (prob * (d_prob - row_dots)).astype(bf16)
+                d_query = d_query + matmul(d_score, key_h, NN)
+                d_keys[before, lanes] += matmul(d_score, query_h, TN)
+                d_values[before, lanes] += matmul(prob.astype(bf16), grad_h, TN)
+            d_proj[rows, lanes] = turned_back(d_query * score_scale, rows).astype(bf16)
+            key_lanes = pl.ds(pl.multiple_of(256 + pair * 128, 128), 128)
+            d_proj[rows, key_lanes] = turned_back(d_keys[rows, lanes] * score_scale, rows).astype(bf16)
+            value_lanes = pl.ds(pl.multiple_of(512 + pair * 128, 128), 128)
+            d_proj[rows, value_lanes] = d_values[rows, lanes].astype(bf16)
+
+        @pl.loop(0, 2048, step=512)
+        def _(column):
+            columns = pl.ds(pl.multiple_of(column, 512), 512)
+            total = matmul(d_proj[rows, 0:256], qkv[0, columns, :], NT)
+            total = total + matmul(d_proj[rows, 256:512], qkv[1, columns, :], NT)
+            total = total + matmul(d_proj[rows, 512:768], qkv[2, columns, :], NT)
+            d_normed[rows, columns] = total.astype(bf16)
+
+        yield
+
+
+ORDER = (
+    "l3", "l0", "f", "l2", "r0", "a2", "r1", "l0", "l1", "f", "l1", "f", "l0", "f",
+    "l0", "l1", "r0", "a2", "f", "l0", "l1", "l2", "f", "l2", "l3", "l1", "l0", "r1",
+    "f", "a1", "l3", "a0", "r0", "f", "l0", "l2", "a2", "l1", "r1", "f", "a1", "f",
+    "a0", "l3", "l2", "l1", "a2", "r0", "a1", "l0", "a1", "a0", "l3", "r1", "l2", "l0",
+    "r0", "f", "l3", "a0", "e", "l1", "f", "r1", "a2", "l2", "r0", "e", "l1", "a1",
+    "l3", "r0", "e", "r1", "a0", "a2", "r1", "l2", "a1", "l3", "e", "a0", "a2", "a1",
+    "l2", "a2", "a0", "a1", "l2", "l3", "a0", "e", "l3",
+)
+
+
 def last_kernel(
-    part,
+    queries_in,
+    keys_in,
+    values_in,
+    d_attended_in,
+    row_info,
+    segment_row,
+    keep,
+    from_after,
+    from_before,
+    qkv,
+    normed,
     tokens,
     d_mid,
     gain,
     ffn_part,
     mid,
-    ff_part,
-    qkv_part,
+    gate_part,
+    gate_beyond,
+    up_part,
+    down_sum,
     out_part,
-    norm_part,
+    gain_part,
+    shift_part,
     mixed,
     input_grad,
-    ff_full,
+    gate_full,
+    up_full,
+    down_full,
     qkv_full,
     out_full,
     sums,
+    up_beyond,
+    qkv_part,
+    queries,
+    keys,
+    values,
+    d_attended,
+    d_keys,
+    d_values,
+    d_proj,
+    d_normed,
+    normed_tile,
+    grad_tile,
     d_in,
     mixed_rows,
-    own_rows,
     ffn_rows,
-    own_sems,
+    normed_sems,
+    grad_sems,
+    ready,
     sends,
     arrives,
     local_sems,
@@ -1150,42 +1442,87 @@
     by_z,
     *scratch,
 ):
+    bf16 = jnp.bfloat16
     place = here()
     x, y, z_hi, z_lo, core = place
     z = z_hi * 2 + z_lo
     around = Around(place)
     links, locals_ = Links(sends, arrives), Locals(local_sems)
     swap_with = device(x, y, core, z_lo, z_hi)
-    terms, ffn_terms = ByRow(part, place), ByStep(ffn_part)
-    scatter = Scatter(
-        lambda step, rows: own_rows[step, rows, :], lambda step: terms.at(step, 1), place, scratch[:7]
-    )
+    terms, ffn_terms = ByRow(d_normed, place), ByStep(ffn_part)
+
+    def own_terms(step, rows):
+        first = (core * SIDE + turned(x, SIDE - step)) * BLOCK
+        return d_normed[pl.ds(pl.multiple_of(first + rows.start, 16), rows.size), :]
+
     scatter_ffn = Scatter(
-        lambda step, rows: ffn_rows[step, rows, :], lambda step: ffn_terms.at(step, 1), place, scratch[7:14]
-    )
-    scratch = scratch[14:]
-    ff_units, attn_units = [], []
-    ff_own, scratch = scratch[:2], scratch[2:]
-    for index in range(2048 // WIDE):
-        mine = ff_own[index % 2]
-        ff_units.append(ff_sum(ff_part, ff_full, index * WIDE, links, locals_, around, mine, scratch[:7]))
-        scratch = scratch[7:]
+        lambda step, rows: ffn_rows[step, rows, :], lambda step: ffn_terms.at(step, 1), place, scratch[:7]
+    )
+    scatter = Scatter(own_terms, lambda step: terms.at(step, 1), place, scratch[:3] + scratch[7:11])
+    scratch = scratch[11:]
+    units = {}
+    mine, *got = scratch[:3]
+    scratch = scratch[3:]
+    refs_of = ((gate_part, gate_beyond, gate_full), (up_part, up_beyond, up_full))
+    for index in range(4):
+        units[f"l{index}"] = left_sum(
+            *refs_of[index // 2],
+            (index % 2) * WIDE,
+            index > 1,
+            links,
+            locals_,
+            around,
+            mine,
+            got[index % 2],
+            scratch[:6],
+        )
+        scratch = scratch[6:]
+    for index in range(2):
+        units[f"r{index}"] = right_sum(down_sum, down_full, index * WIDE, links, locals_, around, scratch[:4])
+        scratch = scratch[4:]
+    out_terms, scratch = scratch[:3], scratch[3:]
+    held_terms = (
+        [ref.at[pl.ds(0, 768)] for ref in (queries, keys, values)],
+        [d_proj.at[pl.ds(0, 768), pl.ds(256 * index, 256)] for index in range(3)],
+        out_terms,
+    )
     for index, unit in enumerate(ATTN_UNITS):
         refs = (out_part, out_full) if index == 2 else (qkv_part, qkv_full)
-        attn_units.append(attn_sum(*refs, unit, links, locals_, around, scratch[:10]))
-        scratch = scratch[10:]
-    load_own = [locals_.of(terms.at(step, 0), own_rows.at[step]) for step in range(SIDE)]
+        units[f"a{index}"] = attn_sum(*refs, unit, links, locals_, around, held_terms[index], scratch[:7])
+        scratch = scratch[7:]
+    units["e"] = sum_everywhere(sums, (by_x, by_core, by_y, by_z), links, place)
+    units["t"] = attention_back(
+        queries,
+        keys,
+        values,
+        d_attended,
+        row_info,
+        segment_row,
+        (keep, from_after, from_before),
+        qkv,
+        d_keys,
+        d_values,
+        d_proj,
+        d_normed,
+        HEAD_DIM ** (-0.5),
+    )
+
+    def on(*names):
+        for name in names:
+            next(units[name])
+
+    load_attn = [
+        locals_.of(source, held)
+        for source, held in (
+            (queries_in, queries),
+            (keys_in, keys),
+            (values_in, values),
+            (d_attended_in, d_attended),
+        )
+    ]
     load_ffn = [locals_.of(ffn_terms.at(step, 0), ffn_rows.at[step]) for step in range(SIDE)]
     swaps = [links.to(mixed_rows, mixed, swap_with), links.to(d_in, input_grad, swap_with)]
     stays = [locals_.of(mixed_rows, mixed), locals_.of(d_in, input_grad)]
-
-    def ff(*indices):
-        for index in indices:
-            next(ff_units[index])
-
-    def attn(*indices):
-        for index in indices:
-            next(attn_units[index])
 
     def give(index):
         @pl.when(around.gives)
@@ -1196,8 +1533,52 @@
         def _():
             stays[index].start()
 
-    for copy in load_own + load_ffn:
+    def load_normed(chunk):
+        columns = pl.ds(pl.multiple_of(chunk * TILE, TILE), TILE)
+        slot = lax.rem(chunk, 2)
+        return pltpu.make_async_copy(normed.at[:, columns], normed_tile.at[slot], normed_sems.at[slot])
+
+    def store_grad(chunk):
+        slot = lax.rem(chunk, 2)
+        return [
+            pltpu.make_async_copy(
+                grad_tile.at[slot, pl.ds(channel * TILE, TILE)],
+                qkv_part.at[pl.ds(pl.multiple_of(channel * 2048 + chunk * TILE, TILE), TILE)],
+                grad_sems.at[slot, channel],
+            )
+            for channel in range(3)
+        ]
+
+    def qkv_grads(first, end):
+        @pl.loop(first, end)
+        def _(chunk):
+            slot = lax.rem(chunk, 2)
+            load_normed(chunk).wait()
+
+            @pl.when(chunk + 1 < 8)
+            def _():
+                load_normed(chunk + 1).start()
+
+            @pl.when(chunk > first + 1)
+            def _():
+                for copy in store_grad(chunk):
+                    copy.wait()
+
+            grads = matmul(normed_tile[slot], d_proj[...], TN).astype(bf16)
+            for channel in range(3):
+                grad_tile[slot, channel * TILE : (channel + 1) * TILE, :] = grads[
+                    :, channel * TILE : (channel + 1) * TILE
+                ]
+            for copy in store_grad(chunk):
+                copy.start()
+
+        for chunk in (end - 2, end - 1):
+            for copy in store_grad(jnp.int32(chunk)):
+                copy.wait()
+
+    for copy in load_ffn + load_attn:
         copy.start()
+    load_normed(jnp.int32(0)).start()
     peers = line_peers(place) + [device(x, turned(y, k), z_hi, z_lo, core) for k in (1, 2, 3)]
     peers += [z_device(x, y, turned(z, k), core) for k in (1, 2, 3)]
 
@@ -1209,23 +1590,15 @@
     def _():
         greet(peers)
 
-    for step in (2, 1, 3, 0):
-        scatter.across[step].start()
-    ff(0, 1)
-    attn(0, 1, 2)
-    for copy in load_own + load_ffn:
-        copy.wait()
-    for step in (2, 1, 3):
-        scatter.merge(step)
-    for step in (2, 1, 3, 0):
-        scatter_ffn.across[step].start()
-    attn(0, 1, 2)
-    for step in (2, 1, 3):
-        scatter_ffn.merge(step)
-    ff(0, 2)
-    attn(0, 1, 2)
-    scatter.finish()
-    sums[...] = norm_part[...]
+    def mix(rows):
+        mixed_rows[rows, :] = (mid[rows, :] + scatter_ffn.rows(rows)).astype(bf16)
+
+    def bias_grads():
+        width = d_proj.shape[1] // 3
+        mine_columns = pl.ds(pl.multiple_of((core * SIDE + x) * width, width), width)
+        for channel in range(3):
+            grads = d_proj[:, channel * width : (channel + 1) * width].astype(jnp.float32)
+            sums[4 + channel : 5 + channel, mine_columns] = jnp.sum(grads, axis=0, keepdims=True)
 
     def back(rows):
         grad = scatter.rows(rows)
@@ -1240,27 +1613,55 @@
             - unit * jnp.mean(scaled * unit, axis=-1, keepdims=True)
         )
 
-    tile_rows(back)
-    give(1)
-    ff(0)
-    attn(0, 1, 2)
-    ff(0, 1, 3)
-    attn(0, 1, 2)
-    scatter_ffn.finish()
-
-    def mix(rows):
-        mixed_rows[rows, :] = (mid[rows, :] + scatter_ffn.rows(rows)).astype(jnp.bfloat16)
-
-    tile_rows(mix)
-    give(0)
-    ff(0, 1, 0)
-    attn(0, 1, 2)
-    sum_everywhere(sums, (by_x, by_core, by_y, by_z), links, place)
-    ff(1, 2, 0, 1, 2)
-    attn(0, 1, 2)
-    ff(0, 1, 2, 3, 1, 2, 3, 2, 1, 3, 2, 3, 2, 3, 3, 3)
-    attn(0, 1, 2)
-    ff(0, 1, 2, 3)
+    def foreground():
+        for step in (2, 1, 3, 0):
+            scatter_ffn.across[step].start()
+        yield
+        for copy in load_ffn:
+            copy.wait()
+        for step in (2, 1, 3):
+            scatter_ffn.merge(step)
+        yield
+        for copy in load_attn:
+            copy.wait()
+        sums[...] = jnp.zeros_like(sums)
+        sums[2:3, :] = gain_part[...]
+        sums[3:4, :] = shift_part[...]
+        on("t")
+        yield
+        on("t")
+        yield
+        on("t")
+        yield
+        on("t")
+        yield
+        qkv_grads(0, 8)
+        bias_grads()
+        yield
+        scatter_ffn.finish()
+        tile_rows(mix)
+        for peer in line_peers(place):
+            pl.semaphore_signal(ready, inc=1, device_id=peer, device_id_type=MESH)
+        give(0)
+        yield
+        pl.semaphore_wait(ready, SIDE)
+        for step in (2, 1, 3, 0):
+            scatter.across[step].start()
+        yield
+        for step in (2, 1, 3):
+            scatter.merge(step)
+        yield
+        scatter.finish()
+        tile_rows(back)
+        yield
+        give(1)
+        yield
+
+    units["f"] = foreground()
+    on(*ORDER)
+    for unit in units.values():
+        for _ in unit:
+            pass
 
     @pl.when(around.gives)
     def _():
@@ -1316,40 +1717,13 @@
     frequency = jnp.power(
         jnp.float32(10000.0), -2.0 * jnp.arange(half_rot, dtype=jnp.float32) / ROT
     )
+    lane = jnp.arange(128) % HEAD_DIM
+    frequency = jnp.where(lane < ROT, jnp.tile(frequency, 128 // half_rot), 0.0)
     angles = position.astype(jnp.float32)[:, None] * frequency[None, :]
-    return (jnp.cos(angles)[:, None, :], jnp.sin(angles)[:, None, :])
-
-
-def rotate(values, cosine, sine_table):
-    half_rot = ROT // 2
-    first_half = values[..., :half_rot]
-    second_half = values[..., half_rot:ROT]
-    return jnp.concatenate(
-        [
-            first_half * cosine - second_half * sine_table,
-            second_half * cosine + first_half * sine_table,
-            values[..., ROT:],
-        ],
-        axis=-1,
-    )
-
-
-def contract_rows(left_rows, right_rows):
-    return lax.dot_general(
-        left_rows, right_rows, (((0,), (0,)), ((), ())), preferred_element_type=jnp.float32
-    )
-
-
-def times_transposed(left_rows, right_rows):
-    return lax.dot_general(
-        left_rows, right_rows, (((1,), (1,)), ((), ())), preferred_element_type=jnp.float32
-    )
-
-
-def block_mask(segment, row_ids, begin_row, end_row):
-    return (segment[begin_row:end_row, None] == segment[None, :end_row]) & (
-        row_ids[None, :end_row] <= row_ids[begin_row:end_row, None]
-    )
+    sine = jnp.sin(angles)
+    from_after = jnp.where(lane < half_rot, sine, 0.0)
+    from_before = jnp.where(lane >= half_rot, -sine, 0.0)
+    return (jnp.cos(angles), from_after, from_before)
 
 
 def body(
@@ -1374,81 +1748,67 @@
     local_heads = qkv_weight.shape[2] // HEAD_DIM
     member = (y * 2 + z_lo) * 2 + z_hi
     shard = core * SIDE + x
-    score_scale = HEAD_DIM ** (-0.5)
     segment, position, live_rows = member_layout(seq_length, seq_owner, member, row_total)
-    row_ids = jnp.arange(row_total, dtype=jnp.int32)
     live = lax.dynamic_slice_in_dim(live_rows, shard * BLOCK, BLOCK, 0)[:, None].astype(f32)
-    bias = permute(qkv_bias, swap_rows)
-
-    dma = pltpu.SemaphoreType.DMA
-    tokens_here, cot, normed1, cot_rows, qkv, out, down = call(
+    segments = segment.astype(f32)[:, None]
+    segment_row = segment.astype(f32)[None]
+    keep, from_after, from_before = rotary_tables(position)
+    flat = (row_total, qkv_weight.shape[2])
+    dma, vmem = pltpu.SemaphoreType.DMA, pltpu.VMEM
+    tokens_here, cot, normed1, cot_rows, attn_part, qkv, out, down, queries, keys, values, attended, row_info = call(
         first_kernel,
         1,
-        (tokens, out_grad, live, ln1_gain[None], ln1_bias[None], qkv_weight, out_weight, down_weight),
-        [ANY, ANY, HELD, HELD, HELD, ANY, ANY, ANY],
+        (
+            tokens,
+            out_grad,
+            live,
+            ln1_gain[None],
+            ln1_bias[None],
+            qkv_weight,
+            out_weight,
+            down_weight,
+            qkv_bias,
+            segments,
+            segment_row,
+            keep,
+            from_after,
+            from_before,
+        ),
+        [ANY, ANY, HELD, HELD, HELD, ANY, ANY, ANY] + [HELD] * 6,
         [
             (rows_here, bf16),
             (rows_here, bf16),
             (rows_all, bf16),
             (rows_all, bf16),
+            (rows_all, bf16),
             (qkv_weight.shape, bf16),
             (out_weight.shape, bf16),
             (down_weight.shape, bf16),
+            (flat, bf16),
+            (flat, bf16),
+            (flat, bf16),
+            (flat, bf16),
+            ((row_total, 128), f32),
         ],
-        [ANY] * 4 + [HELD] * 3,
-        (pltpu.VMEM(rows_here, bf16),) * 4
-        + (dma((2,)), dma((2,)), dma((6,)))
+        [ANY] * 5 + [HELD] * 8,
+        (
+            vmem(rows_here, bf16),
+            vmem(rows_here, bf16),
+            vmem(rows_here, bf16),
+            vmem(qkv_bias.shape, f32),
+            vmem(rows_all, bf16),
+            vmem((PAIR, 2048), bf16),
+            dma((3,)),
+            dma((3,)),
+            dma((16,)),
+        )
         + Gather.scratch * 2
         + fetch_scratch(3),
     )
 
-    cosine, sine_table = rotary_tables(position)
-    projected = [
-        jnp.dot(normed1, qkv[channel], preferred_element_type=jnp.float32) + bias[channel]
-        for channel in range(3)
-    ]
-    queries = rotate(
-        projected[0].reshape(row_total, local_heads, HEAD_DIM), cosine, sine_table
-    ).astype(bf16)
-    keys_low = rotate(
-        projected[1].reshape(row_total, local_heads, HEAD_DIM), cosine, sine_table
-    ).astype(bf16)
-    values_low = projected[2].reshape(row_total, local_heads, HEAD_DIM).astype(bf16)
-    block_size = min(512, row_total)
-    block_count = row_total // block_size
-    out_blocks = []
-    log_norms = []
-    for block_index in range(block_count):
-        begin_row = block_index * block_size
-        end_row = begin_row + block_size
-        allowed = block_mask(segment, row_ids, begin_row, end_row)
-        scores = (
-            jnp.einsum(
-                "qhd,khd->hqk",
-                queries[begin_row:end_row],
-                keys_low[:end_row],
-                preferred_element_type=jnp.float32,
-            )
-            * score_scale
-        )
-        scores = jnp.where(allowed[None], scores, -1e30)
-        row_max = jnp.max(scores, axis=-1, keepdims=True)
-        exp_scores = jnp.exp(scores - row_max)
-        exp_sum = jnp.sum(exp_scores, axis=-1, keepdims=True)
-        attn_prob = (exp_scores / exp_sum).astype(bf16)
-        out_blocks.append(
-            jnp.einsum(
-                "hqk,khd->qhd", attn_prob, values_low[:end_row], preferred_element_type=jnp.float32
-            ).astype(bf16)
-        )
-        log_norms.append(row_max + jnp.log(exp_sum))
-    attended = jnp.concatenate(out_blocks, axis=0).reshape(row_total, local_heads * HEAD_DIM)
-    attn_part = jnp.dot(attended, out, preferred_element_type=jnp.float32).astype(bf16)
-
     gate_up_t = jnp.swapaxes(gate_up_weight, 1, 2)
     ff = down_weight.shape[0]
-    vmem = pltpu.VMEM
-    mid_stream, d_mid, gain2_part, shift2_part, ffn_grad, ffn_part, d_attended, out_grad = call(
+    mid_stream, d_mid, gain2_part, shift2_part, *ff_parts, ffn_part, d_attended, out_grad = call(
         middle_kernel,
         2,
         (
@@ -1469,12 +1829,16 @@
             (rows_here, f32),
             ((1, 2048), f32),
             ((1, 2048), f32),
-            ((3, ff, 2048), bf16),
+            (down_weight.shape, bf16),
+            (down_weight.shape, bf16),
+            (down_weight.shape, bf16),
+            (down_weight.shape, bf16),
+            ((ff // SIDE, 2048), bf16),
             (rows_all, bf16),
             (attended.shape, bf16),
             (out.shape, bf16),
         ],
-        [HELD, HELD, HELD, HELD, ANY, ANY, HELD, HELD],
+        [HELD] * 4 + [ANY] * 6 + [HELD, HELD],
         (
             vmem((2, ff, 2048), bf16),
             vmem((ff, 2048), bf16),
@@ -1490,7 +1854,7 @@
             vmem((SIDE, BLOCK, 2048), bf16),
             vmem((SIDE, BLOCK, 2048), bf16),
             vmem((PAIR, 2048), bf16),
-            vmem((2, ff, 512), bf16),
+            vmem((2, ff, TILE), bf16),
             dma((8,)),
             dma((8,)),
             dma((6,)),
@@ -1500,113 +1864,91 @@
         + Scatter.scratch
         + Scatter.sems
         + Gather.scratch * 2
-        + fetch_scratch(2),
-    )
-
-    d_attended = d_attended.reshape(row_total, local_heads, HEAD_DIM)
-    query_grads = []
-    d_key = jnp.zeros((row_total, local_heads, HEAD_DIM), f32)
-    d_value = jnp.zeros((row_total, local_heads, HEAD_DIM), f32)
-    for block_index in range(block_count):
-        begin_row = block_index * block_size
-        end_row = begin_row + block_size
-        allowed = block_mask(segment, row_ids, begin_row, end_row)
-        query_block = queries[begin_row:end_row]
-        key_block = keys_low[:end_row]
-        grad_block = d_attended[begin_row:end_row]
-        scores = (
-            jnp.einsum("qhd,khd->hqk", query_block, key_block, preferred_element_type=jnp.float32)
-            * score_scale
-        )
-        scores = jnp.where(allowed[None], scores, -1e30)
-        attn_full = jnp.exp(scores - log_norms[block_index])
-        attn_prob = attn_full.astype(bf16)
-        d_prob = jnp.einsum(
-            "qhd,khd->hqk", grad_block, values_low[:end_row], preferred_element_type=jnp.float32
-        )
-        row_dots = jnp.sum(attn_full * d_prob, axis=-1, keepdims=True)
-        d_score = (attn_full * (d_prob - row_dots)).astype(bf16)
-        query_grads.append(
-            jnp.einsum("hqk,khd->qhd", d_score, key_block, preferred_element_type=jnp.float32)
-            * score_scale
-        )
-        d_key = d_key.at[:end_row].add(
-            jnp.einsum("hqk,qhd->khd", d_score, query_block, preferred_element_type=jnp.float32)
-            * score_scale
-        )
-        d_value = d_value.at[:end_row].add(
-            jnp.einsum("hqk,qhd->khd", attn_prob, grad_block, preferred_element_type=jnp.float32)
-        )
-    d_query = jnp.concatenate(query_grads, axis=0)
-    d_proj = [
-        rotate(d_query, cosine, -sine_table).reshape(row_total, -1).astype(bf16),
-        rotate(d_key, cosine, -sine_table).reshape(row_total, -1).astype(bf16),
-        d_value.reshape(row_total, -1).astype(bf16),
-    ]
-    summed = times_transposed(d_proj[0], qkv[0])
-    summed = summed + times_transposed(d_proj[1], qkv[1])
-    d_norm_part = (summed + times_transposed(d_proj[2], qkv[2])).astype(bf16)
-
-    qkv_part = jnp.concatenate(
-        [contract_rows(normed1, d_proj[channel]).astype(bf16) for channel in range(3)]
-    )
-    bias_part = jnp.stack([jnp.sum(d.astype(f32), axis=0) for d in d_proj])
-    bias_part = lax.dynamic_update_slice_in_dim(
-        jnp.zeros((3, 2048), f32), bias_part, shard * bias_part.shape[1], 1
-    )
-    norm_part = jnp.concatenate(
-        [jnp.zeros((2, 2048), f32), gain2_part, shift2_part, bias_part, jnp.zeros((1, 2048), f32)]
-    )
-    ff_part = ffn_grad.reshape(3 * ff, 2048)
-    unit_count = 2048 // WIDE
+        + fetch_scratch(2)
+        + (dma((5,)), dma((5,)))
+        + (vmem((ff // SIDE, 2048), bf16),) * 3
+        + RowRing(*DOWN_RING).scratch(),
+    )
+
+    gate_part, up_part, _, gate_beyond, down_sum = ff_parts
     small = (8, 2048)
-    mixed, input_grad, ff_full, qkv_full, out_full, sums = call(
+    qkv_rows = (3 * 2048, flat[1])
+    mixed, input_grad, gate_full, up_full, down_full, qkv_full, out_full, sums, _, _ = call(
         last_kernel,
         4,
         (
-            d_norm_part,
+            queries,
+            keys,
+            values,
+            d_attended,
+            row_info,
+            segment_row,
+            keep,
+            from_after,
+            from_before,
+            qkv,
+            normed1,
             tokens_here,
             d_mid,
             ln1_gain[None],
             ffn_part,
             mid_stream,
-            ff_part,
-            qkv_part,
+            gate_part,
+            gate_beyond,
+            up_part,
+            down_sum,
             out_grad,
-            norm_part,
+            gain2_part,
+            shift2_part,
         ),
-        [ANY, HELD, HELD, HELD, ANY, HELD, ANY, ANY, ANY, HELD],
+        [ANY] * 4 + [HELD] * 6 + [ANY] + [HELD] * 3 + [ANY, HELD] + [ANY] * 5 + [HELD] * 2,
         [
             (rows_here, bf16),
             (rows_here, f32),
-            (ff_part.shape, bf16),
-            (qkv_part.shape, bf16),
+            (down_weight.shape, bf16),
+            (down_weight.shape, bf16),
+            (down_weight.shape, bf16),
+            (qkv_rows, bf16),
             (out.shape, bf16),
             (small, f32),
+            (down_weight.shape, bf16),
+            (qkv_rows, bf16),
         ],
-        [ANY, ANY, ANY, ANY, ANY, HELD],
+        [ANY] * 7 + [HELD] + [ANY] * 2,
         (
+            vmem(flat, bf16),
+            vmem(flat, bf16),
+            vmem(flat, bf16),
+            vmem(flat, bf16),
+            vmem(flat, f32),
+            vmem(flat, f32),
+            vmem((row_total, 3 * flat[1]), bf16),
+            vmem(rows_all, bf16),
+            vmem((2, row_total, TILE), bf16),
+            vmem((2, 3 * TILE, flat[1]), bf16),
             vmem(rows_here, f32),
             vmem(rows_here, bf16),
             vmem((SIDE, BLOCK, 2048), bf16),
-            vmem((SIDE, BLOCK, 2048), bf16),
-            dma((8,)),
-            dma((FF_LINKS * unit_count + ATTN_LINKS * 3 + 12,)),
-            dma((FF_LINKS * unit_count + ATTN_LINKS * 3 + 12,)),
-            dma((2 * unit_count + 4 * 3 + 10,)),
+            dma((2,)),
+            dma((2, 3)),
+            pltpu.SemaphoreType.REGULAR,
+            dma((LINK_COUNT,)),
+            dma((LINK_COUNT,)),
+            dma((LOCAL_COUNT,)),
             vmem((SIDE, *small), f32),
             vmem((2, *small), f32),
             vmem((SIDE, *small), f32),
             vmem((SIDE, *small), f32),
         )
-        + Scatter.scratch * 2
-        + (vmem((3 * ff, WIDE), bf16),) * 2
-        + ff_scratch(3 * ff) * unit_count
-        + sum((attn_scratch(unit) for unit in ATTN_UNITS), ()),
-    )
-    ff_grads = ff_full.reshape(3, ff, 2048)
-    gate_up_grad = jnp.swapaxes(ff_grads[:2], 1, 2).astype(f32)
-    down_grad = ff_grads[2].astype(f32)
+        + Scatter.scratch
+        + Scatter.sems
+        + left_scratch(ff, 4)
+        + right_scratch(2)
+        + (vmem((64, 2048), bf16),) * 3
+        + attn_scratch(),
+    )
+    gate_up_grad = jnp.swapaxes(jnp.stack([gate_full.astype(f32), up_full.astype(f32)]), 1, 2)
+    down_grad = down_full.astype(f32)
     qkv_weight_grad = qkv_full.reshape(3, 2048, -1).astype(f32)
     out_weight_grad = out_full.astype(f32)
     width = qkv_bias.shape[1]

time: 540 us -> 365 us (0.68); the launches traced: 530 us -> 365 us
  Pallas kernels: 416 us -> 334 us
  matrix products: 56.8 us -> 0 us
  local copies, waits for them, and re-layouts: 16.8 us -> 7.48 us
  other arithmetic: 31.4 us -> 22.1 us
  starting transfers between devices: 6.89 us -> 0 us
    pallas_call x3, Pallas kernels: 416 us -> 334 us  [call(): pl.pallas_call(kernel, out_shape=[jax.ShapeDtypeStruct(shape, kind) for s...]
    dot_general x22 -> x0, matrix products: 56.8 us -> none  [the longest x3 18.8 us: times_transposed(): lax.dot_general(left_rows, right_rows, (((1,), (1,)), ((), ())), preferre...]
    convert_element_type x4 -> x3, other arithmetic: 14.1 us -> 4.8 us  [the longest x1 3.31 us: body(): down_grad = down_full.astype(f32)]
    unnamed x78 -> x14, local copies, waits for them, and re-layouts: 11.3 us -> 3 us
    ppermute x1 -> x0, starting transfers between devices: 6.89 us -> none  [permute(): return lax.ppermute(array, AXES, pairs(move))]
  transfers between devices with their start and end apart: 1 -> 0, of which waited for: 0 -> 0; matrix products, arithmetic and copies ran while one was open for 1% -> 0% of each run, Pallas kernels for 12% -> 0%
where the time goes in v3:
time: 365 us
  Pallas kernels  334 us (92%)
  other arithmetic  22.1 us (6%)
  local copies, waits for them, and re-layouts  7.48 us (2%)
    pallas_call x3, Pallas kernels, call(): pl.pallas_call(kernel, out_shape=[jax.ShapeDtypeStruct(shape, kind) for s...  334 us

profile of v3, /device:TPU:1, one launch (start us, length us, event | category | flops | bytes accessed | tf_op | source)
XLA Modules:
  0.0 364.8 jit_solution(731446660944807895)
XLA Ops:
  0.7 0.7 compare_convert_fusion
  1.3 0.8 select_reduce_fusion
  2.2 0.7 add.78
  2.9 0.1 tile.10
  2.9 0.2 multiply_reduce_fusion
  3.2 0.1 convert_bitcast_fusion.1
  3.2 0.6 add_convert_fusion.1.segment_row
  3.8 0.7 copy.34.live
  4.6 0.2 copy.32
  4.8 0.2 copy.33
  5.0 0.9 add_convert_fusion.segments
  5.9 3.2 fusion.2
  9.1 76.8 %shard_map.212 = (bf16[128,2048]{1,0:T(8,128)(2,1)}, bf16[128,2048]{1,0:T(8,128)(2,1)}, bf16[1024,2048]{1,0:T(8,128)(2,1)}, bf16[1024,2048]{1,0:T(8,128)(2,1)}, ...) custom-call(bf16[128,2048]{1,0:T(8,128)(2,1)} %tokens.1, ...), custom_call_target="tpu_custom_call" | custom-call | tf_op jit(solution)/shard_map/pallas_call | solution.py:1682
  85.9 123.2 %shard_map.213 = (f32[128,2048]{1,0:T(8,128)}, f32[128,2048]{1,0:T(8,128)}, f32[1,2048]{1,0:T(1,128)}, f32[1,2048]{1,0:T(1,128)}, bf16[704,2048]{1,0:T(8,128)(2,...) custom-call(bf16[1024,2048]{1,0:T(8,128)(2,1)} %get-tuple-element.46, ...), custom_call_target="tpu_custom_call" | custom-call | tf_op jit(solution)/shard_map/pallas_call | solution.py:1682
  209.1 134.4 %shard_map.214 = (bf16[128,2048]{1,0:T(8,128)(2,1)}, f32[128,2048]{1,0:T(8,128)}, bf16[704,2048]{1,0:T(8,128)(2,1)}, bf16[704,2048]{1,0:T(8,128)(2,1)}, bf16[704...) custom-call(bf16[1024,256]{1,0:T(8,128)(2,1)} %get-tuple-element.43., ...), custom_call_target="tpu_custom_call" | custom-call | tf_op jit(solution)/shard_map/pallas_call | solution.py:1682
  343.6 0.0 copy-start.1
  343.6 1.0 slice.17
  344.6 1.6 fusion.4
  346.2 0.6 constant_dynamic-slice_fusion
  346.8 2.8 convert_element_type.61
  349.6 0.0 copy-done.1
  349.6 0.0 copy-start
  349.6 3.3 convert_element_type.62
  352.9 0.0 copy-done
  352.9 0.0 copy-start.2
  352.9 0.0 copy-start.3
  352.9 3.7 %convert.5 = f32[3,2048,256]{2,1,0:T(8,128)} convert(bf16[3,2048,256]{2,1,0:T(8,128)(2,1)S(1)} %bitcast.22) | non-fusion elementwise | flops 1572864 | bytes 9437184 | tf_op jit(solution)/shard_map/convert_element_type | solution.py:1952
  356.6 0.0 copy-done.2
  356.6 1.2 copy-done.3
  357.8 0.0 copy-start.5
  357.8 0.0 copy-start.4
  357.8 5.2 %convert_bitcast_fusion = f32[2,2048,704]{1,2,0:T(8,128)} fusion(bf16[1,704,2048]{2,1,0:T(8,128)(2,1)S(1)} %bitcast.24, bf16[1,704,2048]{2,1,0:T(8,128)(2,1)S(1)} %bitcast.23), kind=kLoop, calls=%fused_computation | loop fusion | flops 5767168 | bytes 17301504 | tf_op jit(solution)/shard_map/transpose | solution.py:1950
  363.0 0.0 copy-done.5
  363.0 0.8 copy.37
  363.8 0.0 copy-done.4
  363.8 1.0 copy.38
  (6 shorter events, 0.0 us)
Async XLA Ops:
  343.6 6.0 %copy-start.1 = (bf16[704,2048]{1,0:T(8,128)(2,1)S(1)}, bf16[704,2048]{1,0:T(8,128)(2,1)}, u32[]{:S(2)}) copy-start(bf16[704,2048]{1,0:T(8,128)(2,1)} %get-tuple-element.74) | copy-start | bytes 8650756
  349.6 3.3 copy-start
  352.9 3.7 %copy-start.2 = (bf16[704,2048]{1,0:T(8,128)(2,1)S(1)}, bf16[704,2048]{1,0:T(8,128)(2,1)}, u32[]{:S(2)}) copy-start(bf16[704,2048]{1,0:T(8,128)(2,1)} %get-tuple-element.72) | copy-start | bytes 8650756
  352.9 5.0 %copy-start.3 = (bf16[704,2048]{1,0:T(8,128)(2,1)S(1)}, bf16[704,2048]{1,0:T(8,128)(2,1)}, u32[]{:S(2)}) copy-start(bf16[704,2048]{1,0:T(8,128)(2,1)} %get-tuple-element.73) | copy-start | bytes 8650756
  357.8 5.2 %copy-start.5 = (bf16[128,2048]{1,0:T(8,128)(2,1)S(1)}, bf16[128,2048]{1,0:T(8,128)(2,1)}, u32[]{:S(2)}) copy-start(bf16[128,2048]{1,0:T(8,128)(2,1)} %get-tuple-element.98) | copy-start | bytes 1572868
  357.8 6.0 %copy-start.4 = (f32[128,2048]{1,0:T(8,128)S(1)}, f32[128,2048]{1,0:T(8,128)}, u32[]{:S(2)}) copy-start(f32[128,2048]{1,0:T(8,128)} %get-tuple-element.99) | copy-start | bytes 3145732

commit v4 on v3

--- a/solution.py
+++ b/solution.py
@@ -394,6 +394,9 @@
     qkv,
     out,
     down,
+    gate_up,
+    gain_mid,
+    shift_mid,
     bias,
     segments,
     segment_row,
@@ -404,10 +407,12 @@
     cot_here,
     normed_full,
     cot_full,
-    part,
+    mid,
+    normed_mid,
     qkv_here,
     out_here,
     down_here,
+    gate_up_here,
     queries,
     keys,
     values,
@@ -418,7 +423,7 @@
     cot_buf,
     bias_buf,
     normed,
-    part_tile,
+    part,
     swap_send,
     swap_arrive,
     own_sems,
@@ -429,13 +434,26 @@
     x, y, z_hi, z_lo, core = place
     lacking = core != z_hi
     swap_with = device(x, y, core, z_lo, z_hi)
-    fetch_sems = sems[8:]
+    fetch_sems = sems[8:11]
     fetches = [
         Fetch(weight, filled, cut, place, fetch_sems, index)
         for index, (weight, filled, cut) in enumerate(
-            [(qkv, qkv_here, QKV_CUT), (out, out_here, OUT_CUT), (down, down_here, FF_CUT)]
+            [
+                (qkv, qkv_here, QKV_CUT),
+                (out, out_here, OUT_CUT),
+                (down, down_here, FF_CUT),
+                (gate_up.at[0], gate_up_here.at[0], FF_CUT),
+                (gate_up.at[1], gate_up_here.at[1], FF_CUT),
+            ]
         )
     ]
+
+    def own_terms(step, rows):
+        first = (core * SIDE + turned(x, SIDE - step)) * BLOCK
+        return part[pl.ds(pl.multiple_of(first + rows.start, 16), rows.size), :]
+
+    terms = ByRow(part, place)
+    scatter = Scatter(own_terms, lambda step: terms.at(step, 1), place, sems[11:])
     moved = [(tokens, tok_buf), (out_grad, grad_buf), (bias, bias_buf)]
     swaps = [
         remote(source, target, swap_send, swap_arrive, index, swap_with)
@@ -454,7 +472,6 @@
         locals_.of(cot_buf, cot_here),
         locals_.of(cot_buf, row_block(cot_full, core, x)),
     ]
-    part_sem = own_sems.at[locals_.used]
 
     @pl.when(lacking)
     def _():
@@ -462,10 +479,9 @@
         swaps[0].start()
         swaps[2].start()
         fetches[0].across.start()
+        swaps[0].wait_recv()
         swaps[1].start()
         fetches[1].across.start()
-        fetches[2].across.start()
-        swaps[0].wait_recv()
 
     @pl.when(jnp.logical_not(lacking))
     def _():
@@ -487,10 +503,12 @@
     @pl.when(lacking)
     def _():
         fetches[0].spread()
+        fetches[2].across.start()
         for copy in swaps:
             copy.wait_send()
         swaps[1].wait_recv()
         swaps[2].wait_recv()
+        fetches[3].across.start()
 
     @pl.when(jnp.logical_not(lacking))
     def _():
@@ -512,6 +530,7 @@
         fetches[0].pass_on()
         fetches[1].spread()
         fetches[2].spread()
+        fetches[4].across.start()
 
     gather.arrive(2)
     gather.take()
@@ -525,9 +544,6 @@
     @pl.when(jnp.logical_not(lacking))
     def _():
         fetches[0].own.wait()
-
-    gather_cot.arrive(1)
-    gather_cot.arrive(3)
 
     @pl.loop(0, 8)
     def _(index):
@@ -552,8 +568,10 @@
     def _():
         fetches[1].pass_on()
         fetches[2].pass_on()
-
-    gather_cot.arrive(2)
+        fetches[3].spread()
+
+    gather_cot.arrive(1)
+    gather_cot.arrive(3)
     blocks = attention(
         queries, keys, values, row_info, segments, segment_row, attended, HEAD_DIM ** (-0.5)
     )
@@ -570,44 +588,85 @@
             def _():
                 fetches[1].own.wait()
 
-        else:
-            pltpu.make_async_copy(part_tile, part.at[rows], part_sem).wait()
-
         @pl.loop(0, 2048, step=512)
         def _(column):
             columns = pl.ds(pl.multiple_of(column, 512), 512)
-            part_tile[:, columns] = matmul(attended[rows, :], out_here[:, columns], NN).astype(bf16)
-
-        pltpu.make_async_copy(part_tile, part.at[rows], part_sem).start()
+            part[rows, columns] = matmul(attended[rows, :], out_here[:, columns], NN).astype(bf16)
+
+        if block == 0:
+
+            @pl.when(lacking)
+            def _():
+                fetches[4].spread()
+
+            gather_cot.arrive(2)
+
+        if block == 1:
+
+            @pl.when(core == 1)
+            def _():
+                for step in (2, 1, 3, 0):
+                    scatter.across[step].start()
+
+        if block == 2:
+
+            @pl.when(core == 0)
+            def _():
+                for step in (2, 1, 3):
+                    scatter.merge(step)
+
+    @pl.when(core == 0)
+    def _():
+        for step in (2, 1, 3, 0):
+            scatter.across[step].start()
+
+    @pl.when(core == 1)
+    def _():
+        for step in (2, 1, 3):
+            scatter.merge(step)
+
+    @pl.when(lacking)
+    def _():
+        fetches[3].pass_on()
+        fetches[4].pass_on()
 
     gather_cot.take()
     for each in (gather, gather_cot):
         each.finish()
     for copy in normed_out + stored:
         copy.wait()
-    pltpu.make_async_copy(part_tile, part.at[pl.ds(0, PAIR)], part_sem).wait()
 
     @pl.when(lacking)
     def _():
-        fetches[2].finish()
+        for fetch in fetches[2:]:
+            fetch.finish()
 
     @pl.when(jnp.logical_not(lacking))
     def _():
-        fetches[2].own.wait()
+        for fetch in fetches[2:]:
+            fetch.own.wait()
+
+    scatter.finish()
+
+    def norm_mid(rows):
+        stream = tok_buf[rows, :].astype(jnp.float32) + scatter.rows(rows)
+        mid[rows, :] = stream
+        centre, scale = moments(stream)
+        normed_mid[rows, :] = (centre * scale * gain_mid[...] + shift_mid[...]).astype(bf16)
+
+    tile_rows(norm_mid)
 
 
 def middle_kernel(
-    part,
-    tokens,
+    normed_mid,
+    mid,
     gain,
-    shift,
-    gate_up_own,
+    gate_up_held,
     down_held,
     cot_full,
     attended_full,
     out_held,
     cot,
-    mid,
     d_mid,
     gain_part,
     shift_part,
@@ -645,112 +704,47 @@
     place = here()
     x, y, z_hi, z_lo, core = place
     lacking = core != z_hi
-    attn = ByRow(part, place)
-    first = Scatter(
-        lambda step, rows: own_rows[step, rows, :], lambda step: attn.at(step, 1), place, scratch[:7]
-    )
     second = Scatter(
-        lambda step, rows: own_rows[step, rows, :],
-        lambda step: given_terms.at[step],
-        place,
-        scratch[:3] + scratch[7:11],
-    )
-    gather = Gather(normed.at[pl.ds(0, BLOCK)], ByStep(normed), place, scratch[11:15])
-    gather_d = Gather(d_rows.at[pl.ds(0, BLOCK)], ByStep(d_rows), place, scratch[15:19])
-    fetches = [
-        Fetch(gate_up_own.at[index], gate_up.at[index], FF_CUT, place, scratch[19:22], index) for index in range(2)
-    ]
+        lambda step, rows: own_rows[step, rows, :], lambda step: given_terms.at[step], place, scratch[:7]
+    )
+    gather = Gather(normed.at[pl.ds(0, BLOCK)], ByStep(normed), place, scratch[7:11])
+    gather_d = Gather(d_rows.at[pl.ds(0, BLOCK)], ByStep(d_rows), place, scratch[11:15])
+    scratch = scratch[15:]
     around = Around(place)
-    links = Links(*scratch[22:24])
+    links = Links(*scratch[:2])
     over = links.to(gate_grad, gate_beyond, around.beyond)
     ring = RowRing(*DOWN_RING)
-    ring_terms = scratch[24:27]
+    ring_terms = scratch[2:5]
     ring_loads = [
         pltpu.make_async_copy(ring.quarter(down_grad, turned(y, k)), held, load_sems.at[index])
         for index, (k, held) in enumerate(zip((1, 3, 0), ring_terms))
     ]
-    ring.bind(links, around, scratch[27:], ring.quarter(down_grad, turned(y, 2)), *ring_terms)
+    ring.bind(links, around, scratch[5:], ring.quarter(down_grad, turned(y, 2)), *ring_terms)
     load_cot = Loaded(cot_full, cot_rows, place, load_sems)
     load_att = Loaded(attended_full, attended, place, att_sems)
-    load_own = [
-        pltpu.make_async_copy(attn.at(step, 0), own_rows.at[step], own_sems.at[step]) for step in range(SIDE)
-    ]
-    load_down = pltpu.make_async_copy(down_held, down, own_sems.at[4])
-    load_out = pltpu.make_async_copy(out_held, out, own_sems.at[5])
-
-    for copy in load_own:
-        copy.start()
+    load_normed = pltpu.make_async_copy(normed_mid, normed.at[pl.ds(0, BLOCK)], own_sems.at[0])
+    load_gate_up = pltpu.make_async_copy(gate_up_held, gate_up, own_sems.at[1])
+    load_down = pltpu.make_async_copy(down_held, down, own_sems.at[2])
+    load_out = pltpu.make_async_copy(out_held, out, own_sems.at[3])
+
+    load_normed.start()
     load_down.start()
     load_cot.start()
+    load_gate_up.start()
     load_att.start()
     load_out.start()
-
-    @pl.when(lacking)
-    def _():
-        greet(line_peers(place) + fetch_peers(place) + [around.beyond])
-
-    @pl.when(jnp.logical_not(lacking))
-    def _():
-        greet(line_peers(place) + [around.up, around.down, around.beyond])
-
-    for step in (2, 1, 3, 0):
-        first.across[step].start()
-
-    @pl.when(lacking)
-    def _():
-        for fetch in fetches:
-            fetch.across.start()
-
-    @pl.when(jnp.logical_not(lacking))
-    def _():
-        for fetch in fetches:
-            fetch.own.start()
-
-    for copy in load_own:
-        copy.wait()
-    for step in (2, 1, 3):
-        first.merge(step)
+    greet(line_peers(place) + [around.up, around.down, around.beyond])
+    load_normed.wait()
+    gather.start()
     load_down.wait()
     load_cot.wait()
 
-    @pl.loop(0, 2)
+    @pl.loop(0, 4)
     def _(index):
         rows = pl.ds(pl.multiple_of(index * PAIR, PAIR), PAIR)
         d_hidden[rows, :] = matmul(cot_rows[rows, :], down[...], NT)
 
-    @pl.when(lacking)
-    def _():
-        for fetch in fetches:
-            fetch.spread()
-
-    @pl.loop(2, 4)
-    def _(index):
-        rows = pl.ds(pl.multiple_of(index * PAIR, PAIR), PAIR)
-        d_hidden[rows, :] = matmul(cot_rows[rows, :], down[...], NT)
-
-    first.finish()
-
-    def norm(rows):
-        stream = tokens[rows, :].astype(jnp.float32) + first.rows(rows)
-        mid[rows, :] = stream
-        centre, scale = moments(stream)
-        normed[rows, :] = (centre * scale * gain[...] + shift[...]).astype(bf16)
-
-    tile_rows(norm)
-    gather.start()
-
-    @pl.when(lacking)
-    def _():
-        for fetch in fetches:
-            fetch.pass_on()
-        for fetch in fetches:
-            fetch.finish()
-
-    @pl.when(jnp.logical_not(lacking))
-    def _():
-        for fetch in fetches:
-            fetch.own.wait()
-
+    load_gate_up.wait()
     order = (0, 1, 3, 2)
 
     @pl.loop(0, 4)
@@ -1373,13 +1367,13 @@
 
 
 ORDER = (
-    "l3", "l0", "f", "l2", "r0", "a2", "r1", "l0", "l1", "f", "l1", "f", "l0", "f",
-    "l0", "l1", "r0", "a2", "f", "l0", "l1", "l2", "f", "l2", "l3", "l1", "l0", "r1",
-    "f", "a1", "l3", "a0", "r0", "f", "l0", "l2", "a2", "l1", "r1", "f", "a1", "f",
-    "a0", "l3", "l2", "l1", "a2", "r0", "a1", "l0", "a1", "a0", "l3", "r1", "l2", "l0",
-    "r0", "f", "l3", "a0", "e", "l1", "f", "r1", "a2", "l2", "r0", "e", "l1", "a1",
-    "l3", "r0", "e", "r1", "a0", "a2", "r1", "l2", "a1", "l3", "e", "a0", "a2", "a1",
-    "l2", "a2", "a0", "a1", "l2", "l3", "a0", "e", "l3",
+    "l3", "l0", "f", "l2", "a2", "r0", "r1", "l0", "l1", "f", "l1", "f", "l0", "f",
+    "l1", "l0", "f", "l1", "l2", "l0", "a2", "l2", "l3", "f", "l3", "l1", "l0", "f",
+    "a0", "a1", "l1", "l2", "f", "l0", "l3", "a2", "r0", "f", "r1", "a0", "f", "a1",
+    "l1", "l2", "a2", "l3", "r0", "l0", "r1", "a0", "l0", "l1", "a2", "a0", "a1", "l1",
+    "l2", "r0", "l3", "f", "r1", "e", "a1", "l2", "a2", "f", "a0", "r0", "e", "l3",
+    "e", "a1", "r1", "l2", "a2", "a2", "a0", "r0", "l3", "e", "r0", "a1", "l2", "r1",
+    "a0", "l2", "a1", "r1", "l3", "a0", "e", "a1", "l3",
 )
 
 
@@ -1755,7 +1749,24 @@
     keep, from_after, from_before = rotary_tables(position)
     flat = (row_total, qkv_weight.shape[2])
     dma, vmem = pltpu.SemaphoreType.DMA, pltpu.VMEM
-    tokens_here, cot, normed1, cot_rows, attn_part, qkv, out, down, queries, keys, values, attended, row_info = call(
+    gate_up_t = jnp.swapaxes(gate_up_weight, 1, 2)
+    (
+        tokens_here,
+        cot,
+        normed1,
+        cot_rows,
+        mid_stream,
+        normed2,
+        qkv,
+        out,
+        down,
+        gate_up,
+        queries,
+        keys,
+        values,
+        attended,
+        row_info,
+    ) = call(
         first_kernel,
         1,
         (
@@ -1767,6 +1778,9 @@
             qkv_weight,
             out_weight,
             down_weight,
+            gate_up_t,
+            ln2_gain[None],
+            ln2_bias[None],
             qkv_bias,
             segments,
             segment_row,
@@ -1774,58 +1788,58 @@
             from_after,
             from_before,
         ),
-        [ANY, ANY, HELD, HELD, HELD, ANY, ANY, ANY] + [HELD] * 6,
+        [ANY, ANY, HELD, HELD, HELD, ANY, ANY, ANY, ANY] + [HELD] * 8,
         [
             (rows_here, bf16),
             (rows_here, bf16),
             (rows_all, bf16),
             (rows_all, bf16),
-            (rows_all, bf16),
+            (rows_here, f32),
+            (rows_here, bf16),
             (qkv_weight.shape, bf16),
             (out_weight.shape, bf16),
             (down_weight.shape, bf16),
+            (gate_up_t.shape, bf16),
             (flat, bf16),
             (flat, bf16),
             (flat, bf16),
             (flat, bf16),
             ((row_total, 128), f32),
         ],
-        [ANY] * 5 + [HELD] * 8,
+        [ANY] * 4 + [HELD] * 11,
         (
             vmem(rows_here, bf16),
             vmem(rows_here, bf16),
             vmem(rows_here, bf16),
             vmem(qkv_bias.shape, f32),
             vmem(rows_all, bf16),
-            vmem((PAIR, 2048), bf16),
+            vmem(rows_all, bf16),
             dma((3,)),
             dma((3,)),
             dma((16,)),
         )
         + Gather.scratch * 2
-        + fetch_scratch(3),
-    )
-
-    gate_up_t = jnp.swapaxes(gate_up_weight, 1, 2)
+        + fetch_scratch(5)
+        + Scatter.scratch,
+    )
+
     ff = down_weight.shape[0]
-    mid_stream, d_mid, gain2_part, shift2_part, *ff_parts, ffn_part, d_attended, out_grad = call(
+    d_mid, gain2_part, shift2_part, *ff_parts, ffn_part, d_attended, out_grad = call(
         middle_kernel,
         2,
         (
-            attn_part,
-            tokens_here,
+            normed2,
+            mid_stream,
             ln2_gain[None],
-            ln2_bias[None],
-            gate_up_t,
+            gate_up,
             down,
             cot_rows,
             attended,
             out,
             cot,
         ),
-        [ANY, HELD, HELD, HELD, ANY, ANY, ANY, ANY, ANY, HELD],
+        [ANY, HELD, HELD, ANY, ANY, ANY, ANY, ANY, HELD],
         [
-            (rows_here, f32),
             (rows_here, f32),
             ((1, 2048), f32),
             ((1, 2048), f32),
@@ -1838,7 +1852,7 @@
             (attended.shape, bf16),
             (out.shape, bf16),
         ],
-        [HELD] * 4 + [ANY] * 6 + [HELD, HELD],
+        [HELD] * 3 + [ANY] * 6 + [HELD, HELD],
         (
             vmem((2, ff, 2048), bf16),
             vmem((ff, 2048), bf16),
@@ -1862,9 +1876,7 @@
             dma((2,)),
         )
         + Scatter.scratch
-        + Scatter.sems
         + Gather.scratch * 2
-        + fetch_scratch(2)
         + (dma((5,)), dma((5,)))
         + (vmem((ff // SIDE, 2048), bf16),) * 3
         + RowRing(*DOWN_RING).scratch(),

time: 365 us -> 360 us (0.986)
  Pallas kernels: 334 us -> 329 us
    pallas_call x3, Pallas kernels: 334 us -> 329 us  [call(): pl.pallas_call(kernel, out_shape=[jax.ShapeDtypeStruct(shape, kind) for s...]
where the time goes in v4:
time: 360 us; the launch traced here: 359 us
  Pallas kernels  329 us (91%)
  other arithmetic  22.1 us (6%)
  local copies, waits for them, and re-layouts  7.48 us (2%)
    pallas_call x3, Pallas kernels, call(): pl.pallas_call(kernel, out_shape=[jax.ShapeDtypeStruct(shape, kind) for s...  329 us

profile of v4, /device:TPU:1, one launch (start us, length us, event | category | flops | bytes accessed | tf_op | source)
XLA Modules:
  0.0 359.3 jit_solution(2291381303670857677)
XLA Ops:
  0.7 0.7 compare_convert_fusion
  1.3 0.8 select_reduce_fusion
  2.2 0.7 add.78
  2.9 0.1 tile.10
  2.9 0.2 multiply_reduce_fusion
  3.2 0.1 convert_bitcast_fusion.1
  3.2 0.6 add_convert_fusion.1.segment_row
  3.8 0.7 copy.34.live
  4.6 0.2 copy.32
  4.8 0.2 copy.33
  5.0 0.9 add_convert_fusion.segments
  5.9 3.2 fusion.2
  9.1 102.6 %shard_map.212 = (bf16[128,2048]{1,0:T(8,128)(2,1)}, bf16[128,2048]{1,0:T(8,128)(2,1)}, bf16[1024,2048]{1,0:T(8,128)(2,1)}, bf16[1024,2048]{1,0:T(8,128)(2,1)}, ...) custom-call(bf16[128,2048]{1,0:T(8,128)(2,1)} %tokens.1, ...), custom_call_target="tpu_custom_call" | custom-call | tf_op jit(solution)/shard_map/pallas_call | solution.py:1676
  111.8 90.8 %shard_map.213 = (f32[128,2048]{1,0:T(8,128)}, f32[1,2048]{1,0:T(1,128)}, f32[1,2048]{1,0:T(1,128)}, bf16[704,2048]{1,0:T(8,128)(2,1)}, bf16[704,2048]{1,0:T(8,1...) custom-call(bf16[128,2048]{1,0:T(8,128)(2,1)} %get-tuple-element.47., ...), custom_call_target="tpu_custom_call" | custom-call | tf_op jit(solution)/shard_map/pallas_call | solution.py:1676
  202.5 135.5 %shard_map.214 = (bf16[128,2048]{1,0:T(8,128)(2,1)}, f32[128,2048]{1,0:T(8,128)}, bf16[704,2048]{1,0:T(8,128)(2,1)}, bf16[704,2048]{1,0:T(8,128)(2,1)}, bf16[704...) custom-call(bf16[1024,256]{1,0:T(8,128)(2,1)} %get-tuple-element.44., ...), custom_call_target="tpu_custom_call" | custom-call | tf_op jit(solution)/shard_map/pallas_call | solution.py:1676
  338.0 0.0 copy-start.1
  338.0 1.0 slice.17
  339.0 1.6 fusion.4
  340.7 0.6 constant_dynamic-slice_fusion
  341.2 2.8 convert_element_type.61
  344.0 0.0 copy-done.1
  344.0 0.0 copy-start
  344.0 3.3 convert_element_type.62
  347.3 0.0 copy-done
  347.3 0.0 copy-start.2
  347.4 0.0 copy-start.3
  347.4 3.7 %convert.5 = f32[3,2048,256]{2,1,0:T(8,128)} convert(bf16[3,2048,256]{2,1,0:T(8,128)(2,1)S(1)} %bitcast.22) | non-fusion elementwise | flops 1572864 | bytes 9437184 | tf_op jit(solution)/shard_map/convert_element_type | solution.py:1964
  351.1 0.0 copy-done.2
  351.1 1.2 copy-done.3
  352.3 0.0 copy-start.5
  352.3 0.0 copy-start.4
  352.3 5.2 %convert_bitcast_fusion = f32[2,2048,704]{1,2,0:T(8,128)} fusion(bf16[1,704,2048]{2,1,0:T(8,128)(2,1)S(1)} %bitcast.24, bf16[1,704,2048]{2,1,0:T(8,128)(2,1)S(1)} %bitcast.23), kind=kLoop, calls=%fused_computation | loop fusion | flops 5767168 | bytes 17301504 | tf_op jit(solution)/shard_map/transpose | solution.py:1962
  357.5 0.0 copy-done.5
  357.5 0.8 copy.37
  358.3 0.0 copy-done.4
  358.3 1.0 copy.38
  (6 shorter events, 0.0 us)
Async XLA Ops:
  338.0 6.0 %copy-start.1 = (bf16[704,2048]{1,0:T(8,128)(2,1)S(1)}, bf16[704,2048]{1,0:T(8,128)(2,1)}, u32[]{:S(2)}) copy-start(bf16[704,2048]{1,0:T(8,128)(2,1)} %get-tuple-element.76) | copy-start | bytes 8650756
  344.0 3.3 copy-start
  347.3 3.7 %copy-start.2 = (bf16[704,2048]{1,0:T(8,128)(2,1)S(1)}, bf16[704,2048]{1,0:T(8,128)(2,1)}, u32[]{:S(2)}) copy-start(bf16[704,2048]{1,0:T(8,128)(2,1)} %get-tuple-element.74) | copy-start | bytes 8650756
  347.4 5.0 %copy-start.3 = (bf16[704,2048]{1,0:T(8,128)(2,1)S(1)}, bf16[704,2048]{1,0:T(8,128)(2,1)}, u32[]{:S(2)}) copy-start(bf16[704,2048]{1,0:T(8,128)(2,1)} %get-tuple-element.75) | copy-start | bytes 8650756
  352.3 5.2 %copy-start.5 = (bf16[128,2048]{1,0:T(8,128)(2,1)S(1)}, bf16[128,2048]{1,0:T(8,128)(2,1)}, u32[]{:S(2)}) copy-start(bf16[128,2048]{1,0:T(8,128)(2,1)} %get-tuple-element.100) | copy-start | bytes 1572868
  352.3 6.0 %copy-start.4 = (f32[128,2048]{1,0:T(8,128)S(1)}, f32[128,2048]{1,0:T(8,128)}, u32[]{:S(2)}) copy-start(f32[128,2048]{1,0:T(8,128)} %get-tuple-element.101) | copy-start | bytes 3145732

commit v5 on v4

--- a/solution.py
+++ b/solution.py
@@ -11,6 +11,7 @@
 ROT = 16
 SIDE = 4
 BLOCK = 128
+SEQUENCES = 64
 AXES = ("dp", "tensor")
 MESH = pl.DeviceIdType.MESH
 VMEM_LIMIT = 54 * 2**20
@@ -388,7 +389,6 @@
 def first_kernel(
     tokens,
     out_grad,
-    live,
     gain,
     shift,
     qkv,
@@ -516,7 +516,9 @@
         stays[2].wait()
 
     def mask(rows):
-        cot_buf[rows, :] = (grad_buf[rows, :].astype(jnp.float32) * live[rows, :]).astype(bf16)
+        place_rows = pl.ds(pl.multiple_of((core * SIDE + x) * BLOCK + rows.start, 16), rows.size)
+        grads = grad_buf[rows, :].astype(jnp.float32)
+        cot_buf[rows, :] = jnp.where(segments[place_rows, :] < SEQUENCES, grads, 0.0).astype(bf16)
 
     tile_rows(mask)
     gather.arrive(1)
@@ -868,7 +870,7 @@
     gather_d.arrive(3)
     weight_grad(up_grad, d_up, normed)
     gather_d.arrive(2)
-    for step in range(SIDE):
+    for step in (0, 1, 3, 2):
         gather_d.across[step].wait_recv()
         terms = matmul(d_rows[pl.ds(step * PAIR, PAIR), :], out[...], NT).astype(bf16)
         behind = turned(x, SIDE - step)
@@ -1741,9 +1743,7 @@
     rows_here, rows_all = (BLOCK, 2048), (row_total, 2048)
     local_heads = qkv_weight.shape[2] // HEAD_DIM
     member = (y * 2 + z_lo) * 2 + z_hi
-    shard = core * SIDE + x
-    segment, position, live_rows = member_layout(seq_length, seq_owner, member, row_total)
-    live = lax.dynamic_slice_in_dim(live_rows, shard * BLOCK, BLOCK, 0)[:, None].astype(f32)
+    segment, position, _ = member_layout(seq_length, seq_owner, member, row_total)
     segments = segment.astype(f32)[:, None]
     segment_row = segment.astype(f32)[None]
     keep, from_after, from_before = rotary_tables(position)
@@ -1772,7 +1772,6 @@
         (
             tokens,
             out_grad,
-            live,
             ln1_gain[None],
             ln1_bias[None],
             qkv_weight,
@@ -1788,7 +1787,7 @@
             from_after,
             from_before,
         ),
-        [ANY, ANY, HELD, HELD, HELD, ANY, ANY, ANY, ANY] + [HELD] * 8,
+        [ANY, ANY, HELD, HELD, ANY, ANY, ANY, ANY] + [HELD] * 8,
         [
             (rows_here, bf16),
             (rows_here, bf16),

time: 360 us -> 359 us (level)
  no operation moved by 1% of the time
where the time goes in v5:
time: 359 us; the launch traced here: 358 us
  Pallas kernels  329 us (92%)
  other arithmetic  22 us (6%)
  local copies, waits for them, and re-layouts  6.74 us (2%)
    pallas_call x3, Pallas kernels, call(): pl.pallas_call(kernel, out_shape=[jax.ShapeDtypeStruct(shape, kind) for s...  329 us

profile of v5, /device:TPU:1, one launch (start us, length us, event | category | flops | bytes accessed | tf_op | source)
XLA Modules:
  0.0 358.4 jit_solution(4592341950487700217)
XLA Ops:
  0.7 0.7 compare_convert_fusion
  1.3 0.8 select_reduce_fusion
  2.1 0.7 add.72
  2.8 0.1 tile.10
  2.9 0.2 multiply_reduce_fusion
  3.2 0.6 add_convert_fusion.1.segment_row
  3.8 0.2 copy.29
  4.0 0.2 copy.30
  4.2 0.9 add_convert_fusion.segments
  5.1 3.2 fusion.2
  8.3 102.6 %shard_map.212 = (bf16[128,2048]{1,0:T(8,128)(2,1)}, bf16[128,2048]{1,0:T(8,128)(2,1)}, bf16[1024,2048]{1,0:T(8,128)(2,1)}, bf16[1024,2048]{1,0:T(8,128)(2,1)}, ...) custom-call(bf16[128,2048]{1,0:T(8,128)(2,1)} %tokens.1, ...), custom_call_target="tpu_custom_call" | custom-call | tf_op jit(solution)/shard_map/pallas_call | solution.py:1678
  110.9 90.1 %shard_map.213 = (f32[128,2048]{1,0:T(8,128)}, f32[1,2048]{1,0:T(1,128)}, f32[1,2048]{1,0:T(1,128)}, bf16[704,2048]{1,0:T(8,128)(2,1)}, bf16[704,2048]{1,0:T(8,1...) custom-call(bf16[128,2048]{1,0:T(8,128)(2,1)} %get-tuple-element.47., ...), custom_call_target="tpu_custom_call" | custom-call | tf_op jit(solution)/shard_map/pallas_call | solution.py:1678
  201.0 136.2 %shard_map.214 = (bf16[128,2048]{1,0:T(8,128)(2,1)}, f32[128,2048]{1,0:T(8,128)}, bf16[704,2048]{1,0:T(8,128)(2,1)}, bf16[704,2048]{1,0:T(8,128)(2,1)}, bf16[704...) custom-call(bf16[1024,256]{1,0:T(8,128)(2,1)} %get-tuple-element.44., ...), custom_call_target="tpu_custom_call" | custom-call | tf_op jit(solution)/shard_map/pallas_call | solution.py:1678
  337.2 0.0 copy-start.1
  337.2 1.0 slice.17
  338.2 1.6 fusion.4
  339.8 0.6 constant_dynamic-slice_fusion
  340.4 2.8 convert_element_type.54
  343.2 0.0 copy-done.1
  343.2 0.0 copy-start
  343.2 3.3 convert_element_type.55
  346.5 0.0 copy-done
  346.5 0.0 copy-start.2
  346.5 0.0 copy-start.3
  346.5 3.7 %convert.5 = f32[3,2048,256]{2,1,0:T(8,128)} convert(bf16[3,2048,256]{2,1,0:T(8,128)(2,1)S(1)} %bitcast.20) | non-fusion elementwise | flops 1572864 | bytes 9437184 | tf_op jit(solution)/shard_map/convert_element_type | solution.py:1963
  350.3 0.0 copy-done.2
  350.3 1.2 copy-done.3
  351.5 0.0 copy-start.5
  351.5 0.0 copy-start.4
  351.5 5.2 %convert_bitcast_fusion = f32[2,2048,704]{1,2,0:T(8,128)} fusion(bf16[1,704,2048]{2,1,0:T(8,128)(2,1)S(1)} %bitcast.22, bf16[1,704,2048]{2,1,0:T(8,128)(2,1)S(1)} %bitcast.21), kind=kLoop, calls=%fused_computation | loop fusion | flops 5767168 | bytes 17301504 | tf_op jit(solution)/shard_map/transpose | solution.py:1961
  356.7 0.0 copy-done.5
  356.7 0.8 copy.33
  357.5 0.0 copy-done.4
  357.5 1.0 copy.34
  (6 shorter events, 0.0 us)
Async XLA Ops:
  337.2 6.0 %copy-start.1 = (bf16[704,2048]{1,0:T(8,128)(2,1)S(1)}, bf16[704,2048]{1,0:T(8,128)(2,1)}, u32[]{:S(2)}) copy-start(bf16[704,2048]{1,0:T(8,128)(2,1)} %get-tuple-element.76) | copy-start | bytes 8650756
  343.2 3.3 copy-start
  346.5 3.7 %copy-start.2 = (bf16[704,2048]{1,0:T(8,128)(2,1)S(1)}, bf16[704,2048]{1,0:T(8,128)(2,1)}, u32[]{:S(2)}) copy-start(bf16[704,2048]{1,0:T(8,128)(2,1)} %get-tuple-element.74) | copy-start | bytes 8650756
  346.5 5.0 %copy-start.3 = (bf16[704,2048]{1,0:T(8,128)(2,1)S(1)}, bf16[704,2048]{1,0:T(8,128)(2,1)}, u32[]{:S(2)}) copy-start(bf16[704,2048]{1,0:T(8,128)(2,1)} %get-tuple-element.75) | copy-start | bytes 8650756
  351.5 5.2 %copy-start.5 = (bf16[128,2048]{1,0:T(8,128)(2,1)S(1)}, bf16[128,2048]{1,0:T(8,128)(2,1)}, u32[]{:S(2)}) copy-start(bf16[128,2048]{1,0:T(8,128)(2,1)} %get-tuple-element.100) | copy-start | bytes 1572868
  351.5 6.0 %copy-start.4 = (f32[128,2048]{1,0:T(8,128)S(1)}, f32[128,2048]{1,0:T(8,128)}, u32[]{:S(2)}) copy-start(f32[128,2048]{1,0:T(8,128)} %get-tuple-element.101) | copy-start | bytes 3145732
